TPU v7x, 128 devices: a whole 4x4x4 slice. The times are simulated.
128 devices in a mesh: grp: 4 (over y), dom: 32 (over z, x, core).
Axes of the slice: x: 4, y: 4, z: 4, core: 2. Of those that a mesh axis runs over, the one named last changes fastest.
Arguments:
- right_side: float32 [16, 2048, 16, 128], P(None, ('grp', 'dom')), may hold values from -12 to 12
- diagonal: float32 [2048, 16, 128], P(('grp', 'dom')), may hold values from 1 to 4
- counts: int32 [128], P(('grp', 'dom')), may hold values from 8 to 16, as said below
Outputs:
- solution_field: float32 [16, 2048, 16, 128], P(None, ('grp', 'dom'))
- residual: float32 [16, 2048, 16, 128], P(None, ('grp', 'dom'))
Inputs may be any that keep to these rules, and one draw needn't show every extreme that they name: counts[i] live planes of partition i occupy its first plane slots; some partition has all 16 slots live.
All inputs are finite; a program needn't handle non-finite values.
Results may differ from a plain program's by a relative error of at most 0.00035.
Values sent between devices are 32-bit elements; how exact they have to be, the bound alone decides.
No kernel may reach another device: no remote copies, remote signals or barrier semaphores. Data moves between devices by JAX's collectives and lax.ppermute only.
A program may use at most 128 MiB of HBM per device.

v0:
```python
import jax
import jax.numpy as jnp
from jax import lax
from jax.sharding import PartitionSpec as P

NRHS = 16
SSTEP = 4
OUTER = 2


SHIFT = 8.5
SCALE = 7.5


def passed_along(block, axis, distance):
    devices = range(lax.axis_size(axis))
    route = [(i - distance, i) for i in devices if i - distance in devices]
    return lax.ppermute(block, axis, route)


def apply_op(centre, below, above, diag):
    beside = above + below
    padded = jnp.pad(centre, ((0, 0), (0, 0), (1, 1), (0, 0)))
    beside = beside + padded[:, :, 2:] + padded[:, :, :-2]
    padded = jnp.pad(centre, ((0, 0), (0, 0), (0, 0), (1, 1)))
    beside = beside + padded[..., 2:] + padded[..., :-2]
    return (6.0 + diag) * centre - beside


def change_matrix():
    small = SHIFT * jnp.eye(SSTEP + 1, SSTEP, dtype=jnp.float32) + SCALE * jnp.eye(
        SSTEP + 1, SSTEP, k=-1, dtype=jnp.float32
    )
    return jnp.kron(small, jnp.eye(NRHS, dtype=jnp.float32))


def galerkin(gram):
    change = change_matrix()
    leading = gram[: SSTEP * NRHS]
    system = jnp.dot(leading, change, precision=lax.Precision.HIGHEST)
    system = 0.5 * (system + system.T)
    factor = jnp.linalg.cholesky(system)
    coef = jax.scipy.linalg.cho_solve((factor, True), leading[:, :NRHS])
    return (coef, jnp.dot(change, coef, precision=lax.Precision.HIGHEST))


def local(right_side, diagonal, counts):
    count = counts[0]
    slots = right_side.shape[1]
    position = jnp.arange(slots, dtype=jnp.int32)
    live_mask = (position < count)[None, :, None, None]
    residual = jnp.where(live_mask, right_side, 0.0)
    solution_field = jnp.zeros_like(right_side)
    for outer in range(OUTER):
        basis = [residual]
        for power in range(SSTEP):
            current = basis[-1]
            field_top = lax.dynamic_slice_in_dim(current, count - 1, 1, 1)
            lower = passed_along(field_top, ("grp", "dom"), 1)
            upper = passed_along(current[:, :1], ("grp", "dom"), -1)
            extended = jnp.concatenate([lower, current, jnp.zeros_like(lower)], 1)
            extended = lax.dynamic_update_slice_in_dim(extended, upper, 1 + count, 1)
            image = jnp.where(
                live_mask, apply_op(current, extended[:, :-2], extended[:, 2:], diagonal), 0.0
            )
            basis.append(jnp.where(live_mask, (image - SHIFT * current) / SCALE, 0.0))
        panel = jnp.stack(basis).reshape((SSTEP + 1) * NRHS, -1)
        local_gram = jnp.dot(panel, panel.T, precision=lax.Precision.HIGHEST)
        gram = lax.psum(local_gram, ("grp", "dom"))
        coef, step = galerkin(gram)
        solution_field = solution_field + jnp.dot(
            coef.T, panel[: SSTEP * NRHS], precision=lax.Precision.HIGHEST
        ).reshape(right_side.shape)
        residual = residual - jnp.dot(step.T, panel, precision=lax.Precision.HIGHEST).reshape(
            right_side.shape
        )
    return (solution_field, residual)


def solution(mesh):
    in_specs = (
        P(None, ("grp", "dom"), None, None),
        P(("grp", "dom"), None, None),
        P(("grp", "dom")),
    )
    out_specs = (P(None, ("grp", "dom"), None, None), P(None, ("grp", "dom"), None, None))
    return jax.shard_map(local, mesh=mesh, in_specs=in_specs, out_specs=out_specs, check_vma=False)
```

profile of v0, /device:TPU:0, one launch (start us, length us, event | category | flops | bytes accessed | tf_op | source)
XLA Modules:
  0.0 479.7 jit_solution(8334067575326461679)
XLA Ops:
  1.3 4.3 constant_dynamic-update-slice_fusion.3
  5.7 1.3 collective-permute-start.1
  7.0 3.0 collective-permute-start
  10.1 0.9 collective-permute-done
  11.3 2.4 constant_dynamic-update-slice_fusion.2
  13.8 4.1 collective-permute-start.2
  17.8 1.3 collective-permute-start.3
  19.5 3.6 collective-permute-done.3
  23.0 2.6 constant_dynamic-update-slice_fusion.1
  25.6 5.5 %collective-permute-start.4 = (f32[16,1,16,128]{3,0,2,1:T(8,128)S(1)}, f32[16,1,16,128]{3,0,2,1:T(8,128)S(1)}, u32[]{:S(2)}, u32[]{:S(2)}) collective-permute-start(f32[16,1,16,128]{3,0,2,1:T(8,128)S(1)} %get-tuple-element.33), channel_id=1, source_target_pairs={{0,1},{1,2},{2,3},{3,4},{4,5},{5,6},{6,7},{7,8},{8,9},{9,10},{10,1... | collective-permute-start | bytes 393224 | tf_op jit(solution)/shard_map/ppermute | solution.py:18
  31.2 1.3 collective-permute-start.5
  32.8 1.6 collective-permute-done.5
  34.4 2.6 constant_dynamic-update-slice_fusion
  37.0 1.3 copy-done.6
  38.4 5.0 %collective-permute-start.6 = (f32[16,1,16,128]{3,0,2,1:T(8,128)S(1)}, f32[16,1,16,128]{3,0,2,1:T(8,128)S(1)}, u32[]{:S(2)}, u32[]{:S(2)}) collective-permute-start(f32[16,1,16,128]{3,0,2,1:T(8,128)S(1)} %get-tuple-element.31), channel_id=1, source_target_pairs={{0,1},{1,2},{2,3},{3,4},{4,5},{5,6},{6,7},{7,8},{8,9},{9,10},{10,1... | collective-permute-start | bytes 393224 | tf_op jit(solution)/shard_map/ppermute | solution.py:18
  43.6 1.6 collective-permute-start.7
  45.2 1.9 maximum_maximum_fusion.3
  47.2 2.5 fusion.45
  49.7 11.2 %copy.13 = f32[5,16,16,16,128]{4,3,2,1,0:T(8,128)} copy(f32[5,16,16,16,128]{4,1,3,2,0:T(8,128)} %fusion.45) | data formatting | bytes 20971520 | tf_op jit(solution)/shard_map/stack | solution.py:67
  60.9 11.6 %reshape.76 = f32[80,32768]{1,0:T(8,128)} reshape(f32[5,16,16,16,128]{4,3,2,1,0:T(8,128)} %copy.13) | data formatting | bytes 20971520 | tf_op jit(solution)/shard_map/reshape | solution.py:67
  72.5 12.7 %fusion.130 = f32[80,80]{1,0:T(8,128)S(1)} fusion(f32[80,32768]{1,0:T(8,128)} %reshape.76), kind=kOutput, calls=%fused_computation.215 | convolution fusion | flops 2516582400 | bytes 10511360 | tf_op jit(solution)/shard_map/dot_general | solution.py:68
  85.2 91.1 %psum.14 = f32[80,80]{1,0:T(8,128)S(1)} all-reduce(f32[80,80]{1,0:T(8,128)S(1)} %fusion.130), channel_id=1, replica_groups=mesh['grp'=4,'dom'=32] {'grp','dom'}, use_global_device_ids=true, to_apply=%region_0.1 | all-reduce | flops 6400 | bytes 51200 | tf_op jit(solution)/shard_map/psum | solution.py:69
  176.7 5.8 %cholesky.44 = f32[64,64]{1,0:T(8,128)S(1)} custom-call(f32[64,64]{1,0:T(8,128)S(1)} %fusion.111), custom_call_target="Cholesky" | custom-call | tf_op jit(solution)/shard_map/jit(cholesky)/cholesky | solution.py:42
  183.2 0.7 fusion.93
  183.9 4.9 %custom-call.8 = f32[1,64,64]{1,2,0:T(8,128)S(1)} custom-call(f32[1,64,64]{2,1,0:T(8,128)S(1)} %fusion.93), custom_call_target="InvertDiagBlocksLowerTriangular" | custom-call | tf_op jit(solution)/shard_map/jit(_cho_solve)/triangular_solve | solution.py:43
  189.4 5.8 %copy.32 = f32[10,8,256,128]{3,2,1,0:T(8,128)S(1)} copy(f32[10,8,256,128]{3,1,2,0:T(8,128)} %bitcast.128) | data formatting | bytes 20971520
  195.3 11.2 %constant_dynamic-update-slice_fusion.7 = (f32[5,16,16,16,128]{4,1,3,2,0:T(8,128)S(1)}, f32[16,16,16,128]{3,0,2,1:T(8,128)S(1)}) fusion(f32[16,16,16,128]{3,0,2,1:T(8,128)S(1)} %get-tuple-element.21, f32[80,16,1,1]{0,1,3,2:T(8,128)S(1)} %convolution_bitcast_fusion.1, f32[16,16,128,80]{2,1,0,3:T(8,128)S(1)} %bitcast.131), kind=kOutput, calls=%fused_computation.179 | convolution fusion | flops 503840768 | bytes 16782336 | tf_op jit(solution)/shard_map/dot_general | solution.py:74
  206.5 1.7 collective-permute-start.8
  208.3 1.3 collective-permute-start.9
  209.9 2.5 collective-permute-done.9
  212.4 1.6 constant_dynamic-update-slice_fusion.6
  214.1 5.5 %collective-permute-start.10 = (f32[16,1,16,128]{3,0,2,1:T(8,128)S(1)}, f32[16,1,16,128]{3,0,2,1:T(8,128)S(1)}, u32[]{:S(2)}, u32[]{:S(2)}) collective-permute-start(f32[16,1,16,128]{3,0,2,1:T(8,128)S(1)} %get-tuple-element.27), channel_id=1, source_target_pairs={{0,1},{1,2},{2,3},{3,4},{4,5},{5,6},{6,7},{7,8},{8,9},{9,10},{10,1... | collective-permute-start | bytes 393224 | tf_op jit(solution)/shard_map/ppermute | solution.py:18
  219.5 1.3 collective-permute-start.11
  221.2 1.6 collective-permute-done.11
  222.8 2.6 constant_dynamic-update-slice_fusion.5
  225.4 1.3 copy-done.11
  226.8 5.0 %collective-permute-start.12 = (f32[16,1,16,128]{3,0,2,1:T(8,128)S(1)}, f32[16,1,16,128]{3,0,2,1:T(8,128)S(1)}, u32[]{:S(2)}, u32[]{:S(2)}) collective-permute-start(f32[16,1,16,128]{3,0,2,1:T(8,128)S(1)} %get-tuple-element.25), channel_id=1, source_target_pairs={{0,1},{1,2},{2,3},{3,4},{4,5},{5,6},{6,7},{7,8},{8,9},{9,10},{10,1... | collective-permute-start | bytes 393224 | tf_op jit(solution)/shard_map/ppermute | solution.py:18
  231.8 0.9 pad_maximum_fusion
  232.6 6.0 %copy.16 = f32[4,16,16,16,128]{4,3,2,1,0:T(8,128)} copy(f32[4,16,16,16,128]{4,1,3,2,0:T(8,128)S(1)} %pad_maximum_fusion) | data formatting | bytes 16777216 | tf_op jit(solution)/shard_map/stack | solution.py:67
  238.6 9.4 %slice.234 = f32[64,32768]{1,0:T(8,128)} reshape(f32[4,16,16,16,128]{4,3,2,1,0:T(8,128)} %copy.16) | data formatting | bytes 16777216 | tf_op jit(solution)/shard_map/slice | solution.py:72
  248.0 8.3 %copy.31 = f32[8,8,256,128]{3,2,1,0:T(8,128)} copy(f32[8,8,256,128]{3,1,2,0:T(8,128)} %bitcast.141) | data formatting | bytes 16777216
  256.3 1.3 collective-permute-start.13
  257.9 1.6 collective-permute-done.13
  259.5 2.7 constant_dynamic-update-slice_fusion.4
  262.2 1.3 collective-permute-start.15
  263.5 5.6 %collective-permute-start.14 = (f32[16,1,16,128]{3,0,2,1:T(8,128)S(1)}, f32[16,1,16,128]{3,0,2,1:T(8,128)S(1)}, u32[]{:S(2)}, u32[]{:S(2)}) collective-permute-start(f32[16,1,16,128]{3,0,2,1:T(8,128)S(1)} %get-tuple-element.23), channel_id=1, source_target_pairs={{0,1},{1,2},{2,3},{3,4},{4,5},{5,6},{6,7},{7,8},{8,9},{9,10},{10,1... | collective-permute-start | bytes 393224 | tf_op jit(solution)/shard_map/ppermute | solution.py:18
  269.2 1.0 pad_maximum_fusion.1
  270.2 5.9 %copy.22 = f32[4,16,16,16,128]{4,3,2,1,0:T(8,128)} copy(f32[4,16,16,16,128]{4,1,3,2,0:T(8,128)S(1)} %pad_maximum_fusion.1) | data formatting | bytes 16777216 | tf_op jit(solution)/shard_map/stack | solution.py:67
  276.1 9.4 %slice.265 = f32[64,32768]{1,0:T(8,128)} reshape(f32[4,16,16,16,128]{4,3,2,1,0:T(8,128)} %copy.22) | data formatting | bytes 16777216 | tf_op jit(solution)/shard_map/slice | solution.py:72
  285.5 8.3 %copy.33 = f32[8,8,256,128]{3,2,1,0:T(8,128)} copy(f32[8,8,256,128]{3,1,2,0:T(8,128)} %bitcast.142) | data formatting | bytes 16777216
  294.2 2.4 fusion.83
  296.6 11.1 %copy.19 = f32[5,16,16,16,128]{4,3,2,1,0:T(8,128)} copy(f32[5,16,16,16,128]{4,1,3,2,0:T(8,128)} %fusion.83) | data formatting | bytes 20971520 | tf_op jit(solution)/shard_map/stack | solution.py:67
  307.7 11.6 %reshape.77 = f32[80,32768]{1,0:T(8,128)} reshape(f32[5,16,16,16,128]{4,3,2,1,0:T(8,128)} %copy.19) | data formatting | bytes 20971520 | tf_op jit(solution)/shard_map/reshape | solution.py:67
  319.3 12.9 %fusion.131 = f32[80,80]{1,0:T(8,128)S(1)} fusion(f32[80,32768]{1,0:T(8,128)} %reshape.77), kind=kOutput, calls=%fused_computation.216 | convolution fusion | flops 2516582400 | bytes 10511360 | tf_op jit(solution)/shard_map/dot_general | solution.py:68
  332.2 83.7 %psum.15 = f32[80,80]{1,0:T(8,128)S(1)} all-reduce(f32[80,80]{1,0:T(8,128)S(1)} %fusion.131), channel_id=1, replica_groups=mesh['grp'=4,'dom'=32] {'grp','dom'}, use_global_device_ids=true, to_apply=%region_3.6 | all-reduce | flops 6400 | bytes 51200 | tf_op jit(solution)/shard_map/psum | solution.py:69
  416.2 5.8 %cholesky.55 = f32[64,64]{1,0:T(8,128)S(1)} custom-call(f32[64,64]{1,0:T(8,128)S(1)} %fusion.106), custom_call_target="Cholesky" | custom-call | tf_op jit(solution)/shard_map/jit(cholesky)/cholesky | solution.py:42
  422.8 0.7 fusion.94
  423.4 4.9 %custom-call.9 = f32[1,64,64]{1,2,0:T(8,128)S(1)} custom-call(f32[1,64,64]{2,1,0:T(8,128)S(1)} %fusion.94), custom_call_target="InvertDiagBlocksLowerTriangular" | custom-call | tf_op jit(solution)/shard_map/jit(_cho_solve)/triangular_solve | solution.py:43
  429.0 12.5 %fusion.4 = f32[16,16,16,128]{3,0,2,1:T(8,128)S(1)} fusion(f32[16,16,128,64]{2,1,0,3:T(8,128)} %bitcast.140, f32[64,16]{0,1:T(8,128)S(1)} %fusion.103), kind=kOutput, calls=%fused_computation.6 | convolution fusion | flops 402653184 | bytes 10489856 | tf_op jit(solution)/shard_map/dot_general | solution.py:71
  441.5 12.9 %fusion.84 = f32[16,16,16,128]{3,0,2,1:T(8,128)S(1)} fusion(f32[16,16,16,128]{3,0,2,1:T(8,128)S(1)} %fusion.4, f32[16,16,128,64]{2,1,0,3:T(8,128)} %bitcast.139, f32[64,16]{0,1:T(8,128)S(1)} %fusion.108), kind=kOutput, calls=%fused_computation.135 | convolution fusion | flops 403177472 | bytes 12587008 | tf_op jit(solution)/shard_map/dot_general | solution.py:71
  454.4 2.0 copy.25
  456.4 5.8 %copy.34 = f32[10,8,256,128]{3,2,1,0:T(8,128)} copy(f32[10,8,256,128]{3,1,2,0:T(8,128)S(1)} %bitcast.127) | data formatting | bytes 20971520
  462.2 15.3 %fusion.90 = f32[16,16,16,128]{3,0,2,1:T(8,128)S(1)} fusion(f32[16,16,16,128]{3,0,2,1:T(8,128)S(1)} %copy-done.1, f32[80,16,1,1]{0,1,3,2:T(8,128)S(1)} %convolution_bitcast_fusion, f32[16,16,128,80]{2,1,0,3:T(8,128)} %bitcast.132), kind=kOutput, calls=%fused_computation.137 | convolution fusion | flops 503840768 | bytes 14685184 | tf_op jit(solution)/shard_map/dot_general | solution.py:74
  477.5 2.0 copy.26
  (100 shorter events, 6.1 us)
Async XLA Ops:
  1.3 8.8 %copy-start.16 = (f32[16,16,128]{2,1,0:T(8,128)S(1)}, f32[16,16,128]{2,1,0:T(8,128)}, u32[]{:S(2)}) copy-start(f32[16,16,128]{2,1,0:T(8,128)} %param.7) | copy-start | bytes 393220
  5.7 5.6 %collective-permute-start.1 = (f32[16,1,16,128]{3,0,2,1:T(8,128)S(1)}, f32[16,1,16,128]{3,0,2,1:T(8,128)S(1)}, u32[]{:S(2)}, u32[]{:S(2)}) collective-permute-start(f32[16,1,16,128]{3,0,2,1:T(8,128)S(1)} %get-tuple-element.36), channel_id=1, source_target_pairs={{1,0},{2,1},{3,2},{4,3},{5,4},{6,5},{7,6},{8,7},{9,8},{10,9},{11,1... | collective-permute-start | bytes 393224 | tf_op jit(solution)/shard_map/ppermute | solution.py:18
  7.0 4.0 collective-permute-start
  13.7 9.3 %copy-start.2 = (f32[16,16,16,128]{3,0,2,1:T(8,128)}, f32[16,16,16,128]{3,0,2,1:T(8,128)S(1)}, u32[]{:S(2)}) copy-start(f32[16,16,16,128]{3,0,2,1:T(8,128)S(1)} %get-tuple-element.19) | copy-start | bytes 6291460
  13.8 5.4 %collective-permute-start.2 = (f32[16,1,16,128]{3,0,2,1:T(8,128)S(1)}, f32[16,1,16,128]{3,0,2,1:T(8,128)S(1)}, u32[]{:S(2)}, u32[]{:S(2)}) collective-permute-start(f32[16,1,16,128]{3,0,2,1:T(8,128)S(1)} %get-tuple-element.35), channel_id=1, source_target_pairs={{0,1},{1,2},{2,3},{3,4},{4,5},{5,6},{6,7},{7,8},{8,9},{9,10},{10,1... | collective-permute-start | bytes 393224 | tf_op jit(solution)/shard_map/ppermute | solution.py:18
  17.8 5.2 %collective-permute-start.3 = (f32[16,1,16,128]{3,0,2,1:T(8,128)S(1)}, f32[16,1,16,128]{3,0,2,1:T(8,128)S(1)}, u32[]{:S(2)}, u32[]{:S(2)}) collective-permute-start(f32[16,1,16,128]{3,0,2,1:T(8,128)S(1)} %get-tuple-element.34), channel_id=1, source_target_pairs={{1,0},{2,1},{3,2},{4,3},{5,4},{6,5},{7,6},{8,7},{9,8},{10,9},{11,1... | collective-permute-start | bytes 393224 | tf_op jit(solution)/shard_map/ppermute | solution.py:18
  25.6 8.8 %copy-start.4 = (f32[16,16,16,128]{3,0,2,1:T(8,128)}, f32[16,16,16,128]{3,0,2,1:T(8,128)S(1)}, u32[]{:S(2)}) copy-start(f32[16,16,16,128]{3,0,2,1:T(8,128)S(1)} %get-tuple-element.17) | copy-start | bytes 6291460
  25.6 6.8 %collective-permute-start.4 = (f32[16,1,16,128]{3,0,2,1:T(8,128)S(1)}, f32[16,1,16,128]{3,0,2,1:T(8,128)S(1)}, u32[]{:S(2)}, u32[]{:S(2)}) collective-permute-start(f32[16,1,16,128]{3,0,2,1:T(8,128)S(1)} %get-tuple-element.33), channel_id=1, source_target_pairs={{0,1},{1,2},{2,3},{3,4},{4,5},{5,6},{6,7},{7,8},{8,9},{9,10},{10,1... | collective-permute-start | bytes 393224 | tf_op jit(solution)/shard_map/ppermute | solution.py:18
  31.2 3.2 collective-permute-start.5
  37.0 1.3 copy-start.6
  38.4 6.8 %collective-permute-start.6 = (f32[16,1,16,128]{3,0,2,1:T(8,128)S(1)}, f32[16,1,16,128]{3,0,2,1:T(8,128)S(1)}, u32[]{:S(2)}, u32[]{:S(2)}) collective-permute-start(f32[16,1,16,128]{3,0,2,1:T(8,128)S(1)} %get-tuple-element.31), channel_id=1, source_target_pairs={{0,1},{1,2},{2,3},{3,4},{4,5},{5,6},{6,7},{7,8},{8,9},{9,10},{10,1... | collective-permute-start | bytes 393224 | tf_op jit(solution)/shard_map/ppermute | solution.py:18
  43.6 3.6 copy-start.7
  43.6 3.6 collective-permute-start.7
  206.5 5.9 %copy-start = (f32[16,16,16,128]{3,0,2,1:T(8,128)}, f32[16,16,16,128]{3,0,2,1:T(8,128)S(1)}, u32[]{:S(2)}) copy-start(f32[16,16,16,128]{3,0,2,1:T(8,128)S(1)} %get-tuple-element.39) | copy-start | bytes 6291460
  206.5 3.1 collective-permute-start.8
  208.3 4.1 collective-permute-start.9
  214.0 6.8 %copy-start.15 = (f32[5,16,16,16,128]{4,1,3,2,0:T(8,128)}, f32[5,16,16,16,128]{4,1,3,2,0:T(8,128)S(1)}, u32[]{:S(2)}) copy-start(f32[5,16,16,16,128]{4,1,3,2,0:T(8,128)S(1)} %get-tuple-element.12) | copy-start | bytes 31457284
  214.0 8.8 %copy-start.9 = (f32[16,16,16,128]{3,0,2,1:T(8,128)}, f32[16,16,16,128]{3,0,2,1:T(8,128)S(1)}, u32[]{:S(2)}) copy-start(f32[16,16,16,128]{3,0,2,1:T(8,128)S(1)} %get-tuple-element.13) | copy-start | bytes 6291460
  214.1 6.8 %collective-permute-start.10 = (f32[16,1,16,128]{3,0,2,1:T(8,128)S(1)}, f32[16,1,16,128]{3,0,2,1:T(8,128)S(1)}, u32[]{:S(2)}, u32[]{:S(2)}) collective-permute-start(f32[16,1,16,128]{3,0,2,1:T(8,128)S(1)} %get-tuple-element.27), channel_id=1, source_target_pairs={{0,1},{1,2},{2,3},{3,4},{4,5},{5,6},{6,7},{7,8},{8,9},{9,10},{10,1... | collective-permute-start | bytes 393224 | tf_op jit(solution)/shard_map/ppermute | solution.py:18
  219.5 3.2 collective-permute-start.11
  222.8 8.9 %copy-start.3 = (f32[16,16,16,128]{3,0,2,1:T(8,128)S(1)}, f32[16,16,16,128]{3,0,2,1:T(8,128)}, u32[]{:S(2)}) copy-start(f32[16,16,16,128]{3,0,2,1:T(8,128)} %copy-done.2) | copy-start | bytes 6291460
  222.8 8.9 %copy-start.5 = (f32[16,16,16,128]{3,0,2,1:T(8,128)S(1)}, f32[16,16,16,128]{3,0,2,1:T(8,128)}, u32[]{:S(2)}) copy-start(f32[16,16,16,128]{3,0,2,1:T(8,128)} %copy-done.4) | copy-start | bytes 6291460
  222.8 8.9 %copy-start.8 = (f32[16,16,16,128]{3,0,2,1:T(8,128)S(1)}, f32[16,16,16,128]{3,0,2,1:T(8,128)}, u32[]{:S(2)}) copy-start(f32[16,16,16,128]{3,0,2,1:T(8,128)} %copy-done.6) | copy-start | bytes 6291460
  225.4 1.3 copy-start.11
  226.8 30.8 %collective-permute-start.12 = (f32[16,1,16,128]{3,0,2,1:T(8,128)S(1)}, f32[16,1,16,128]{3,0,2,1:T(8,128)S(1)}, u32[]{:S(2)}, u32[]{:S(2)}) collective-permute-start(f32[16,1,16,128]{3,0,2,1:T(8,128)S(1)} %get-tuple-element.25), channel_id=1, source_target_pairs={{0,1},{1,2},{2,3},{3,4},{4,5},{5,6},{6,7},{7,8},{8,9},{9,10},{10,1... | collective-permute-start | bytes 393224 | tf_op jit(solution)/shard_map/ppermute | solution.py:18
  248.0 9.6 %copy-start.12 = (f32[16,16,16,128]{3,0,2,1:T(8,128)S(1)}, f32[16,16,16,128]{3,0,2,1:T(8,128)}, u32[]{:S(2)}) copy-start(f32[16,16,16,128]{3,0,2,1:T(8,128)} %copy-done.11) | copy-start | bytes 6291460
  256.3 3.2 collective-permute-start.13
  259.5 9.6 %copy-start.1 = (f32[16,16,16,128]{3,0,2,1:T(8,128)S(1)}, f32[16,16,16,128]{3,0,2,1:T(8,128)}, u32[]{:S(2)}) copy-start(f32[16,16,16,128]{3,0,2,1:T(8,128)} %copy-done) | copy-start | bytes 6291460
  259.5 9.6 %copy-start.10 = (f32[16,16,16,128]{3,0,2,1:T(8,128)S(1)}, f32[16,16,16,128]{3,0,2,1:T(8,128)}, u32[]{:S(2)}) copy-start(f32[16,16,16,128]{3,0,2,1:T(8,128)} %copy-done.9) | copy-start | bytes 6291460
  262.2 6.9 %copy-start.13 = (f32[16,16,16,128]{3,0,2,1:T(8,128)}, f32[16,16,16,128]{3,0,2,1:T(8,128)S(1)}, u32[]{:S(2)}) copy-start(f32[16,16,16,128]{3,0,2,1:T(8,128)S(1)} %get-tuple-element.9) | copy-start | bytes 6291460
  262.2 31.9 %collective-permute-start.15 = (f32[16,1,16,128]{3,0,2,1:T(8,128)S(1)}, f32[16,1,16,128]{3,0,2,1:T(8,128)S(1)}, u32[]{:S(2)}, u32[]{:S(2)}) collective-permute-start(f32[16,1,16,128]{3,0,2,1:T(8,128)S(1)} %get-tuple-element.22), channel_id=1, source_target_pairs={{1,0},{2,1},{3,2},{4,3},{5,4},{6,5},{7,6},{8,7},{9,8},{10,9},{11,1... | collective-permute-start | bytes 393224 | tf_op jit(solution)/shard_map/ppermute | solution.py:18
  263.5 30.3 %collective-permute-start.14 = (f32[16,1,16,128]{3,0,2,1:T(8,128)S(1)}, f32[16,1,16,128]{3,0,2,1:T(8,128)S(1)}, u32[]{:S(2)}, u32[]{:S(2)}) collective-permute-start(f32[16,1,16,128]{3,0,2,1:T(8,128)S(1)} %get-tuple-element.23), channel_id=1, source_target_pairs={{0,1},{1,2},{2,3},{3,4},{4,5},{5,6},{6,7},{7,8},{8,9},{9,10},{10,1... | collective-permute-start | bytes 393224 | tf_op jit(solution)/shard_map/ppermute | solution.py:18
  285.5 8.3 %copy-start.14 = (f32[16,16,16,128]{3,0,2,1:T(8,128)S(1)}, f32[16,16,16,128]{3,0,2,1:T(8,128)}, u32[]{:S(2)}) copy-start(f32[16,16,16,128]{3,0,2,1:T(8,128)} %copy-done.13) | copy-start | bytes 6291460
  429.0 27.4 %slice-start = ((s8[10485760]{0:T(1024)(128)(4,1)}), s8[4194304]{0:T(1024)(128)(4,1)S(1)}, s32[]{:S(2)}) async-start(s8[10485760]{0:T(1024)(128)(4,1)} %bitcast.125), calls=%async_computation | async-start | bytes 8388608
  429.0 27.4 %slice-start.1 = ((s8[10485760]{0:T(1024)(128)(4,1)}), s8[4194304]{0:T(1024)(128)(4,1)S(1)}, s32[]{:S(2)}) async-start(s8[10485760]{0:T(1024)(128)(4,1)} %bitcast.125), calls=%async_computation.1 | async-start | bytes 8388608
  441.5 14.9 %slice-start.2 = ((s8[10485760]{0:T(1024)(128)(4,1)}), s8[2097152]{0:T(1024)(128)(4,1)S(1)}, s32[]{:S(2)}) async-start(s8[10485760]{0:T(1024)(128)(4,1)} %bitcast.125), calls=%async_computation.2 | async-start | bytes 4194304
where the time goes:
time: 486 us; the launch traced here: 480 us
  blocking collectives  175 us (36%)
  local copies, waits for them, and re-layouts  112 us (23%)
  matrix products  79.1 us (16%)
  other arithmetic  54 us (11%)
  starting transfers between devices  45.9 us (9%)
  waiting for transfers between devices  11.8 us (2%)
    psum x2, blocking collectives, local(): gram = lax.psum(local_gram, ('grp', 'dom'))  175 us
    ppermute x16, starting transfers between devices, passed_along(): return lax.ppermute(block, axis, route)  45.9 us
    unnamed x46, local copies, waits for them, and re-layouts  35 us
    another operation x4, local copies, waits for them, and re-layouts, local(): panel = jnp.stack(basis).reshape((SSTEP + 1) * NRHS, -1)  34.1 us
    dot_general x2, matrix products, local(): jnp.dot(step.T, panel, precision=lax.Precision.HIGHEST)  26.5 us
    dot_general x2, matrix products, local(): local_gram = jnp.dot(panel, panel.T, precision=lax.Precision.HIGHEST)  25.6 us
    dot_general x2, matrix products, local(): jnp.dot(coef.T, panel[:SSTEP * NRHS], precision=lax.Precision.HIGHEST)  25.4 us
    reshape x2, local copies, waits for them, and re-layouts, local(): panel = jnp.stack(basis).reshape((SSTEP + 1) * NRHS, -1)  23.2 us
  transfers between devices with their start and end apart: 16, of which 6 were waited for; matrix products, arithmetic and copies ran while one was open for 11% of the time, Pallas kernels for 0%

commit v1 on v0

v1 whole, which is shorter than its diff:
```python
import functools

import jax
import jax.numpy as jnp
from jax import lax
from jax.experimental import pallas as pl
from jax.experimental.pallas import tpu as pltpu
from jax.sharding import PartitionSpec as P

NRHS = 16
SSTEP = 4
SHIFT = 8.5
SCALE = 7.5
CX = 16
NY = 16
NZ = 128
GHOST = 8
KB = SSTEP + 1
PIECE = KB * NRHS
AXES = ("grp", "dom")
F32 = jnp.float32
BF16 = jnp.bfloat16


def pieces(value):
    hi = value.astype(BF16)
    rest = value - hi.astype(F32)
    mid = rest.astype(BF16)
    lo = (rest - mid.astype(F32)).astype(BF16)
    return hi, mid, lo


def store_pieces(panel, plane, y, power, value):
    for i, part in enumerate(pieces(value)):
        panel[plane, y, pl.ds(i * PIECE + power * NRHS, NRHS), :] = part


def plane_step(src, dst, coef, weight, plane, panel, panel_plane, power):
    lane = lax.broadcasted_iota(jnp.int32, (NRHS, NZ), 1)
    first = lane == 0
    last = lane == NZ - 1
    zero = jnp.zeros((NRHS, NZ), F32)
    before = zero
    centre = src[plane, 0]
    for y in range(NY):
        after = src[plane, y + 1] if y + 1 < NY else zero
        beside = src[plane - 1, y] + src[plane + 1, y] + (before + after)
        beside = beside + jnp.where(first, 0.0, pltpu.roll(centre, 1, 1))
        beside = beside + jnp.where(last, 0.0, pltpu.roll(centre, NZ - 1, 1))
        value = coef[plane, pl.ds(y, 1), :] * centre - weight * beside
        if dst is not None:
            dst[plane, y] = value
        if panel is not None:
            store_pieces(panel, panel_plane, y, power, value)
        before, centre = centre, after


def moments(panel, start, stop):
    def body(plane, acc):
        for y in range(0, NY, 2):
            def rows(at, size):
                return jnp.concatenate(
                    [panel[plane, y, pl.ds(at, size), :], panel[plane, y + 1, pl.ds(at, size), :]], 1
                )

            left = jnp.concatenate(
                [rows(0, NRHS), rows(PIECE, NRHS), rows(SSTEP * NRHS, NRHS), rows(PIECE + SSTEP * NRHS, NRHS)], 0
            )
            right = rows(0, 2 * PIECE)
            acc = acc + lax.dot_general(
                left, right, (((1,), (1,)), ((), ())), preferred_element_type=F32
            )
        return acc

    acc = lax.fori_loop(start, stop, body, jnp.zeros((4 * NRHS, 2 * PIECE), F32))
    low = acc[:NRHS] + acc[NRHS : 2 * NRHS]
    high = acc[2 * NRHS : 3 * NRHS] + acc[3 * NRHS :]
    low = low[:, :PIECE] + low[:, PIECE:]
    high = high[:, :PIECE] + high[:, PIECE:]
    return jnp.concatenate([low, high[:, NRHS : 4 * NRHS]], 1)


def solve(mom):
    size = SSTEP * NRHS
    shifted = jnp.concatenate([mom[:, NRHS:], mom[:, :NRHS]], 1)
    band = SHIFT * mom + SCALE * shifted
    blocks = [band[:, i * NRHS : i * NRHS + size] for i in range(SSTEP)]
    right = mom[:, :size]
    work = jnp.concatenate(blocks + [right], 0)
    lane = lax.broadcasted_iota(jnp.int32, (1, size), 1)
    scale = jnp.zeros((1, size), F32)
    for j in range(size):
        base = j // 8 * 8
        tail = work[base:]
        row = tail[j - base : j - base + 1]
        inv = 1.0 / row[:, j : j + 1]
        scale = jnp.where(lane == j, inv, scale)
        row = jnp.where(lane == j, 0.0, row * inv)
        tail = tail - tail[:, j : j + 1] * row
        work = tail if base == 0 else jnp.concatenate([work[:base], tail], 0)
    return work[size:] * scale


def coef_rows(coef_t):
    size = SSTEP * NRHS
    pad = jnp.zeros((NRHS, NRHS), F32)
    eye = (
        lax.broadcasted_iota(jnp.int32, (NRHS, PIECE), 0)
        == lax.broadcasted_iota(jnp.int32, (NRHS, PIECE), 1)
    ).astype(F32)
    same = jnp.concatenate([coef_t, pad], 1)
    up = jnp.concatenate([pad, coef_t], 1)
    left = eye - (SHIFT * same + SCALE * up)
    l_hi, l_mid, l_lo = pieces(left)
    c_hi, c_mid, _ = pieces(same)
    none = jnp.zeros((NRHS, PIECE), BF16)
    rows = [
        [l_hi, l_hi, l_hi],
        [l_mid, l_mid, none],
        [l_lo, none, none],
        [c_hi, c_hi, none],
        [c_mid, none, none],
    ]
    return jnp.concatenate([jnp.concatenate(r, 1) for r in rows], 0)


def combine(coefs, panel, plane, y):
    block = jnp.concatenate([panel[plane, y], panel[plane, y + 1]], 1)
    out = jnp.dot(coefs, block, preferred_element_type=F32)
    left = out[:NRHS] + out[NRHS : 2 * NRHS] + out[2 * NRHS : 3 * NRHS]
    step = out[3 * NRHS : 4 * NRHS] + out[4 * NRHS :]
    return left, step


def first_kernel(info, right, lower, upper, diag, panel, ghosts, coef, mom, field_a, field_b):
    count = info[0]
    has_lower = info[1]
    has_upper = info[2]
    rows = NY * CX
    ghost_rows = GHOST * NY
    total = CX + 2 * GHOST

    def weight_of(plane):
        inside = (
            ((plane >= GHOST) | (has_lower > 0))
            & ((plane < GHOST + count) | (has_upper > 0))
            & (plane < 2 * GHOST + count)
        )
        return jnp.where(inside, 1.0 / SCALE, 0.0).astype(F32)

    def load_own(p, carry):
        live = (p < count).astype(F32)
        for y in range(NY):
            value = right[pl.Slice(p * NY + y, NRHS, rows), :]
            field_a[GHOST + p, y] = value * live
        coef[GHOST + p] = (diag[p] + (6.0 - SHIFT)) * (1.0 / SCALE)
        return carry

    def load_ghost(p, carry):
        for src, at in ((lower, p), (upper, GHOST + count + p)):
            for y in range(NY):
                field_a[at, y] = src[pl.Slice(p * NY + y, NRHS, ghost_rows), :]
            d = src[pl.ds(NRHS * ghost_rows + p * NY, NY), :]
            coef[at] = (d + (6.0 - SHIFT)) * (1.0 / SCALE)
        return carry

    for p in range(GHOST):
        coef[GHOST + CX + p] = jnp.zeros((NY, NZ), F32)
        field_a[GHOST + CX + p] = jnp.zeros((NY, NRHS, NZ), F32)
    lax.fori_loop(0, CX, load_own, 0)
    lax.fori_loop(0, GHOST, load_ghost, 0)

    parts = (
        (SSTEP, GHOST, ghosts, SSTEP),
        (GHOST, GHOST + CX, panel, GHOST),
        (GHOST + CX, total - SSTEP, ghosts, GHOST + CX - SSTEP),
    )
    for start, stop, store, base in parts:

        def split_body(p, carry, store=store, base=base):
            for y in range(NY):
                store_pieces(store, p - base, y, 0, field_a[p, y])
            return carry

        lax.fori_loop(start, stop, split_body, 0)
    fields = (field_a, field_b)
    for power in range(1, SSTEP + 1):
        src, dst = fields[(power - 1) % 2], fields[power % 2]

        def bare(p, carry, src=src, dst=dst, power=power):
            plane_step(src, dst, coef, weight_of(p), p, None, p, power)
            return carry

        if power < SSTEP:
            lax.fori_loop(power, SSTEP, bare, 0)
            lax.fori_loop(total - SSTEP, total - power, bare, 0)
        for start, stop, store, base in parts:

            def full(p, carry, src=src, dst=dst, power=power, store=store, base=base):
                plane_step(src, dst, coef, weight_of(p), p, store, p - base, power)
                return carry

            lax.fori_loop(start, stop, full, 0)
    mom[...] = moments(panel, 0, count)


def middle_kernel(info, mom_in, coef, panel_in, ghosts, panel, mom, iterate, field_a, field_b):
    count = info[0]
    has_lower = info[1]
    has_upper = info[2]
    total = CX + 2 * SSTEP

    def weight_of(plane):
        inside = (
            ((plane >= SSTEP) | (has_lower > 0))
            & ((plane < SSTEP + count) | (has_upper > 0))
            & (plane < 2 * SSTEP + count)
        )
        return jnp.where(inside, 1.0 / SCALE, 0.0).astype(F32)

    coefs = coef_rows(solve(mom_in[...]))

    def update(p, own, store, base, carry):
        for y in range(0, NY, 2):
            left, step = combine(coefs, store, p - base, y)
            for k in range(2):
                value = left[:, k * NZ : (k + 1) * NZ]
                field_a[p, y + k] = value
                if own:
                    store_pieces(panel, p - SSTEP, y + k, 0, value)
                    iterate[p - SSTEP, y + k] = step[:, k * NZ : (k + 1) * NZ]
        return carry

    lax.fori_loop(0, SSTEP, lambda p, c: update(p, False, ghosts, 0, c), 0)
    lax.fori_loop(SSTEP, SSTEP + CX, lambda p, c: update(p, True, panel_in, SSTEP, c), 0)
    lax.fori_loop(SSTEP + CX, total, lambda p, c: update(p, False, ghosts, CX, c), 0)
    shifted = coef.at[pl.ds(SSTEP, total)]
    fields = (field_a, field_b)
    for power in range(1, SSTEP + 1):
        src, dst = fields[(power - 1) % 2], fields[power % 2]
        if power == SSTEP:
            dst = None

        def bare(p, carry, src=src, dst=dst, power=power):
            plane_step(src, dst, shifted, weight_of(p), p, None, p, power)
            return carry

        def full(p, carry, src=src, dst=dst, power=power):
            plane_step(src, dst, shifted, weight_of(p), p, panel, p - SSTEP, power)
            return carry

        if power < SSTEP:
            lax.fori_loop(power, SSTEP, bare, 0)
            lax.fori_loop(total - SSTEP, total - power, bare, 0)
        lax.fori_loop(SSTEP, total - SSTEP, full, 0)
    mom[...] = moments(panel, 0, count)


def last_kernel(info, mom_in, panel, iterate, solution_field, residual):
    count = info[0]
    rows = NY * CX
    coefs = coef_rows(solve(mom_in[...]))

    def live(p, carry):
        for y in range(0, NY, 2):
            left, step = combine(coefs, panel, p, y)
            for k in range(2):
                at = pl.Slice(p * NY + y + k, NRHS, rows)
                residual[at, :] = left[:, k * NZ : (k + 1) * NZ]
                solution_field[at, :] = iterate[p, y + k] + step[:, k * NZ : (k + 1) * NZ]
        return carry

    def dead(p, carry):
        for y in range(NY):
            at = pl.Slice(p * NY + y, NRHS, rows)
            residual[at, :] = jnp.zeros((NRHS, NZ), F32)
            solution_field[at, :] = jnp.zeros((NRHS, NZ), F32)
        return carry

    lax.fori_loop(0, count, live, 0)
    lax.fori_loop(count, CX, dead, 0)


SMEM_SPEC = pl.BlockSpec(memory_space=pltpu.SMEM)
VMEM_SPEC = pl.BlockSpec(memory_space=pltpu.VMEM)


def call(body, limit, operands, outs, scratch, kept_operands=(), aliases={}):
    operands = [
        pltpu.with_memory_space_constraint(x, pltpu.VMEM) if i in kept_operands else x
        for i, x in enumerate(operands)
    ]
    return pl.pallas_call(
        body,
        out_shape=[pltpu.VMEM(s, d) if kept else jax.ShapeDtypeStruct(s, d) for s, d, kept in outs],
        in_specs=[SMEM_SPEC] + [VMEM_SPEC] * (len(operands) - 1),
        out_specs=[VMEM_SPEC] * len(outs),
        scratch_shapes=scratch,
        input_output_aliases=aliases,
        compiler_params=pltpu.CompilerParams(vmem_limit_bytes=limit * 1024 * 1024),
    )(*operands)


def reduce_all(value, size, last):
    rounds = []
    if size == 128:
        rounds = [(1, 2), (2, 4), (8, 4), (32, 4)]
    else:
        stride = 1
        while stride < size:
            rounds.append((stride, 2))
            stride *= 2
    for stride, width in rounds:
        total = value
        for turn in range(1, width):
            route = []
            for i in range(size):
                place = i // stride % width
                route.append((i, i + ((place + turn) % width - place) * stride))
            total = total + lax.ppermute(value, AXES, route)
        value = total
    return value


def local(right_side, diagonal, counts):
    count = counts[0]
    size = lax.axis_size(AXES)
    me = lax.axis_index(AXES)
    info = jnp.stack([count, me, size - 1 - me]).astype(jnp.int32)
    both = jnp.concatenate([right_side, diagonal[None]], 0)
    tops = lax.dynamic_slice_in_dim(both, count - GHOST, GHOST, 1)
    firsts = both[:, :GHOST]
    lower = lax.ppermute(tops, AXES, [(i, i + 1) for i in range(size - 1)])
    upper = lax.ppermute(firsts, AXES, [(i + 1, i) for i in range(size - 1)])
    ghost_shape = ((NRHS + 1) * GHOST * NY, NZ)
    field = (NY, NRHS, NZ)
    total = CX + 2 * GHOST
    middle = CX + 2 * SSTEP
    panel1, ghosts, coef, mom = call(
        first_kernel,
        16,
        (
            info,
            right_side.reshape(NRHS * CX * NY, NZ),
            lower.reshape(ghost_shape),
            upper.reshape(ghost_shape),
            diagonal,
        ),
        [
            ((CX, NY, 3 * PIECE, NZ), BF16, True),
            ((2 * SSTEP, NY, 3 * PIECE, NZ), BF16, True),
            ((total, NY, NZ), F32, True),
            ((NRHS, NZ), F32, False),
        ],
        [pltpu.VMEM((total,) + field, F32), pltpu.VMEM((total,) + field, F32)],
    )
    mom = reduce_all(mom, size, False)
    panel2, mom, iterate = call(
        middle_kernel,
        8,
        (info, mom, coef, panel1, ghosts),
        [
            ((CX, NY, 3 * PIECE, NZ), BF16, True),
            ((NRHS, NZ), F32, False),
            ((CX,) + field, F32, True),
        ],
        [pltpu.VMEM((middle,) + field, F32), pltpu.VMEM((middle,) + field, F32)],
        (2, 3, 4),
    )
    mom = reduce_all(mom, size, True)
    out = (NRHS * CX * NY, NZ)
    solution_field, residual = call(
        last_kernel,
        8,
        (info, mom, panel2, iterate),
        [(out, F32, False), (out, F32, False)],
        [],
        (2, 3),
    )
    return (solution_field.reshape(right_side.shape), residual.reshape(right_side.shape))


def solution(mesh):
    in_specs = (
        P(None, AXES, None, None),
        P(AXES, None, None),
        P(AXES),
    )
    out_specs = (P(None, AXES, None, None), P(None, AXES, None, None))
    return jax.shard_map(local, mesh=mesh, in_specs=in_specs, out_specs=out_specs, check_vma=False)
```

time: 486 us -> 151 us (0.31); the launches traced: 480 us -> 152 us
  blocking collectives: 175 us -> 0 us
  local copies, waits for them, and re-layouts: 112 us -> 4.73 us
  matrix products: 79.1 us -> 0 us
  Pallas kernels: 0 us -> 69.1 us
  other arithmetic: 54 us -> 2.95 us
  waiting for transfers between devices: 11.8 us -> 29.7 us
    psum x2 -> x0, blocking collectives: 175 us -> none  [local(): gram = lax.psum(local_gram, ('grp', 'dom'))]
    dot_general x10 -> x0, matrix products: 78.2 us -> none  [the longest x2 26.5 us: local(): jnp.dot(step.T, panel, precision=lax.Precision.HIGHEST)]
    pallas_call x0 -> x3, Pallas kernels: none -> 69.1 us  [call(): pl.pallas_call(body, out_shape=[pltpu.VMEM(s, d) if kept else jax.ShapeDt...]
    another operation x4 -> x0, local copies, waits for them, and re-layouts: 34.1 us -> none  [local(): panel = jnp.stack(basis).reshape((SSTEP + 1) * NRHS, -1)]
    another operation x14 -> x1, other arithmetic: 31 us -> 0.08 us  [local(): info = jnp.stack([count, me, size - 1 - me]).astype(jnp.int32)]
    unnamed x46 -> x8, local copies, waits for them, and re-layouts: 35 us -> 4.73 us
    reshape x2 -> x0, local copies, waits for them, and re-layouts: 23.2 us -> none  [local(): panel = jnp.stack(basis).reshape((SSTEP + 1) * NRHS, -1)]
    slice x10 -> x0, local copies, waits for them, and re-layouts: 18.9 us -> none  [the longest x2 18.8 us: local(): panel[:SSTEP * NRHS]]
  transfers between devices with their start and end apart: 16 -> 22, of which waited for: 6 -> 18; matrix products, arithmetic and copies ran while one was open for 11% -> 0% of each run, Pallas kernels for 0% -> 0%
where the time goes in v1:
time: 151 us; the launch traced here: 152 us
  Pallas kernels  69.1 us (46%)
  starting transfers between devices  43.9 us (29%)
  waiting for transfers between devices  29.7 us (20%)
  local copies, waits for them, and re-layouts  4.73 us (3%)
  other arithmetic  2.95 us (2%)
    pallas_call x3, Pallas kernels, call(): pl.pallas_call(body, out_shape=[pltpu.VMEM(s, d) if kept else jax.ShapeDt...  69.1 us
    ppermute x20, starting transfers between devices, reduce_all(): total = total + lax.ppermute(value, AXES, route)  39.5 us
    ppermute x20, waiting for transfers between devices, reduce_all(): total = total + lax.ppermute(value, AXES, route)  27.5 us
    unnamed x8, local copies, waits for them, and re-layouts  4.73 us
    ppermute x1, starting transfers between devices, local(): lower = lax.ppermute(tops, AXES, [(i, i + 1) for i in range(size - 1)])  3.1 us
  transfers between devices with their start and end apart: 22, of which 18 were waited for; matrix products, arithmetic and copies ran while one was open for 0% of the time, Pallas kernels for 0%

profile of v1, /device:TPU:0, one launch (start us, length us, event | category | flops | bytes accessed | tf_op | source)
XLA Modules:
  0.0 151.7 jit_solution(17815534848557241407)
XLA Ops:
  1.3 2.8 %pad_maximum_fusion = (f32[17,8,16,128]{3,2,1,0:T(8,128)}, f32[17,8,16,128]{3,2,1,0:T(8,128)S(1)}) fusion(f32[1,16,16,128]{3,2,1,0:T(8,128)} %bitcast.13, f32[16,16,16,128]{3,2,1,0:T(8,128)} %param.3, s32[]{:T(128)S(6)} %select_n.3), kind=kLoop, calls=%fused_computation.3 | loop fusion | flops 557056 | bytes 4456452 | tf_op jit(solution)/shard_map/concatenate | solution.py:330
  4.1 1.3 collective-permute-start.1
  5.4 3.1 %collective-permute-start = (f32[17,8,16,128]{3,2,1,0:T(8,128)S(1)}, f32[17,8,16,128]{3,2,1,0:T(8,128)S(1)}, u32[]{:S(2)}, u32[]{:S(2)}) collective-permute-start(f32[17,8,16,128]{3,2,1,0:T(8,128)S(1)} %get-tuple-element.21), channel_id=1, source_target_pairs={{0,1},{1,2},{2,3},{3,4},{4,5},{5,6},{6,7},{7,8},{8,9},{9,10},{10,1... | collective-permute-start | bytes 3342344 | tf_op jit(solution)/shard_map/ppermute | solution.py:333
  8.5 0.1 pad_add_fusion.info
  8.6 0.4 collective-permute-done.1
  9.0 1.8 %collective-permute-done = f32[17,8,16,128]{3,2,1,0:T(8,128)S(1)} collective-permute-done((f32[17,8,16,128]{3,2,1,0:T(8,128)S(1)}, f32[17,8,16,128]{3,2,1,0:T(8,128)S(1)}, u32[]{:S(2)}, u32[]{:S(2)}) %collective-permute-start) | collective-permute-done | bytes 1114144 | tf_op jit(solution)/shard_map/ppermute | solution.py:333
  10.8 0.0 copy-start.1
  10.8 1.0 copy-done.1
  11.8 0.0 copy-start
  11.8 1.6 %copy-done = f32[16,16,16,128]{3,2,1,0:T(8,128)S(1)} copy-done((f32[16,16,16,128]{3,2,1,0:T(8,128)S(1)}, f32[16,16,16,128]{3,2,1,0:T(8,128)}, u32[]{:S(2)}) %copy-start) | copy-done | bytes 2097176
  13.4 0.0 copy-start.2
  13.4 1.2 copy-done.2
  14.6 0.0 copy-start.3
  14.6 0.9 copy-done.3
  15.5 25.6 %shard_map.50 = (bf16[16,16,240,128]{3,2,1,0:T(8,128)(2,1)S(1)}, bf16[8,16,240,128]{3,2,1,0:T(8,128)(2,1)S(1)}, f32[32,16,128]{2,1,0:T(8,128)S(1)}, f32[16,128]{1,0:T(8,128)S(1)}) custom-call(s32[3]{0:T(128)S(1)} %pad_add_fusion.info, f32[4096,128]{1,0:T(8,128)S(1)} %bitcast.10, f32[2176,128]{1,0:T(8,128)S(1)} %bitcast.12, f32[2176,128]{1,0:T(8,128)S(1)} %bitcast.11, ...), custom_call_target="tpu_custom_call" | custom-call | tf_op jit(solution)/shard_map/pallas_call | solution.py:293
  41.1 11.3 %collective-permute-start.2 = (f32[16,128]{1,0:T(8,128)S(1)}, f32[16,128]{1,0:T(8,128)S(1)}, u32[]{:S(2)}, u32[]{:S(2)}) collective-permute-start(f32[16,128]{1,0:T(8,128)S(1)} %get-tuple-element.11), channel_id=1, source_target_pairs={{0,1},{1,0},{2,3},{3,2},{4,5},{5,4},{6,7},{7,6},{8,9},{9,8},{10,11... | collective-permute-start | bytes 24584 | tf_op jit(solution)/shard_map/ppermute | solution.py:320
  52.4 0.8 collective-permute-done.2
  53.2 3.9 %collective-permute-start.5 = (f32[16,128]{1,0:T(8,128)S(1)}, f32[16,128]{1,0:T(8,128)S(1)}, u32[]{:S(2)}, u32[]{:S(2)}) collective-permute-start(f32[16,128]{1,0:T(8,128)S(1)} %add.76), channel_id=1, source_target_pairs={{0,6},{1,7},{2,0},{3,1},{4,2},{5,3},{6,4},{7,5},{8,14},{9,15},{10,... | collective-permute-start | bytes 24584 | tf_op jit(solution)/shard_map/ppermute | solution.py:320
  57.1 0.0 collective-permute-start.4
  57.1 0.9 collective-permute-start.3
  58.0 0.5 collective-permute-done.5
  58.5 3.8 %collective-permute-done.4 = f32[16,128]{1,0:T(8,128)S(1)} collective-permute-done((f32[16,128]{1,0:T(8,128)S(1)}, f32[16,128]{1,0:T(8,128)S(1)}, u32[]{:S(2)}, u32[]{:S(2)}) %collective-permute-start.4) | collective-permute-done | bytes 8224 | tf_op jit(solution)/shard_map/ppermute | solution.py:320
  62.3 0.0 collective-permute-done.3
  62.3 6.3 %collective-permute-start.8 = (f32[16,128]{1,0:T(8,128)S(1)}, f32[16,128]{1,0:T(8,128)S(1)}, u32[]{:S(2)}, u32[]{:S(2)}) collective-permute-start(f32[16,128]{1,0:T(8,128)S(1)} %add_add_fusion.5), channel_id=1, source_target_pairs={{0,24},{1,25},{2,26},{3,27},{4,28},{5,29},{6,30},{7,31},{8,0},{9,1... | collective-permute-start | bytes 24584 | tf_op jit(solution)/shard_map/ppermute | solution.py:320
  68.6 0.0 collective-permute-start.7
  68.6 0.9 collective-permute-start.6
  69.6 0.4 collective-permute-done.8
  70.0 3.8 %collective-permute-done.7 = f32[16,128]{1,0:T(8,128)S(1)} collective-permute-done((f32[16,128]{1,0:T(8,128)S(1)}, f32[16,128]{1,0:T(8,128)S(1)}, u32[]{:S(2)}, u32[]{:S(2)}) %collective-permute-start.7) | collective-permute-done | bytes 8224 | tf_op jit(solution)/shard_map/ppermute | solution.py:320
  73.8 0.0 collective-permute-done.6
  73.8 5.7 %collective-permute-start.11 = (f32[16,128]{1,0:T(8,128)S(1)}, f32[16,128]{1,0:T(8,128)S(1)}, u32[]{:S(2)}, u32[]{:S(2)}) collective-permute-start(f32[16,128]{1,0:T(8,128)S(1)} %add_add_fusion.4), channel_id=1, source_target_pairs={{0,96},{1,97},{2,98},{3,99},{4,100},{5,101},{6,102},{7,103},{8,104... | collective-permute-start | bytes 24584 | tf_op jit(solution)/shard_map/ppermute | solution.py:320
  79.5 0.0 collective-permute-start.10
  79.5 0.9 collective-permute-start.9
  80.4 0.4 collective-permute-done.11
  80.9 3.8 %collective-permute-done.10 = f32[16,128]{1,0:T(8,128)S(1)} collective-permute-done((f32[16,128]{1,0:T(8,128)S(1)}, f32[16,128]{1,0:T(8,128)S(1)}, u32[]{:S(2)}, u32[]{:S(2)}) %collective-permute-start.10) | collective-permute-done | bytes 8224 | tf_op jit(solution)/shard_map/ppermute | solution.py:320
  84.7 0.0 collective-permute-done.9
  84.7 29.9 %shard_map.51 = (bf16[16,16,240,128]{3,2,1,0:T(8,128)(2,1)S(1)}, f32[16,128]{1,0:T(8,128)S(1)}, f32[16,16,16,128]{3,2,1,0:T(8,128)S(1)}) custom-call(s32[3]{0:T(128)S(1)} %pad_add_fusion.info, f32[16,128]{1,0:T(8,128)S(1)} %add_add_fusion.3.mom_in, f32[32,16,128]{2,1,0:T(8,128)S(1)} %get-tuple-element.12.coef, ...), custom_call_target="tpu_custom_call" | custom-call | tf_op jit(solution)/shard_map/pallas_call | solution.py:293
  114.6 0.0 collective-permute-start.12
  114.6 1.2 collective-permute-done.12
  115.7 1.7 %collective-permute-start.15 = (f32[16,128]{1,0:T(8,128)S(1)}, f32[16,128]{1,0:T(8,128)S(1)}, u32[]{:S(2)}, u32[]{:S(2)}) collective-permute-start(f32[16,128]{1,0:T(8,128)S(1)} %add.86), channel_id=1, source_target_pairs={{0,6},{1,7},{2,0},{3,1},{4,2},{5,3},{6,4},{7,5},{8,14},{9,15},{10,... | collective-permute-start | bytes 24584 | tf_op jit(solution)/shard_map/ppermute | solution.py:320
  117.4 0.3 collective-permute-start.14
  117.7 0.6 collective-permute-start.13
  118.3 1.1 collective-permute-done.15
  119.4 3.2 %collective-permute-done.14 = f32[16,128]{1,0:T(8,128)S(1)} collective-permute-done((f32[16,128]{1,0:T(8,128)S(1)}, f32[16,128]{1,0:T(8,128)S(1)}, u32[]{:S(2)}, u32[]{:S(2)}) %collective-permute-start.14) | collective-permute-done | bytes 8224 | tf_op jit(solution)/shard_map/ppermute | solution.py:320
  122.6 0.1 collective-permute-done.13
  122.7 1.1 collective-permute-start.18
  123.8 2.2 %collective-permute-start.17 = (f32[16,128]{1,0:T(8,128)S(1)}, f32[16,128]{1,0:T(8,128)S(1)}, u32[]{:S(2)}, u32[]{:S(2)}) collective-permute-start(f32[16,128]{1,0:T(8,128)S(1)} %add_add_fusion.2), channel_id=1, source_target_pairs={{0,16},{1,17},{2,18},{3,19},{4,20},{5,21},{6,22},{7,23},{8,24},{9,... | collective-permute-start | bytes 24584 | tf_op jit(solution)/shard_map/ppermute | solution.py:320
  125.9 0.0 collective-permute-start.16
  125.9 0.4 collective-permute-done.18
  126.3 2.6 %collective-permute-done.17 = f32[16,128]{1,0:T(8,128)S(1)} collective-permute-done((f32[16,128]{1,0:T(8,128)S(1)}, f32[16,128]{1,0:T(8,128)S(1)}, u32[]{:S(2)}, u32[]{:S(2)}) %collective-permute-start.17) | collective-permute-done | bytes 8224 | tf_op jit(solution)/shard_map/ppermute | solution.py:320
  128.9 1.9 %collective-permute-done.16 = f32[16,128]{1,0:T(8,128)S(1)} collective-permute-done((f32[16,128]{1,0:T(8,128)S(1)}, f32[16,128]{1,0:T(8,128)S(1)}, u32[]{:S(2)}, u32[]{:S(2)}) %collective-permute-start.16) | collective-permute-done | bytes 8224 | tf_op jit(solution)/shard_map/ppermute | solution.py:320
  130.8 0.7 collective-permute-start.21
  131.5 1.7 %collective-permute-start.20 = (f32[16,128]{1,0:T(8,128)S(1)}, f32[16,128]{1,0:T(8,128)S(1)}, u32[]{:S(2)}, u32[]{:S(2)}) collective-permute-start(f32[16,128]{1,0:T(8,128)S(1)} %add_add_fusion.1), channel_id=1, source_target_pairs={{0,64},{1,65},{2,66},{3,67},{4,68},{5,69},{6,70},{7,71},{8,72},{9,... | collective-permute-start | bytes 24584 | tf_op jit(solution)/shard_map/ppermute | solution.py:320
  133.2 1.3 collective-permute-start.19
  134.6 0.0 collective-permute-done.21
  134.6 2.1 %collective-permute-done.20 = f32[16,128]{1,0:T(8,128)S(1)} collective-permute-done((f32[16,128]{1,0:T(8,128)S(1)}, f32[16,128]{1,0:T(8,128)S(1)}, u32[]{:S(2)}, u32[]{:S(2)}) %collective-permute-start.20) | collective-permute-done | bytes 8224 | tf_op jit(solution)/shard_map/ppermute | solution.py:320
  136.7 1.4 collective-permute-done.19
  138.1 13.6 %shard_map.52 = (f32[4096,128]{1,0:T(8,128)}, f32[4096,128]{1,0:T(8,128)}) custom-call(s32[3]{0:T(128)S(1)} %pad_add_fusion.info, f32[16,128]{1,0:T(8,128)S(1)} %add_add_fusion.mom_in, bf16[16,16,240,128]{3,2,1,0:T(8,128)(2,1)S(1)} %get-tuple-element.16.panel, f32[16,16,16,128]{3,2,1,0:T(8,128)S(1)} %get-tuple-element.17.iterate), custom_call_target="tpu_custom_call" | custom-call | tf_op jit(solution)/shard_map/pallas_call | solution.py:293
  (8 shorter events, 0.0 us)
Async XLA Ops:
  4.1 4.8 %collective-permute-start.1 = (f32[17,8,16,128]{3,2,1,0:T(8,128)}, f32[17,8,16,128]{3,2,1,0:T(8,128)S(1)}, u32[]{:S(2)}, u32[]{:S(2)}) collective-permute-start(f32[17,8,16,128]{3,2,1,0:T(8,128)} %get-tuple-element.20), channel_id=1, source_target_pairs={{1,0},{2,1},{3,2},{4,3},{5,4},{6,5},{7,6},{8,7},{9,8},{10,9},{11,1... | collective-permute-start | bytes 3342344 | tf_op jit(solution)/shard_map/ppermute | solution.py:334
  5.4 5.4 %collective-permute-start = (f32[17,8,16,128]{3,2,1,0:T(8,128)S(1)}, f32[17,8,16,128]{3,2,1,0:T(8,128)S(1)}, u32[]{:S(2)}, u32[]{:S(2)}) collective-permute-start(f32[17,8,16,128]{3,2,1,0:T(8,128)S(1)} %get-tuple-element.21), channel_id=1, source_target_pairs={{0,1},{1,2},{2,3},{3,4},{4,5},{5,6},{6,7},{7,8},{8,9},{9,10},{10,1... | collective-permute-start | bytes 3342344 | tf_op jit(solution)/shard_map/ppermute | solution.py:333
  10.8 1.0 copy-start.1
  11.8 1.6 %copy-start = (f32[16,16,16,128]{3,2,1,0:T(8,128)S(1)}, f32[16,16,16,128]{3,2,1,0:T(8,128)}, u32[]{:S(2)}) copy-start(f32[16,16,16,128]{3,2,1,0:T(8,128)} %param.3) | copy-start | bytes 6291460
  13.4 1.2 copy-start.2
  14.6 0.9 copy-start.3
  41.1 12.1 %collective-permute-start.2 = (f32[16,128]{1,0:T(8,128)S(1)}, f32[16,128]{1,0:T(8,128)S(1)}, u32[]{:S(2)}, u32[]{:S(2)}) collective-permute-start(f32[16,128]{1,0:T(8,128)S(1)} %get-tuple-element.11), channel_id=1, source_target_pairs={{0,1},{1,0},{2,3},{3,2},{4,5},{5,4},{6,7},{7,6},{8,9},{9,8},{10,11... | collective-permute-start | bytes 24584 | tf_op jit(solution)/shard_map/ppermute | solution.py:320
  53.2 5.3 %collective-permute-start.5 = (f32[16,128]{1,0:T(8,128)S(1)}, f32[16,128]{1,0:T(8,128)S(1)}, u32[]{:S(2)}, u32[]{:S(2)}) collective-permute-start(f32[16,128]{1,0:T(8,128)S(1)} %add.76), channel_id=1, source_target_pairs={{0,6},{1,7},{2,0},{3,1},{4,2},{5,3},{6,4},{7,5},{8,14},{9,15},{10,... | collective-permute-start | bytes 24584 | tf_op jit(solution)/shard_map/ppermute | solution.py:320
  57.1 5.2 %collective-permute-start.4 = (f32[16,128]{1,0:T(8,128)S(1)}, f32[16,128]{1,0:T(8,128)S(1)}, u32[]{:S(2)}, u32[]{:S(2)}) collective-permute-start(f32[16,128]{1,0:T(8,128)S(1)} %add.76), channel_id=1, source_target_pairs={{0,4},{1,5},{2,6},{3,7},{4,0},{5,1},{6,2},{7,3},{8,12},{9,13},{10,... | collective-permute-start | bytes 24584 | tf_op jit(solution)/shard_map/ppermute | solution.py:320
  57.1 5.2 %collective-permute-start.3 = (f32[16,128]{1,0:T(8,128)S(1)}, f32[16,128]{1,0:T(8,128)S(1)}, u32[]{:S(2)}, u32[]{:S(2)}) collective-permute-start(f32[16,128]{1,0:T(8,128)S(1)} %add.76), channel_id=1, source_target_pairs={{0,2},{1,3},{2,4},{3,5},{4,6},{5,7},{6,0},{7,1},{8,10},{9,11},{10,... | collective-permute-start | bytes 24584 | tf_op jit(solution)/shard_map/ppermute | solution.py:320
  62.3 7.7 %collective-permute-start.8 = (f32[16,128]{1,0:T(8,128)S(1)}, f32[16,128]{1,0:T(8,128)S(1)}, u32[]{:S(2)}, u32[]{:S(2)}) collective-permute-start(f32[16,128]{1,0:T(8,128)S(1)} %add_add_fusion.5), channel_id=1, source_target_pairs={{0,24},{1,25},{2,26},{3,27},{4,28},{5,29},{6,30},{7,31},{8,0},{9,1... | collective-permute-start | bytes 24584 | tf_op jit(solution)/shard_map/ppermute | solution.py:320
  68.6 5.2 %collective-permute-start.7 = (f32[16,128]{1,0:T(8,128)S(1)}, f32[16,128]{1,0:T(8,128)S(1)}, u32[]{:S(2)}, u32[]{:S(2)}) collective-permute-start(f32[16,128]{1,0:T(8,128)S(1)} %add_add_fusion.5), channel_id=1, source_target_pairs={{0,16},{1,17},{2,18},{3,19},{4,20},{5,21},{6,22},{7,23},{8,24},{9,... | collective-permute-start | bytes 24584 | tf_op jit(solution)/shard_map/ppermute | solution.py:320
  68.6 5.2 %collective-permute-start.6 = (f32[16,128]{1,0:T(8,128)S(1)}, f32[16,128]{1,0:T(8,128)S(1)}, u32[]{:S(2)}, u32[]{:S(2)}) collective-permute-start(f32[16,128]{1,0:T(8,128)S(1)} %add_add_fusion.5), channel_id=1, source_target_pairs={{0,8},{1,9},{2,10},{3,11},{4,12},{5,13},{6,14},{7,15},{8,16},{9,17... | collective-permute-start | bytes 24584 | tf_op jit(solution)/shard_map/ppermute | solution.py:320
  73.8 7.1 %collective-permute-start.11 = (f32[16,128]{1,0:T(8,128)S(1)}, f32[16,128]{1,0:T(8,128)S(1)}, u32[]{:S(2)}, u32[]{:S(2)}) collective-permute-start(f32[16,128]{1,0:T(8,128)S(1)} %add_add_fusion.4), channel_id=1, source_target_pairs={{0,96},{1,97},{2,98},{3,99},{4,100},{5,101},{6,102},{7,103},{8,104... | collective-permute-start | bytes 24584 | tf_op jit(solution)/shard_map/ppermute | solution.py:320
  79.5 5.2 %collective-permute-start.10 = (f32[16,128]{1,0:T(8,128)S(1)}, f32[16,128]{1,0:T(8,128)S(1)}, u32[]{:S(2)}, u32[]{:S(2)}) collective-permute-start(f32[16,128]{1,0:T(8,128)S(1)} %add_add_fusion.4), channel_id=1, source_target_pairs={{0,64},{1,65},{2,66},{3,67},{4,68},{5,69},{6,70},{7,71},{8,72},{9,... | collective-permute-start | bytes 24584 | tf_op jit(solution)/shard_map/ppermute | solution.py:320
  79.5 5.2 %collective-permute-start.9 = (f32[16,128]{1,0:T(8,128)S(1)}, f32[16,128]{1,0:T(8,128)S(1)}, u32[]{:S(2)}, u32[]{:S(2)}) collective-permute-start(f32[16,128]{1,0:T(8,128)S(1)} %add_add_fusion.4), channel_id=1, source_target_pairs={{0,32},{1,33},{2,34},{3,35},{4,36},{5,37},{6,38},{7,39},{8,40},{9,... | collective-permute-start | bytes 24584 | tf_op jit(solution)/shard_map/ppermute | solution.py:320
  114.6 1.2 collective-permute-start.12
  115.7 3.7 %collective-permute-start.15 = (f32[16,128]{1,0:T(8,128)S(1)}, f32[16,128]{1,0:T(8,128)S(1)}, u32[]{:S(2)}, u32[]{:S(2)}) collective-permute-start(f32[16,128]{1,0:T(8,128)S(1)} %add.86), channel_id=1, source_target_pairs={{0,6},{1,7},{2,0},{3,1},{4,2},{5,3},{6,4},{7,5},{8,14},{9,15},{10,... | collective-permute-start | bytes 24584 | tf_op jit(solution)/shard_map/ppermute | solution.py:320
  117.4 5.2 %collective-permute-start.14 = (f32[16,128]{1,0:T(8,128)S(1)}, f32[16,128]{1,0:T(8,128)S(1)}, u32[]{:S(2)}, u32[]{:S(2)}) collective-permute-start(f32[16,128]{1,0:T(8,128)S(1)} %add.86), channel_id=1, source_target_pairs={{0,4},{1,5},{2,6},{3,7},{4,0},{5,1},{6,2},{7,3},{8,12},{9,13},{10,... | collective-permute-start | bytes 24584 | tf_op jit(solution)/shard_map/ppermute | solution.py:320
  117.7 4.9 %collective-permute-start.13 = (f32[16,128]{1,0:T(8,128)S(1)}, f32[16,128]{1,0:T(8,128)S(1)}, u32[]{:S(2)}, u32[]{:S(2)}) collective-permute-start(f32[16,128]{1,0:T(8,128)S(1)} %add.86), channel_id=1, source_target_pairs={{0,2},{1,3},{2,4},{3,5},{4,6},{5,7},{6,0},{7,1},{8,10},{9,11},{10,... | collective-permute-start | bytes 24584 | tf_op jit(solution)/shard_map/ppermute | solution.py:320
  122.7 3.7 %collective-permute-start.18 = (f32[16,128]{1,0:T(8,128)S(1)}, f32[16,128]{1,0:T(8,128)S(1)}, u32[]{:S(2)}, u32[]{:S(2)}) collective-permute-start(f32[16,128]{1,0:T(8,128)S(1)} %add_add_fusion.2), channel_id=1, source_target_pairs={{0,24},{1,25},{2,26},{3,27},{4,28},{5,29},{6,30},{7,31},{8,0},{9,1... | collective-permute-start | bytes 24584 | tf_op jit(solution)/shard_map/ppermute | solution.py:320
  123.8 5.2 %collective-permute-start.17 = (f32[16,128]{1,0:T(8,128)S(1)}, f32[16,128]{1,0:T(8,128)S(1)}, u32[]{:S(2)}, u32[]{:S(2)}) collective-permute-start(f32[16,128]{1,0:T(8,128)S(1)} %add_add_fusion.2), channel_id=1, source_target_pairs={{0,16},{1,17},{2,18},{3,19},{4,20},{5,21},{6,22},{7,23},{8,24},{9,... | collective-permute-start | bytes 24584 | tf_op jit(solution)/shard_map/ppermute | solution.py:320
  125.9 4.9 %collective-permute-start.16 = (f32[16,128]{1,0:T(8,128)S(1)}, f32[16,128]{1,0:T(8,128)S(1)}, u32[]{:S(2)}, u32[]{:S(2)}) collective-permute-start(f32[16,128]{1,0:T(8,128)S(1)} %add_add_fusion.2), channel_id=1, source_target_pairs={{0,8},{1,9},{2,10},{3,11},{4,12},{5,13},{6,14},{7,15},{8,16},{9,17... | collective-permute-start | bytes 24584 | tf_op jit(solution)/shard_map/ppermute | solution.py:320
  130.8 3.8 %collective-permute-start.21 = (f32[16,128]{1,0:T(8,128)S(1)}, f32[16,128]{1,0:T(8,128)S(1)}, u32[]{:S(2)}, u32[]{:S(2)}) collective-permute-start(f32[16,128]{1,0:T(8,128)S(1)} %add_add_fusion.1), channel_id=1, source_target_pairs={{0,96},{1,97},{2,98},{3,99},{4,100},{5,101},{6,102},{7,103},{8,104... | collective-permute-start | bytes 24584 | tf_op jit(solution)/shard_map/ppermute | solution.py:320
  131.5 5.2 %collective-permute-start.20 = (f32[16,128]{1,0:T(8,128)S(1)}, f32[16,128]{1,0:T(8,128)S(1)}, u32[]{:S(2)}, u32[]{:S(2)}) collective-permute-start(f32[16,128]{1,0:T(8,128)S(1)} %add_add_fusion.1), channel_id=1, source_target_pairs={{0,64},{1,65},{2,66},{3,67},{4,68},{5,69},{6,70},{7,71},{8,72},{9,... | collective-permute-start | bytes 24584 | tf_op jit(solution)/shard_map/ppermute | solution.py:320
  133.2 4.9 %collective-permute-start.19 = (f32[16,128]{1,0:T(8,128)S(1)}, f32[16,128]{1,0:T(8,128)S(1)}, u32[]{:S(2)}, u32[]{:S(2)}) collective-permute-start(f32[16,128]{1,0:T(8,128)S(1)} %add_add_fusion.1), channel_id=1, source_target_pairs={{0,32},{1,33},{2,34},{3,35},{4,36},{5,37},{6,38},{7,39},{8,40},{9,... | collective-permute-start | bytes 24584 | tf_op jit(solution)/shard_map/ppermute | solution.py:320

commit v2 on v0

v2 whole, which is shorter than its diff:
```python
import jax
import jax.numpy as jnp
from jax import lax
from jax.experimental import pallas as pl
from jax.experimental.pallas import tpu as pltpu
from jax.sharding import PartitionSpec as P

NRHS = 16
SSTEP = 4
SHIFT = 8.5
SCALE = 7.5
CX = 16
NY = 16
NZ = 128
KB = SSTEP + 1
PIECE = KB * NRHS
MID = CX - 2 * SSTEP
MIDDLE = CX + 2 * SSTEP
AXES = ("grp", "dom")
F32 = jnp.float32
BF16 = jnp.bfloat16
FIELD = (NY, NRHS, NZ)
PANEL = (NY, 3 * PIECE, NZ)


def over(start, stop, body, group=4):
    whole = (stop - start) // group

    def step(i, carry):
        for k in range(group):
            body(start + i * group + k)
        return carry

    if whole:
        lax.fori_loop(0, whole, step, 0)
    for plane in range(start + whole * group, stop):
        body(plane)


def pieces(value):
    hi = value.astype(BF16)
    rest = value - hi.astype(F32)
    mid = rest.astype(BF16)
    lo = (rest - mid.astype(F32)).astype(BF16)
    return hi, mid, lo


def store_pieces(panel, plane, y, power, value):
    for i, part in enumerate(pieces(value)):
        panel[plane, y, pl.ds(i * PIECE + power * NRHS, NRHS), :] = part


def split_plane(panel, at, power, field, plane):
    for y in range(NY):
        store_pieces(panel, at, y, power, field[plane, y])


def coef_of(diag):
    return (diag + (6.0 - SHIFT)) * (1.0 / SCALE)


def plane_step(below, centre_at, above, coef, weight, emit):
    lane = lax.broadcasted_iota(jnp.int32, (NRHS, NZ), 1)
    first = lane == 0
    last = lane == NZ - 1
    zero = jnp.zeros((NRHS, NZ), F32)
    src, plane = centre_at
    before = zero
    centre = src[plane, 0]
    for y in range(NY):
        after = src[plane, y + 1] if y + 1 < NY else zero
        beside = below[0][below[1], y] + above[0][above[1], y] + (before + after)
        beside = beside + jnp.where(first, 0.0, pltpu.roll(centre, 1, 1))
        beside = beside + jnp.where(last, 0.0, pltpu.roll(centre, NZ - 1, 1))
        emit(y, coef(y) * centre - weight * beside)
        before, centre = centre, after


def moments(panel, planes):
    def plane_sum(plane, acc):
        for y in range(0, NY, 2):

            def rows(at, size):
                return jnp.concatenate(
                    [panel[plane, y, pl.ds(at, size), :], panel[plane, y + 1, pl.ds(at, size), :]], 1
                )

            ends = [rows(at, NRHS) for at in (0, PIECE, SSTEP * NRHS, PIECE + SSTEP * NRHS)]
            acc = acc + lax.dot_general(
                rows(0, 2 * PIECE),
                jnp.concatenate(ends, 0),
                (((1,), (1,)), ((), ())),
                preferred_element_type=F32,
            )
        return acc

    def body(i, acc):
        return plane_sum(2 * i + 1, plane_sum(2 * i, acc))

    acc = lax.fori_loop(0, planes // 2, body, jnp.zeros((2 * PIECE, 4 * NRHS), F32))
    acc = acc[:PIECE] + acc[PIECE:]
    low = acc[:, :NRHS] + acc[:, NRHS : 2 * NRHS]
    high = acc[:, 2 * NRHS : 3 * NRHS] + acc[:, 3 * NRHS :]
    blocks = [low[j * NRHS : (j + 1) * NRHS] for j in range(KB)]
    blocks += [high[j * NRHS : (j + 1) * NRHS] for j in range(1, SSTEP)]
    return jnp.concatenate(blocks, 1)


def solve(mom):
    size = SSTEP * NRHS
    step = 4
    shifted = jnp.concatenate([mom[:, NRHS:], mom[:, :NRHS]], 1)
    band = SHIFT * mom + SCALE * shifted
    blocks = [band[:, i * NRHS : i * NRHS + size] for i in range(SSTEP)]
    work = jnp.concatenate(blocks + [mom[:, :size]], 0)
    lane = lax.broadcasted_iota(jnp.int32, (1, size), 1)
    sub = lax.broadcasted_iota(jnp.int32, (step, 1), 0)
    for j in range(0, size, step):
        off = j % 8
        if off == 0 and j:
            work = work[8:]
        inside = (lane >= j) & (lane < j + step)
        rows = work[off : off + step]
        cols = [jnp.broadcast_to(rows[:, j + t : j + t + 1], (step, size)) for t in range(step)]
        rows = jnp.where(inside, (lane - j == sub).astype(F32), rows)
        for t in range(step):
            inv = 1.0 / cols[t][t : t + 1]
            factor = jnp.where(sub == t, 0.0, cols[t])

            def eliminate(m):
                row = m[t : t + 1] * inv
                return jnp.where(sub == t, row, m - factor * row)

            rows = eliminate(rows)
            cols = [eliminate(c) if u > t else c for u, c in enumerate(cols)]
        acc = work[:, j : j + 1] * rows[0:1]
        for t in range(1, step):
            acc = acc + work[:, j + t : j + t + 1] * rows[t : t + 1]
        work = jnp.where(inside, acc, work - acc)
    return work[8:]


def coef_rows(coef_t):
    pad = jnp.zeros((NRHS, NRHS), F32)
    eye = (
        lax.broadcasted_iota(jnp.int32, (NRHS, PIECE), 0)
        == lax.broadcasted_iota(jnp.int32, (NRHS, PIECE), 1)
    ).astype(F32)
    same = jnp.concatenate([coef_t, pad], 1)
    up = jnp.concatenate([pad, coef_t], 1)
    left = eye - (SHIFT * same + SCALE * up)
    l_hi, l_mid, l_lo = pieces(left)
    c_hi, c_mid, _ = pieces(same)
    none = jnp.zeros((NRHS, PIECE), BF16)
    rows = [
        [l_hi, l_hi, l_hi],
        [l_mid, l_mid, none],
        [l_lo, none, none],
        [c_hi, c_hi, none],
        [c_mid, none, none],
    ]
    return jnp.concatenate([jnp.concatenate(r, 1) for r in rows], 0)


def combine(coefs, panel, plane, emit):
    for y in range(0, NY, 2):
        block = jnp.concatenate([panel[plane, y], panel[plane, y + 1]], 1)
        out = jnp.dot(coefs, block, preferred_element_type=F32)
        left = out[:NRHS] + out[NRHS : 2 * NRHS] + out[2 * NRHS : 3 * NRHS]
        step = out[3 * NRHS : 4 * NRHS] + out[4 * NRHS :]
        for k in range(2):
            emit(y + k, left[:, k * NZ : (k + 1) * NZ], step[:, k * NZ : (k + 1) * NZ])


def pack_kernel(info, right, diag, near_top, near_first, far_top, far_first, sems):
    count = info[0]
    copies = []
    places = ((near_top, count - SSTEP), (near_first, 0), (far_top, count - 2 * SSTEP), (far_first, SSTEP))
    for i, (out, at) in enumerate(places):
        copies.append(
            pltpu.make_async_copy(
                right.at[:, pl.ds(at, SSTEP)], out.at[pl.ds(0, NRHS)], sems.at[2 * i]
            )
        )
        copies.append(
            pltpu.make_async_copy(diag.at[pl.ds(at, SSTEP)], out.at[NRHS], sems.at[2 * i + 1])
        )
    for copy in copies:
        copy.start()
    for copy in copies:
        copy.wait()


def inner_kernel(info, right, diag, panel, mom, field_0, field_1, field_2, field_3):
    count = info[0]
    rows = NY * CX
    fields = (field_0, field_1, field_2, field_3)

    def load(p):
        for y in range(NY):
            field_0[p, y] = right[pl.Slice(p * NY + y, NRHS, rows), :]

    over(0, CX, load)

    def keep_of(p):
        return (p < count - SSTEP).astype(F32)

    def split(p):
        keep = keep_of(p + SSTEP)
        for y in range(NY):
            store_pieces(panel, p, y, 0, field_0[p + SSTEP, y] * keep)

    over(0, MID, split)
    weight = 1.0 / SCALE
    for power in range(1, SSTEP + 1):
        src = fields[power - 1]

        def apply(p, inner):
            keep = keep_of(p)

            def emit(y, value):
                if power < SSTEP:
                    fields[power][p, y] = value
                if inner:
                    store_pieces(panel, p - SSTEP, y, power, value * keep)

            plane_step(
                (src, p - 1), (src, p), (src, p + 1),
                lambda y: coef_of(diag[p, pl.ds(y, 1), :]), weight, emit,
            )

        for p in range(power, SSTEP):
            apply(p, False)
            apply(CX - 1 - p, False)
        over(SSTEP, CX - SSTEP, lambda p: apply(p, True))
    mom[...] = moments(panel, MID)


def halo_diag(halo, i, y):
    return halo[pl.ds(NRHS * SSTEP * NY + i * NY + y, 1), :]


def edge_kernel(
    info, lower, upper, diag, mom_in, field_0, field_1, field_2, field_3, panel, mom, side_l, side_u
):
    count = info[0]
    fields = (field_0, field_1, field_2, field_3)
    for i in range(SSTEP):
        for y in range(NY):
            side_l[0, i, y] = lower[pl.Slice(i * NY + y, NRHS, SSTEP * NY), :]
            side_u[0, i, y] = upper[pl.Slice((SSTEP - 1 - i) * NY + y, NRHS, SSTEP * NY), :]
    for top in (False, True):
        side, halo = (side_u, upper) if top else (side_l, lower)
        outside = jnp.where(info[2 if top else 1] > 0, 1.0 / SCALE, 0.0).astype(F32)

        def own(q):
            return count - 1 - q if top else q

        for power in range(SSTEP + 1):

            def source(level, q):
                if q <= level - 1:
                    return side.at[level], q - (level - SSTEP)
                return fields[level], own(q)

            for q in range(power, SSTEP):
                split_plane(panel, q + (SSTEP if top else 0), power, fields[power], own(q))
            if power == 0:
                continue
            for q in range(power - SSTEP, power):

                def coef(y):
                    if q >= 0:
                        return coef_of(diag[own(q), pl.ds(y, 1), :])
                    return coef_of(halo_diag(halo, -1 - q if top else q + SSTEP, y))

                def emit(y, value):
                    if power < SSTEP:
                        side[power, q - (power - SSTEP), y] = value
                    if q >= 0:
                        store_pieces(panel, q + (SSTEP if top else 0), y, power, value)

                plane_step(
                    source(power - 1, q - 1), source(power - 1, q), source(power - 1, q + 1),
                    coef, outside if q < 0 else 1.0 / SCALE, emit,
                )
    mom[...] = mom_in[...] + moments(panel, 2 * SSTEP)


def ghost_kernel(
    info, lower, upper, far_lower, far_upper, diag, side_l, side_u, panel, coef, far_a, far_b
):
    count = info[0]
    for i in range(MIDDLE - CX):
        coef[CX + i] = jnp.zeros((NY, NZ), F32)
    for i in range(CX):
        coef[SSTEP + i] = coef_of(diag[i])
    base = NRHS * SSTEP * NY
    for i in range(SSTEP):
        coef[i] = coef_of(lower[pl.ds(base + i * NY, NY), :])
        coef[SSTEP + count + i] = coef_of(upper[pl.ds(base + i * NY, NY), :])
    for top in (False, True):
        side, near, far = (side_u, upper, far_upper) if top else (side_l, lower, far_lower)
        weight = jnp.where(info[2 if top else 1] > 0, 1.0 / SCALE, 0.0).astype(F32)
        shift = SSTEP if top else 0
        for i in range(SSTEP):
            for y in range(NY):
                j = SSTEP - 1 - i if top else i
                far_a[i, y] = far[pl.Slice(j * NY + y, NRHS, SSTEP * NY), :]
        buffers = (far_a, far_b)
        for power in range(SSTEP + 1):
            for q in range(power - SSTEP, 0):
                split_plane(panel, q + SSTEP + shift, power, side.at[power], q - (power - SSTEP))
            if power == 0:
                continue
            src, dst = buffers[(power - 1) % 2], buffers[power % 2]

            def source(q):
                if q <= power - 6:
                    return src, q - (power - 9)
                return side.at[power - 1], q - (power - 5)

            for q in range(power - 8, power - 4):

                def diag_row(y):
                    if q >= -SSTEP:
                        return coef_of(halo_diag(near, -1 - q if top else q + SSTEP, y))
                    return coef_of(halo_diag(far, -5 - q if top else q + 8, y))

                def emit(y, value):
                    if power < SSTEP:
                        dst[q - (power - 8), y] = value
                    if q >= -SSTEP:
                        store_pieces(panel, q + SSTEP + shift, y, power, value)

                plane_step(source(q - 1), source(q), source(q + 1), diag_row, weight, emit)


def middle_kernel(
    info, mom_in, coef, inner, edge, ghost, panel_a, panel_b, mom, iterate, field_a, field_b
):
    count = info[0]
    coefs = coef_rows(solve(mom_in[...]))

    def weight_of(plane):
        inside = (
            ((plane >= SSTEP) | (info[1] > 0))
            & ((plane < SSTEP + count) | (info[2] > 0))
            & (plane < 2 * SSTEP + count)
        )
        return jnp.where(inside, 1.0 / SCALE, 0.0).astype(F32)

    def update(store, plane, at, own):
        def emit(y, left, step):
            field_a[at, y] = left
            if own:
                iterate[at - SSTEP, y] = step

        combine(coefs, store, plane, emit)

    for i in range(MIDDLE - CX):
        field_a[CX + i] = jnp.zeros(FIELD, F32)
    for i in range(SSTEP):
        iterate[CX - SSTEP + i] = jnp.zeros(FIELD, F32)
    over(0, SSTEP, lambda p: update(ghost, p, p, False))
    over(0, SSTEP, lambda p: update(edge, p, p + SSTEP, True))
    over(0, MID, lambda p: update(inner, p, p + 2 * SSTEP, True))
    over(0, SSTEP, lambda p: update(edge, 2 * SSTEP - 1 - p, count + p, True))
    over(0, SSTEP, lambda p: update(ghost, 2 * SSTEP - 1 - p, count + SSTEP + p, False))

    def keep_of(p):
        return (p < SSTEP + count).astype(F32)

    halves = ((panel_a, SSTEP), (panel_b, SSTEP + MID))
    for panel, base in halves:

        def split(p):
            keep = keep_of(p)
            for y in range(NY):
                store_pieces(panel, p - base, y, 0, field_a[p, y] * keep)

        over(base, base + MID, split)
    fields = (field_a, field_b)
    for power in range(1, SSTEP + 1):
        src, dst = fields[(power - 1) % 2], fields[power % 2]

        def apply(p, panel, base):
            keep = keep_of(p)

            def emit(y, value):
                if power < SSTEP:
                    dst[p, y] = value
                if panel is not None:
                    store_pieces(panel, p - base, y, power, value * keep)

            plane_step(
                (src, p - 1), (src, p), (src, p + 1),
                lambda y: coef[p, pl.ds(y, 1), :], weight_of(p), emit,
            )

        for p in range(power, SSTEP):
            apply(p, None, 0)
            apply(MIDDLE - 1 - p, None, 0)
        for panel, base in halves:
            over(base, base + MID, lambda p: apply(p, panel, base))
    mom[...] = moments(panel_a, MID) + moments(panel_b, MID)


def last_kernel(info, mom_in, panel_a, panel_b, iterate, solution_field, residual):
    count = info[0]
    rows = NY * CX
    coefs = coef_rows(solve(mom_in[...]))

    def update(panel, plane, p):
        keep = (p < count).astype(F32)

        def emit(y, left, step):
            at = pl.Slice(p * NY + y, NRHS, rows)
            residual[at, :] = left
            solution_field[at, :] = iterate[p, y] * keep + step

        combine(coefs, panel, plane, emit)

    over(0, MID, lambda p: update(panel_a, p, p))
    over(0, MID, lambda p: update(panel_b, p, p + MID))


SMEM_SPEC = pl.BlockSpec(memory_space=pltpu.SMEM)
VMEM_SPEC = pl.BlockSpec(memory_space=pltpu.VMEM)


def call(body, limit, operands, outs, scratch, kept_operands=(), cost=1, aliases={}):
    operands = [
        pltpu.with_memory_space_constraint(x, pltpu.VMEM) if i in kept_operands else x
        for i, x in enumerate(operands)
    ]
    return pl.pallas_call(
        body,
        out_shape=[pltpu.VMEM(s, d) if kept else jax.ShapeDtypeStruct(s, d) for s, d, kept in outs],
        in_specs=[SMEM_SPEC] + [VMEM_SPEC] * (len(operands) - 1),
        out_specs=[VMEM_SPEC] * len(outs),
        scratch_shapes=scratch,
        input_output_aliases=aliases,
        cost_estimate=pl.CostEstimate(
            flops=cost * 1_000_000_000, bytes_accessed=cost * 3_000_000, transcendentals=0
        ),
        compiler_params=pltpu.CompilerParams(vmem_limit_bytes=limit * 1024 * 1024),
    )(*operands)


def reduce_all(value, size, beside=None):
    if size == 128:
        rounds = [(1, 2), (2, 4), (8, 4), (32, 4)]
    else:
        rounds = [(1 << b, 2) for b in range(size.bit_length() - 1)]
    for place_in_order, (stride, width) in enumerate(rounds):
        total = value
        if beside is not None and place_in_order == 2:
            total, beside = lax.optimization_barrier((total, beside))
        for turn in range(1, width):
            route = []
            for i in range(size):
                place = i // stride % width
                route.append((i, i + ((place + turn) % width - place) * stride))
            total = total + lax.ppermute(value, AXES, route)
        value = total
    return value, beside


def local(right_side, diagonal, counts):
    count = counts[0]
    size = lax.axis_size(AXES)
    me = lax.axis_index(AXES)
    info = jnp.stack([count, me, size - 1 - me]).astype(jnp.int32)

    packed = ((NRHS + 1, SSTEP, NY, NZ), F32, True)
    near_top, near_first, far_top, far_first = pl.pallas_call(
        pack_kernel,
        out_shape=[pltpu.VMEM(packed[0], F32)] * 4,
        in_specs=[SMEM_SPEC] + [pl.BlockSpec(memory_space=pltpu.HBM)] * 2,
        out_specs=[VMEM_SPEC] * 4,
        scratch_shapes=[pltpu.SemaphoreType.DMA((8,))],
        compiler_params=pltpu.CompilerParams(vmem_limit_bytes=8 * 1024 * 1024),
    )(
        info,
        pltpu.with_memory_space_constraint(right_side, pltpu.HBM),
        pltpu.with_memory_space_constraint(diagonal, pltpu.HBM),
    )
    upward = [(i, i + 1) for i in range(size - 1)]
    downward = [(i + 1, i) for i in range(size - 1)]
    halo = ((NRHS + 1) * SSTEP * NY, NZ)
    lower = lax.ppermute(near_top, AXES, upward)
    upper = lax.ppermute(near_first, AXES, downward)
    inner, mom_inner, f0, f1, f2, f3 = call(
        inner_kernel,
        12,
        (info, right_side.reshape(NRHS * CX * NY, NZ), diagonal),
        [((MID,) + PANEL, BF16, True), ((NRHS, NZ), F32, False)]
        + [((CX,) + FIELD, F32, True)] * SSTEP,
        [],
        cost=4,
    )
    lower, upper = lower.reshape(halo), upper.reshape(halo)
    edge, mom, side_l, side_u = call(
        edge_kernel,
        8,
        (info, lower, upper, diagonal, mom_inner, f0, f1, f2, f3),
        [
            ((2 * SSTEP,) + PANEL, BF16, True),
            ((NRHS, NZ), F32, False),
            ((SSTEP, SSTEP) + FIELD, F32, True),
            ((SSTEP, SSTEP) + FIELD, F32, True),
        ],
        [],
        (5, 6, 7, 8),
        cost=4,
    )
    mom, far_top, far_first = lax.optimization_barrier((mom, far_top, far_first))
    far_lower = lax.ppermute(far_top, AXES, upward).reshape(halo)
    far_upper = lax.ppermute(far_first, AXES, downward).reshape(halo)
    ghost, coef = call(
        ghost_kernel,
        8,
        (info, lower, upper, far_lower, far_upper, diagonal, side_l, side_u),
        [((2 * SSTEP,) + PANEL, BF16, True), ((MIDDLE, NY, NZ), F32, True)],
        [pltpu.VMEM((SSTEP,) + FIELD, F32), pltpu.VMEM((SSTEP,) + FIELD, F32)],
        (6, 7),
        cost=3,
    )
    mom, coef = reduce_all(mom, size, coef)
    panel_a, panel_b, mom, iterate = call(
        middle_kernel,
        8,
        (info, mom, coef, inner, edge, ghost),
        [
            ((MID,) + PANEL, BF16, True),
            ((MID,) + PANEL, BF16, True),
            ((NRHS, NZ), F32, False),
            ((CX,) + FIELD, F32, True),
        ],
        [pltpu.VMEM((MIDDLE,) + FIELD, F32), pltpu.VMEM((MIDDLE,) + FIELD, F32)],
        (2, 3, 4, 5),
        cost=10,
        aliases={3: 0, 4: 1},
    )
    mom, _ = reduce_all(mom, size)
    out = (NRHS * CX * NY, NZ)
    solution_field, residual = call(
        last_kernel,
        8,
        (info, mom, panel_a, panel_b, iterate),
        [(out, F32, False), (out, F32, False)],
        [],
        (2, 3, 4),
        cost=4,
    )
    return (solution_field.reshape(right_side.shape), residual.reshape(right_side.shape))


def solution(mesh):
    in_specs = (
        P(None, AXES, None, None),
        P(AXES, None, None),
        P(AXES),
    )
    out_specs = (P(None, AXES, None, None), P(None, AXES, None, None))
    return jax.shard_map(local, mesh=mesh, in_specs=in_specs, out_specs=out_specs, check_vma=False)
```

time: 486 us -> 113 us (0.23); the launches traced: 480 us -> 113 us
  blocking collectives: 175 us -> 0 us
  local copies, waits for them, and re-layouts: 112 us -> 0.01 us
  matrix products: 79.1 us -> 0 us
  other arithmetic: 54 us -> 0.11 us
  Pallas kernels: 0 us -> 47.6 us
  waiting for transfers between devices: 11.8 us -> 22.5 us
    psum x2 -> x0, blocking collectives: 175 us -> none  [local(): gram = lax.psum(local_gram, ('grp', 'dom'))]
    dot_general x10 -> x0, matrix products: 78.2 us -> none  [the longest x2 26.5 us: local(): jnp.dot(step.T, panel, precision=lax.Precision.HIGHEST)]
    pallas_call x0 -> x6, Pallas kernels: none -> 47.6 us  [the longest x5 45.4 us: call(): pl.pallas_call(body, out_shape=[pltpu.VMEM(s, d) if kept else jax.ShapeDt...]
    unnamed x46 -> x4, local copies, waits for them, and re-layouts: 35 us -> 0.01 us
    another operation x4 -> x0, local copies, waits for them, and re-layouts: 34.1 us -> none  [local(): panel = jnp.stack(basis).reshape((SSTEP + 1) * NRHS, -1)]
    another operation x14 -> x1, other arithmetic: 31 us -> 0.08 us  [local(): info = jnp.stack([count, me, size - 1 - me]).astype(jnp.int32)]
    reshape x2 -> x0, local copies, waits for them, and re-layouts: 23.2 us -> none  [local(): panel = jnp.stack(basis).reshape((SSTEP + 1) * NRHS, -1)]
    slice x10 -> x0, local copies, waits for them, and re-layouts: 18.9 us -> none  [the longest x2 18.8 us: local(): panel[:SSTEP * NRHS]]
  transfers between devices with their start and end apart: 16 -> 24, of which waited for: 6 -> 14; matrix products, arithmetic and copies ran while one was open for 11% -> 0% of each run, Pallas kernels for 0% -> 11%
where the time goes in v2:
time: 113 us
  Pallas kernels  47.6 us (42%)
  starting transfers between devices  41.2 us (36%)
  waiting for transfers between devices  22.5 us (20%)
  between operations  1.59 us (1%)
    pallas_call x5, Pallas kernels, call(): pl.pallas_call(body, out_shape=[pltpu.VMEM(s, d) if kept else jax.ShapeDt...  45.4 us
    ppermute x20, starting transfers between devices, reduce_all(): total = total + lax.ppermute(value, AXES, route)  31.6 us
    ppermute x20, waiting for transfers between devices, reduce_all(): total = total + lax.ppermute(value, AXES, route)  22.5 us
    ppermute x1, starting transfers between devices, local(): far_lower = lax.ppermute(far_top, AXES, upward).reshape(halo)  5.69 us
  transfers between devices with their start and end apart: 24, of which 14 were waited for; matrix products, arithmetic and copies ran while one was open for 0% of the time, Pallas kernels for 11%

profile of v2, /device:TPU:0, one launch (start us, length us, event | category | flops | bytes accessed | tf_op | source)
XLA Modules:
  0.0 113.0 jit_solution(16614234868608113326)
XLA Ops:
  0.6 0.0 copy-start.1
  0.6 0.0 copy-start
  1.5 0.1 pad_add_fusion.info
  1.5 2.2 %shard_map.50 = (f32[17,4,16,128]{3,2,1,0:T(8,128)S(1)}, f32[17,4,16,128]{3,2,1,0:T(8,128)S(1)}, f32[17,4,16,128]{3,2,1,0:T(8,128)S(1)}, f32[17,4,16,128]{3,2,1,0:T(8,128)S(1)}) custom-call(s32[3]{0:T(128)S(1)} %pad_add_fusion.info, f32[16,16,16,128]{3,2,1,0:T(8,128)} %right.1, f32[16,16,128]{2,1,0:T(8,128)} %diag.7), custom_call_target="tpu_custom_call" | custom-call | tf_op jit(solution)/shard_map/pallas_call | solution.py:477
  3.7 1.3 %collective-permute-start = (f32[17,4,16,128]{3,2,1,0:T(8,128)S(1)}, f32[17,4,16,128]{3,2,1,0:T(8,128)S(1)}, u32[]{:S(2)}, u32[]{:S(2)}) collective-permute-start(f32[17,4,16,128]{3,2,1,0:T(8,128)S(1)} %get-tuple-element.29), channel_id=1, source_target_pairs={{0,1},{1,2},{2,3},{3,4},{4,5},{5,6},{6,7},{7,8},{8,9},{9,10},{10,1... | collective-permute-start | bytes 1671176 | tf_op jit(solution)/shard_map/ppermute | solution.py:492
  5.1 1.3 %collective-permute-start.1 = (f32[17,4,16,128]{3,2,1,0:T(8,128)S(1)}, f32[17,4,16,128]{3,2,1,0:T(8,128)S(1)}, u32[]{:S(2)}, u32[]{:S(2)}) collective-permute-start(f32[17,4,16,128]{3,2,1,0:T(8,128)S(1)} %get-tuple-element.30), channel_id=1, source_target_pairs={{1,0},{2,1},{3,2},{4,3},{5,4},{6,5},{7,6},{8,7},{9,8},{10,9},{11,1... | collective-permute-start | bytes 1671176 | tf_op jit(solution)/shard_map/ppermute | solution.py:493
  6.4 0.0 copy-done.1
  6.4 0.0 copy-done
  6.4 8.0 %shard_map.51 = (bf16[8,16,240,128]{3,2,1,0:T(8,128)(2,1)S(1)}, f32[16,128]{1,0:T(8,128)S(1)}, f32[16,16,16,128]{3,2,1,0:T(8,128)S(1)}, f32[16,16,16,128]{3,2,1,...) custom-call(s32[3]{0:T(128)S(1)} %pad_add_fusion.info, f32[4096,128]{1,0:T(8,128)S(1)} %bitcast.9, ...), custom_call_target="tpu_custom_call" | custom-call | flops 4000000000 | bytes 12000000 | tf_op jit(solution)/shard_map/pallas_call | solution.py:437
  14.4 0.0 collective-permute-done
  14.4 0.0 collective-permute-done.1
  14.4 5.9 %shard_map.52 = (bf16[8,16,240,128]{3,2,1,0:T(8,128)(2,1)S(1)}, f32[16,128]{1,0:T(8,128)S(1)}, f32[4,4,16,16,128]{4,3,2,1,0:T(8,128)S(1)}, f32[4,4,16,16,128]{4,3,2,1,0:T(8,128)S(1)}) custom-call(s32[3]{0:T(128)S(1)} %pad_add_fusion.info, f32[1088,128]{1,0:T(8,128)S(1)} %bitcast.10, f32[1088,128]{1,0:T(8,128)S(1)} %bitcast.12, f32[16,16,128]{2,1,0:T(8,128)S(1)} %copy-done.1, ...), custom_call_target="tpu_custom_call" | custom-call | flops 4000000000 | bytes 12000000 | tf_op jit(solution)/shard_map/pallas_call | solution.py:437
  20.3 5.7 %collective-permute-start.6 = (f32[17,4,16,128]{3,2,1,0:T(8,128)S(1)}, f32[17,4,16,128]{3,2,1,0:T(8,128)S(1)}, u32[]{:S(2)}, u32[]{:S(2)}) collective-permute-start(f32[17,4,16,128]{3,2,1,0:T(8,128)S(1)} %get-tuple-element.40), channel_id=1, source_target_pairs={{0,1},{1,2},{2,3},{3,4},{4,5},{5,6},{6,7},{7,8},{8,9},{9,10},{10,1... | collective-permute-start | bytes 1671176 | tf_op jit(solution)/shard_map/ppermute | solution.py:519
  26.0 1.3 %collective-permute-start.7 = (f32[17,4,16,128]{3,2,1,0:T(8,128)S(1)}, f32[17,4,16,128]{3,2,1,0:T(8,128)S(1)}, u32[]{:S(2)}, u32[]{:S(2)}) collective-permute-start(f32[17,4,16,128]{3,2,1,0:T(8,128)S(1)} %get-tuple-element.41), channel_id=1, source_target_pairs={{1,0},{2,1},{3,2},{4,3},{5,4},{6,5},{7,6},{8,7},{9,8},{10,9},{11,1... | collective-permute-start | bytes 1671176 | tf_op jit(solution)/shard_map/ppermute | solution.py:520
  27.3 1.6 %collective-permute-start.2 = (f32[16,128]{1,0:T(8,128)S(1)}, f32[16,128]{1,0:T(8,128)S(1)}, u32[]{:S(2)}, u32[]{:S(2)}) collective-permute-start(f32[16,128]{1,0:T(8,128)S(1)} %get-tuple-element.39), channel_id=1, source_target_pairs={{0,1},{1,0},{2,3},{3,2},{4,5},{5,4},{6,7},{7,6},{8,9},{9,8},{10,11... | collective-permute-start | bytes 24584 | tf_op jit(solution)/shard_map/ppermute | solution.py:465
  28.9 1.4 %collective-permute-done.2 = f32[16,128]{1,0:T(8,128)S(1)} collective-permute-done((f32[16,128]{1,0:T(8,128)S(1)}, f32[16,128]{1,0:T(8,128)S(1)}, u32[]{:S(2)}, u32[]{:S(2)}) %collective-permute-start.2) | collective-permute-done | bytes 8224 | tf_op jit(solution)/shard_map/ppermute | solution.py:465
  30.2 5.2 %collective-permute-start.5 = (f32[16,128]{1,0:T(8,128)S(1)}, f32[16,128]{1,0:T(8,128)S(1)}, u32[]{:S(2)}, u32[]{:S(2)}) collective-permute-start(f32[16,128]{1,0:T(8,128)S(1)} %add.64), channel_id=1, source_target_pairs={{0,6},{1,7},{2,0},{3,1},{4,2},{5,3},{6,4},{7,5},{8,14},{9,15},{10,... | collective-permute-start | bytes 24584 | tf_op jit(solution)/shard_map/ppermute | solution.py:465
  35.5 0.0 collective-permute-start.4
  35.5 0.9 collective-permute-start.3
  36.3 1.8 %collective-permute-done.5 = f32[16,128]{1,0:T(8,128)S(1)} collective-permute-done((f32[16,128]{1,0:T(8,128)S(1)}, f32[16,128]{1,0:T(8,128)S(1)}, u32[]{:S(2)}, u32[]{:S(2)}) %collective-permute-start.5) | collective-permute-done | bytes 8224 | tf_op jit(solution)/shard_map/ppermute | solution.py:465
  38.2 2.5 %collective-permute-done.4 = f32[16,128]{1,0:T(8,128)S(1)} collective-permute-done((f32[16,128]{1,0:T(8,128)S(1)}, f32[16,128]{1,0:T(8,128)S(1)}, u32[]{:S(2)}, u32[]{:S(2)}) %collective-permute-start.4) | collective-permute-done | bytes 8224 | tf_op jit(solution)/shard_map/ppermute | solution.py:465
  40.6 0.0 collective-permute-done.3
  40.6 4.5 %collective-permute-start.10 = (f32[16,128]{1,0:T(8,128)S(1)}, f32[16,128]{1,0:T(8,128)S(1)}, u32[]{:S(2)}, u32[]{:S(2)}) collective-permute-start(f32[16,128]{1,0:T(8,128)S(1)} %add_add_fusion.5), channel_id=1, source_target_pairs={{0,24},{1,25},{2,26},{3,27},{4,28},{5,29},{6,30},{7,31},{8,0},{9,1... | collective-permute-start | bytes 24584 | tf_op jit(solution)/shard_map/ppermute | solution.py:465
  45.2 0.0 collective-permute-start.9
  45.2 0.9 collective-permute-start.8
  46.1 0.0 collective-permute-done.6
  46.1 0.0 collective-permute-done.7
  46.1 3.8 %shard_map.53 = (bf16[8,16,240,128]{3,2,1,0:T(8,128)(2,1)S(1)}, f32[24,16,128]{2,1,0:T(8,128)S(1)}) custom-call(s32[3]{0:T(128)S(1)} %pad_add_fusion.info, f32[1088,128]{1,0:T(8,128)S(1)} %bitcast.11, f32[1088,128]{1,0:T(8,128)S(1)} %bitcast.13, f32[1088,128]{1,0:T(8,128)S(1)} %bitcast.14, f32[1088,128]{1,0:T(8,128)S(1)} %bitcast.15, ...), custom_call_target="tpu_custom_call" | custom-call | flops 3000000000 | bytes 9000000 | tf_op jit(solution)/shard_map/pallas_call | solution.py:437
  50.0 0.0 collective-permute-done.10
  50.0 0.3 collective-permute-done.9
  50.3 0.0 collective-permute-done.8
  50.4 4.0 %collective-permute-start.13 = (f32[16,128]{1,0:T(8,128)S(1)}, f32[16,128]{1,0:T(8,128)S(1)}, u32[]{:S(2)}, u32[]{:S(2)}) collective-permute-start(f32[16,128]{1,0:T(8,128)S(1)} %add_add_fusion.4), channel_id=1, source_target_pairs={{0,96},{1,97},{2,98},{3,99},{4,100},{5,101},{6,102},{7,103},{8,104... | collective-permute-start | bytes 24584 | tf_op jit(solution)/shard_map/ppermute | solution.py:465
  54.4 0.6 collective-permute-start.12
  55.0 0.9 collective-permute-start.11
  55.9 0.0 collective-permute-done.13
  55.9 3.6 %collective-permute-done.12 = f32[16,128]{1,0:T(8,128)S(1)} collective-permute-done((f32[16,128]{1,0:T(8,128)S(1)}, f32[16,128]{1,0:T(8,128)S(1)}, u32[]{:S(2)}, u32[]{:S(2)}) %collective-permute-start.12) | collective-permute-done | bytes 8224 | tf_op jit(solution)/shard_map/ppermute | solution.py:465
  59.5 0.4 collective-permute-done.11
  59.9 18.6 %shard_map.54 = (bf16[8,16,240,128]{3,2,1,0:T(8,128)(2,1)S(1)}, bf16[8,16,240,128]{3,2,1,0:T(8,128)(2,1)S(1)}, f32[16,128]{1,0:T(8,128)S(1)}, f32[16,16,16,128]{3,2,1,0:T(8,128)S(1)}) custom-call(s32[3]{0:T(128)S(1)} %pad_add_fusion.info, f32[16,128]{1,0:T(8,128)S(1)} %add_add_fusion.3.mom_in, ...), custom_call_target="tpu_custom_call", output_to_operand_aliasing={{0}: (3, {}), {1}: (4, {})} | custom-call | flops 10000000000 | bytes 30000000 | tf_op jit(solution)/shard_map/pallas_call | solution.py:437
  78.4 0.1 collective-permute-start.14
  78.5 1.2 %collective-permute-done.14 = f32[16,128]{1,0:T(8,128)S(1)} collective-permute-done((f32[16,128]{1,0:T(8,128)S(1)}, f32[16,128]{1,0:T(8,128)S(1)}, u32[]{:S(2)}, u32[]{:S(2)}) %collective-permute-start.14) | collective-permute-done | bytes 8224 | tf_op jit(solution)/shard_map/ppermute | solution.py:465
  79.7 3.6 %collective-permute-start.17 = (f32[16,128]{1,0:T(8,128)S(1)}, f32[16,128]{1,0:T(8,128)S(1)}, u32[]{:S(2)}, u32[]{:S(2)}) collective-permute-start(f32[16,128]{1,0:T(8,128)S(1)} %add.74), channel_id=1, source_target_pairs={{0,6},{1,7},{2,0},{3,1},{4,2},{5,3},{6,4},{7,5},{8,14},{9,15},{10,... | collective-permute-start | bytes 24584 | tf_op jit(solution)/shard_map/ppermute | solution.py:465
  83.2 0.0 collective-permute-start.16
  83.2 0.9 collective-permute-start.15
  84.1 0.5 collective-permute-done.17
  84.6 3.8 %collective-permute-done.16 = f32[16,128]{1,0:T(8,128)S(1)} collective-permute-done((f32[16,128]{1,0:T(8,128)S(1)}, f32[16,128]{1,0:T(8,128)S(1)}, u32[]{:S(2)}, u32[]{:S(2)}) %collective-permute-start.16) | collective-permute-done | bytes 8224 | tf_op jit(solution)/shard_map/ppermute | solution.py:465
  88.4 0.0 collective-permute-done.15
  88.4 2.4 %collective-permute-start.20 = (f32[16,128]{1,0:T(8,128)S(1)}, f32[16,128]{1,0:T(8,128)S(1)}, u32[]{:S(2)}, u32[]{:S(2)}) collective-permute-start(f32[16,128]{1,0:T(8,128)S(1)} %add_add_fusion.2), channel_id=1, source_target_pairs={{0,24},{1,25},{2,26},{3,27},{4,28},{5,29},{6,30},{7,31},{8,0},{9,1... | collective-permute-start | bytes 24584 | tf_op jit(solution)/shard_map/ppermute | solution.py:465
  90.8 1.5 %collective-permute-start.19 = (f32[16,128]{1,0:T(8,128)S(1)}, f32[16,128]{1,0:T(8,128)S(1)}, u32[]{:S(2)}, u32[]{:S(2)}) collective-permute-start(f32[16,128]{1,0:T(8,128)S(1)} %add_add_fusion.2), channel_id=1, source_target_pairs={{0,16},{1,17},{2,18},{3,19},{4,20},{5,21},{6,22},{7,23},{8,24},{9,... | collective-permute-start | bytes 24584 | tf_op jit(solution)/shard_map/ppermute | solution.py:465
  92.4 1.3 %collective-permute-start.18 = (f32[16,128]{1,0:T(8,128)S(1)}, f32[16,128]{1,0:T(8,128)S(1)}, u32[]{:S(2)}, u32[]{:S(2)}) collective-permute-start(f32[16,128]{1,0:T(8,128)S(1)} %add_add_fusion.2), channel_id=1, source_target_pairs={{0,8},{1,9},{2,10},{3,11},{4,12},{5,13},{6,14},{7,15},{8,16},{9,17... | collective-permute-start | bytes 24584 | tf_op jit(solution)/shard_map/ppermute | solution.py:465
  93.7 0.0 collective-permute-done.20
  93.7 2.3 %collective-permute-done.19 = f32[16,128]{1,0:T(8,128)S(1)} collective-permute-done((f32[16,128]{1,0:T(8,128)S(1)}, f32[16,128]{1,0:T(8,128)S(1)}, u32[]{:S(2)}, u32[]{:S(2)}) %collective-permute-start.19) | collective-permute-done | bytes 8224 | tf_op jit(solution)/shard_map/ppermute | solution.py:465
  96.0 1.3 %collective-permute-done.18 = f32[16,128]{1,0:T(8,128)S(1)} collective-permute-done((f32[16,128]{1,0:T(8,128)S(1)}, f32[16,128]{1,0:T(8,128)S(1)}, u32[]{:S(2)}, u32[]{:S(2)}) %collective-permute-start.18) | collective-permute-done | bytes 8224 | tf_op jit(solution)/shard_map/ppermute | solution.py:465
  97.2 0.4 collective-permute-start.23
  97.6 1.4 %collective-permute-start.22 = (f32[16,128]{1,0:T(8,128)S(1)}, f32[16,128]{1,0:T(8,128)S(1)}, u32[]{:S(2)}, u32[]{:S(2)}) collective-permute-start(f32[16,128]{1,0:T(8,128)S(1)} %add_add_fusion.1), channel_id=1, source_target_pairs={{0,64},{1,65},{2,66},{3,67},{4,68},{5,69},{6,70},{7,71},{8,72},{9,... | collective-permute-start | bytes 24584 | tf_op jit(solution)/shard_map/ppermute | solution.py:465
  99.0 1.3 %collective-permute-start.21 = (f32[16,128]{1,0:T(8,128)S(1)}, f32[16,128]{1,0:T(8,128)S(1)}, u32[]{:S(2)}, u32[]{:S(2)}) collective-permute-start(f32[16,128]{1,0:T(8,128)S(1)} %add_add_fusion.1), channel_id=1, source_target_pairs={{0,32},{1,33},{2,34},{3,35},{4,36},{5,37},{6,38},{7,39},{8,40},{9,... | collective-permute-start | bytes 24584 | tf_op jit(solution)/shard_map/ppermute | solution.py:465
  100.3 0.6 collective-permute-done.23
  100.9 1.9 %collective-permute-done.22 = f32[16,128]{1,0:T(8,128)S(1)} collective-permute-done((f32[16,128]{1,0:T(8,128)S(1)}, f32[16,128]{1,0:T(8,128)S(1)}, u32[]{:S(2)}, u32[]{:S(2)}) %collective-permute-start.22) | collective-permute-done | bytes 8224 | tf_op jit(solution)/shard_map/ppermute | solution.py:465
  102.8 1.1 collective-permute-done.21
  103.9 9.1 %shard_map.55 = (f32[4096,128]{1,0:T(8,128)}, f32[4096,128]{1,0:T(8,128)}) custom-call(s32[3]{0:T(128)S(1)} %pad_add_fusion.info, f32[16,128]{1,0:T(8,128)S(1)} %add_add_fusion.mom_in, bf16[8,16,240,128]{3,2,1,0:T(8,128)(2,1)S(1)} %get-tuple-element.51.panel_a, bf16[8,16,240,128]{3,2,1,0:T(8,128)(2,1)S(1)} %get-tuple-element.52.panel_b, ...), custom_call_target="tpu_custom_call" | custom-call | flops 4000000000 | bytes 12000000 | tf_op jit(solution)/shard_map/pallas_call | solution.py:437
  (8 shorter events, 0.0 us)
Async XLA Ops:
  0.6 5.7 %copy-start.1 = (f32[16,16,128]{2,1,0:T(8,128)S(1)}, f32[16,16,128]{2,1,0:T(8,128)}, u32[]{:S(2)}) copy-start(f32[16,16,128]{2,1,0:T(8,128)} %diag.7) | copy-start | bytes 393220
  0.6 5.7 %copy-start = (f32[16,16,16,128]{3,2,1,0:T(8,128)S(1)}, f32[16,16,16,128]{3,2,1,0:T(8,128)}, u32[]{:S(2)}) copy-start(f32[16,16,16,128]{3,2,1,0:T(8,128)} %right.1) | copy-start | bytes 6291460
  3.7 10.7 %collective-permute-start = (f32[17,4,16,128]{3,2,1,0:T(8,128)S(1)}, f32[17,4,16,128]{3,2,1,0:T(8,128)S(1)}, u32[]{:S(2)}, u32[]{:S(2)}) collective-permute-start(f32[17,4,16,128]{3,2,1,0:T(8,128)S(1)} %get-tuple-element.29), channel_id=1, source_target_pairs={{0,1},{1,2},{2,3},{3,4},{4,5},{5,6},{6,7},{7,8},{8,9},{9,10},{10,1... | collective-permute-start | bytes 1671176 | tf_op jit(solution)/shard_map/ppermute | solution.py:492
  5.1 9.4 %collective-permute-start.1 = (f32[17,4,16,128]{3,2,1,0:T(8,128)S(1)}, f32[17,4,16,128]{3,2,1,0:T(8,128)S(1)}, u32[]{:S(2)}, u32[]{:S(2)}) collective-permute-start(f32[17,4,16,128]{3,2,1,0:T(8,128)S(1)} %get-tuple-element.30), channel_id=1, source_target_pairs={{1,0},{2,1},{3,2},{4,3},{5,4},{6,5},{7,6},{8,7},{9,8},{10,9},{11,1... | collective-permute-start | bytes 1671176 | tf_op jit(solution)/shard_map/ppermute | solution.py:493
  20.3 25.8 %collective-permute-start.6 = (f32[17,4,16,128]{3,2,1,0:T(8,128)S(1)}, f32[17,4,16,128]{3,2,1,0:T(8,128)S(1)}, u32[]{:S(2)}, u32[]{:S(2)}) collective-permute-start(f32[17,4,16,128]{3,2,1,0:T(8,128)S(1)} %get-tuple-element.40), channel_id=1, source_target_pairs={{0,1},{1,2},{2,3},{3,4},{4,5},{5,6},{6,7},{7,8},{8,9},{9,10},{10,1... | collective-permute-start | bytes 1671176 | tf_op jit(solution)/shard_map/ppermute | solution.py:519
  26.0 20.1 %collective-permute-start.7 = (f32[17,4,16,128]{3,2,1,0:T(8,128)S(1)}, f32[17,4,16,128]{3,2,1,0:T(8,128)S(1)}, u32[]{:S(2)}, u32[]{:S(2)}) collective-permute-start(f32[17,4,16,128]{3,2,1,0:T(8,128)S(1)} %get-tuple-element.41), channel_id=1, source_target_pairs={{1,0},{2,1},{3,2},{4,3},{5,4},{6,5},{7,6},{8,7},{9,8},{10,9},{11,1... | collective-permute-start | bytes 1671176 | tf_op jit(solution)/shard_map/ppermute | solution.py:520
  27.3 2.9 %collective-permute-start.2 = (f32[16,128]{1,0:T(8,128)S(1)}, f32[16,128]{1,0:T(8,128)S(1)}, u32[]{:S(2)}, u32[]{:S(2)}) collective-permute-start(f32[16,128]{1,0:T(8,128)S(1)} %get-tuple-element.39), channel_id=1, source_target_pairs={{0,1},{1,0},{2,3},{3,2},{4,5},{5,4},{6,7},{7,6},{8,9},{9,8},{10,11... | collective-permute-start | bytes 24584 | tf_op jit(solution)/shard_map/ppermute | solution.py:465
  30.2 7.9 %collective-permute-start.5 = (f32[16,128]{1,0:T(8,128)S(1)}, f32[16,128]{1,0:T(8,128)S(1)}, u32[]{:S(2)}, u32[]{:S(2)}) collective-permute-start(f32[16,128]{1,0:T(8,128)S(1)} %add.64), channel_id=1, source_target_pairs={{0,6},{1,7},{2,0},{3,1},{4,2},{5,3},{6,4},{7,5},{8,14},{9,15},{10,... | collective-permute-start | bytes 24584 | tf_op jit(solution)/shard_map/ppermute | solution.py:465
  35.5 5.2 %collective-permute-start.4 = (f32[16,128]{1,0:T(8,128)S(1)}, f32[16,128]{1,0:T(8,128)S(1)}, u32[]{:S(2)}, u32[]{:S(2)}) collective-permute-start(f32[16,128]{1,0:T(8,128)S(1)} %add.64), channel_id=1, source_target_pairs={{0,4},{1,5},{2,6},{3,7},{4,0},{5,1},{6,2},{7,3},{8,12},{9,13},{10,... | collective-permute-start | bytes 24584 | tf_op jit(solution)/shard_map/ppermute | solution.py:465
  35.5 5.2 %collective-permute-start.3 = (f32[16,128]{1,0:T(8,128)S(1)}, f32[16,128]{1,0:T(8,128)S(1)}, u32[]{:S(2)}, u32[]{:S(2)}) collective-permute-start(f32[16,128]{1,0:T(8,128)S(1)} %add.64), channel_id=1, source_target_pairs={{0,2},{1,3},{2,4},{3,5},{4,6},{5,7},{6,0},{7,1},{8,10},{9,11},{10,... | collective-permute-start | bytes 24584 | tf_op jit(solution)/shard_map/ppermute | solution.py:465
  40.6 9.4 %collective-permute-start.10 = (f32[16,128]{1,0:T(8,128)S(1)}, f32[16,128]{1,0:T(8,128)S(1)}, u32[]{:S(2)}, u32[]{:S(2)}) collective-permute-start(f32[16,128]{1,0:T(8,128)S(1)} %add_add_fusion.5), channel_id=1, source_target_pairs={{0,24},{1,25},{2,26},{3,27},{4,28},{5,29},{6,30},{7,31},{8,0},{9,1... | collective-permute-start | bytes 24584 | tf_op jit(solution)/shard_map/ppermute | solution.py:465
  45.2 5.2 %collective-permute-start.9 = (f32[16,128]{1,0:T(8,128)S(1)}, f32[16,128]{1,0:T(8,128)S(1)}, u32[]{:S(2)}, u32[]{:S(2)}) collective-permute-start(f32[16,128]{1,0:T(8,128)S(1)} %add_add_fusion.5), channel_id=1, source_target_pairs={{0,16},{1,17},{2,18},{3,19},{4,20},{5,21},{6,22},{7,23},{8,24},{9,... | collective-permute-start | bytes 24584 | tf_op jit(solution)/shard_map/ppermute | solution.py:465
  45.2 5.2 %collective-permute-start.8 = (f32[16,128]{1,0:T(8,128)S(1)}, f32[16,128]{1,0:T(8,128)S(1)}, u32[]{:S(2)}, u32[]{:S(2)}) collective-permute-start(f32[16,128]{1,0:T(8,128)S(1)} %add_add_fusion.5), channel_id=1, source_target_pairs={{0,8},{1,9},{2,10},{3,11},{4,12},{5,13},{6,14},{7,15},{8,16},{9,17... | collective-permute-start | bytes 24584 | tf_op jit(solution)/shard_map/ppermute | solution.py:465
  50.4 5.6 %collective-permute-start.13 = (f32[16,128]{1,0:T(8,128)S(1)}, f32[16,128]{1,0:T(8,128)S(1)}, u32[]{:S(2)}, u32[]{:S(2)}) collective-permute-start(f32[16,128]{1,0:T(8,128)S(1)} %add_add_fusion.4), channel_id=1, source_target_pairs={{0,96},{1,97},{2,98},{3,99},{4,100},{5,101},{6,102},{7,103},{8,104... | collective-permute-start | bytes 24584 | tf_op jit(solution)/shard_map/ppermute | solution.py:465
  54.4 5.2 %collective-permute-start.12 = (f32[16,128]{1,0:T(8,128)S(1)}, f32[16,128]{1,0:T(8,128)S(1)}, u32[]{:S(2)}, u32[]{:S(2)}) collective-permute-start(f32[16,128]{1,0:T(8,128)S(1)} %add_add_fusion.4), channel_id=1, source_target_pairs={{0,64},{1,65},{2,66},{3,67},{4,68},{5,69},{6,70},{7,71},{8,72},{9,... | collective-permute-start | bytes 24584 | tf_op jit(solution)/shard_map/ppermute | solution.py:465
  55.0 4.9 %collective-permute-start.11 = (f32[16,128]{1,0:T(8,128)S(1)}, f32[16,128]{1,0:T(8,128)S(1)}, u32[]{:S(2)}, u32[]{:S(2)}) collective-permute-start(f32[16,128]{1,0:T(8,128)S(1)} %add_add_fusion.4), channel_id=1, source_target_pairs={{0,32},{1,33},{2,34},{3,35},{4,36},{5,37},{6,38},{7,39},{8,40},{9,... | collective-permute-start | bytes 24584 | tf_op jit(solution)/shard_map/ppermute | solution.py:465
  78.4 1.3 %collective-permute-start.14 = (f32[16,128]{1,0:T(8,128)S(1)}, f32[16,128]{1,0:T(8,128)S(1)}, u32[]{:S(2)}, u32[]{:S(2)}) collective-permute-start(f32[16,128]{1,0:T(8,128)S(1)} %get-tuple-element.50), channel_id=1, source_target_pairs={{0,1},{1,0},{2,3},{3,2},{4,5},{5,4},{6,7},{7,6},{8,9},{9,8},{10,11... | collective-permute-start | bytes 24584 | tf_op jit(solution)/shard_map/ppermute | solution.py:465
  79.7 4.9 %collective-permute-start.17 = (f32[16,128]{1,0:T(8,128)S(1)}, f32[16,128]{1,0:T(8,128)S(1)}, u32[]{:S(2)}, u32[]{:S(2)}) collective-permute-start(f32[16,128]{1,0:T(8,128)S(1)} %add.74), channel_id=1, source_target_pairs={{0,6},{1,7},{2,0},{3,1},{4,2},{5,3},{6,4},{7,5},{8,14},{9,15},{10,... | collective-permute-start | bytes 24584 | tf_op jit(solution)/shard_map/ppermute | solution.py:465
  83.2 5.2 %collective-permute-start.16 = (f32[16,128]{1,0:T(8,128)S(1)}, f32[16,128]{1,0:T(8,128)S(1)}, u32[]{:S(2)}, u32[]{:S(2)}) collective-permute-start(f32[16,128]{1,0:T(8,128)S(1)} %add.74), channel_id=1, source_target_pairs={{0,4},{1,5},{2,6},{3,7},{4,0},{5,1},{6,2},{7,3},{8,12},{9,13},{10,... | collective-permute-start | bytes 24584 | tf_op jit(solution)/shard_map/ppermute | solution.py:465
  83.2 5.2 %collective-permute-start.15 = (f32[16,128]{1,0:T(8,128)S(1)}, f32[16,128]{1,0:T(8,128)S(1)}, u32[]{:S(2)}, u32[]{:S(2)}) collective-permute-start(f32[16,128]{1,0:T(8,128)S(1)} %add.74), channel_id=1, source_target_pairs={{0,2},{1,3},{2,4},{3,5},{4,6},{5,7},{6,0},{7,1},{8,10},{9,11},{10,... | collective-permute-start | bytes 24584 | tf_op jit(solution)/shard_map/ppermute | solution.py:465
  88.4 5.3 %collective-permute-start.20 = (f32[16,128]{1,0:T(8,128)S(1)}, f32[16,128]{1,0:T(8,128)S(1)}, u32[]{:S(2)}, u32[]{:S(2)}) collective-permute-start(f32[16,128]{1,0:T(8,128)S(1)} %add_add_fusion.2), channel_id=1, source_target_pairs={{0,24},{1,25},{2,26},{3,27},{4,28},{5,29},{6,30},{7,31},{8,0},{9,1... | collective-permute-start | bytes 24584 | tf_op jit(solution)/shard_map/ppermute | solution.py:465
  90.8 5.2 %collective-permute-start.19 = (f32[16,128]{1,0:T(8,128)S(1)}, f32[16,128]{1,0:T(8,128)S(1)}, u32[]{:S(2)}, u32[]{:S(2)}) collective-permute-start(f32[16,128]{1,0:T(8,128)S(1)} %add_add_fusion.2), channel_id=1, source_target_pairs={{0,16},{1,17},{2,18},{3,19},{4,20},{5,21},{6,22},{7,23},{8,24},{9,... | collective-permute-start | bytes 24584 | tf_op jit(solution)/shard_map/ppermute | solution.py:465
  92.4 4.9 %collective-permute-start.18 = (f32[16,128]{1,0:T(8,128)S(1)}, f32[16,128]{1,0:T(8,128)S(1)}, u32[]{:S(2)}, u32[]{:S(2)}) collective-permute-start(f32[16,128]{1,0:T(8,128)S(1)} %add_add_fusion.2), channel_id=1, source_target_pairs={{0,8},{1,9},{2,10},{3,11},{4,12},{5,13},{6,14},{7,15},{8,16},{9,17... | collective-permute-start | bytes 24584 | tf_op jit(solution)/shard_map/ppermute | solution.py:465
  97.2 3.7 %collective-permute-start.23 = (f32[16,128]{1,0:T(8,128)S(1)}, f32[16,128]{1,0:T(8,128)S(1)}, u32[]{:S(2)}, u32[]{:S(2)}) collective-permute-start(f32[16,128]{1,0:T(8,128)S(1)} %add_add_fusion.1), channel_id=1, source_target_pairs={{0,96},{1,97},{2,98},{3,99},{4,100},{5,101},{6,102},{7,103},{8,104... | collective-permute-start | bytes 24584 | tf_op jit(solution)/shard_map/ppermute | solution.py:465
  97.6 5.2 %collective-permute-start.22 = (f32[16,128]{1,0:T(8,128)S(1)}, f32[16,128]{1,0:T(8,128)S(1)}, u32[]{:S(2)}, u32[]{:S(2)}) collective-permute-start(f32[16,128]{1,0:T(8,128)S(1)} %add_add_fusion.1), channel_id=1, source_target_pairs={{0,64},{1,65},{2,66},{3,67},{4,68},{5,69},{6,70},{7,71},{8,72},{9,... | collective-permute-start | bytes 24584 | tf_op jit(solution)/shard_map/ppermute | solution.py:465
  99.0 4.9 %collective-permute-start.21 = (f32[16,128]{1,0:T(8,128)S(1)}, f32[16,128]{1,0:T(8,128)S(1)}, u32[]{:S(2)}, u32[]{:S(2)}) collective-permute-start(f32[16,128]{1,0:T(8,128)S(1)} %add_add_fusion.1), channel_id=1, source_target_pairs={{0,32},{1,33},{2,34},{3,35},{4,36},{5,37},{6,38},{7,39},{8,40},{9,... | collective-permute-start | bytes 24584 | tf_op jit(solution)/shard_map/ppermute | solution.py:465

commit v3 on v2

v3 whole, which is shorter than its diff:
```python
import jax
import jax.numpy as jnp
from jax import lax
from jax.experimental import pallas as pl
from jax.experimental.pallas import tpu as pltpu
from jax.sharding import PartitionSpec as P

NRHS = 16
SSTEP = 4
SHIFT = 8.5
SCALE = 7.5
CX = 16
NY = 16
NZ = 128
KB = SSTEP + 1
PIECE = KB * NRHS
MID = CX - 2 * SSTEP
MIDDLE = CX + 2 * SSTEP
AXES = ("grp", "dom")
F32 = jnp.float32
BF16 = jnp.bfloat16
FIELD = (NY, NRHS, NZ)
PANEL = (NY, 3 * PIECE, NZ)


def over(start, stop, body, group=4):
    whole = (stop - start) // group

    def step(i, carry):
        for k in range(group):
            body(start + i * group + k)
        return carry

    if whole:
        lax.fori_loop(0, whole, step, 0)
    for plane in range(start + whole * group, stop):
        body(plane)


def pieces(value):
    hi = value.astype(BF16)
    rest = value - hi.astype(F32)
    mid = rest.astype(BF16)
    lo = (rest - mid.astype(F32)).astype(BF16)
    return hi, mid, lo


def store_pieces(panel, plane, y, power, value):
    for i, part in enumerate(pieces(value)):
        panel[plane, y, pl.ds(i * PIECE + power * NRHS, NRHS), :] = part


def split_plane(panel, at, power, field, plane):
    for y in range(NY):
        store_pieces(panel, at, y, power, field[plane, y])


def coef_of(diag):
    return (diag + (6.0 - SHIFT)) * (1.0 / SCALE)


def plane_step(below, centre_at, above, coef, weight, emit):
    lane = lax.broadcasted_iota(jnp.int32, (NRHS, NZ), 1)
    first = lane == 0
    last = lane == NZ - 1
    zero = jnp.zeros((NRHS, NZ), F32)
    src, plane = centre_at
    before = zero
    centre = src[plane, 0]
    for y in range(NY):
        after = src[plane, y + 1] if y + 1 < NY else zero
        beside = below[0][below[1], y] + above[0][above[1], y] + (before + after)
        beside = beside + jnp.where(first, 0.0, pltpu.roll(centre, 1, 1))
        beside = beside + jnp.where(last, 0.0, pltpu.roll(centre, NZ - 1, 1))
        emit(y, coef(y) * centre - weight * beside)
        before, centre = centre, after


def moment_sum(panel, plane, acc):
    for y in range(0, NY, 2):

        def rows(at, size):
            return jnp.concatenate(
                [panel[plane, y, pl.ds(at, size), :], panel[plane, y + 1, pl.ds(at, size), :]], 1
            )

        ends = [rows(at, NRHS) for at in (0, PIECE, SSTEP * NRHS, PIECE + SSTEP * NRHS)]
        acc = acc + lax.dot_general(
            rows(0, 2 * PIECE),
            jnp.concatenate(ends, 0),
            (((1,), (1,)), ((), ())),
            preferred_element_type=F32,
        )
    return acc


def moment_zero():
    return jnp.zeros((2 * PIECE, 4 * NRHS), F32)


def moment_blocks(acc):
    acc = acc[:PIECE] + acc[PIECE:]
    low = acc[:, :NRHS] + acc[:, NRHS : 2 * NRHS]
    high = acc[:, 2 * NRHS : 3 * NRHS] + acc[:, 3 * NRHS :]
    blocks = [low[j * NRHS : (j + 1) * NRHS] for j in range(KB)]
    blocks += [high[j * NRHS : (j + 1) * NRHS] for j in range(1, SSTEP)]
    return jnp.concatenate(blocks, 1)


def inverse4(m):
    def inverse2(a, b, d):
        scale = 1.0 / (a * d - b * b)
        return d * scale, -b * scale, a * scale

    p, q, r = inverse2(m[0][0], m[0][1], m[1][1])
    f00, f01 = p * m[0][2] + q * m[1][2], p * m[0][3] + q * m[1][3]
    f10, f11 = q * m[0][2] + r * m[1][2], q * m[0][3] + r * m[1][3]
    a = m[2][2] - (m[0][2] * f00 + m[1][2] * f10)
    b = m[2][3] - (m[0][2] * f01 + m[1][2] * f11)
    d = m[3][3] - (m[0][3] * f01 + m[1][3] * f11)
    u, v, w = inverse2(a, b, d)
    g00, g01 = f00 * u + f01 * v, f00 * v + f01 * w
    g10, g11 = f10 * u + f11 * v, f10 * v + f11 * w
    x00 = p + (g00 * f00 + g01 * f01)
    x01 = q + (g00 * f10 + g01 * f11)
    x11 = r + (g10 * f10 + g11 * f11)
    return [
        [x00, x01, -g00, -g01],
        [x01, x11, -g10, -g11],
        [-g00, -g10, u, v],
        [-g01, -g11, v, w],
    ]


def solve(mom):
    size = SSTEP * NRHS
    step = 4
    shifted = jnp.concatenate([mom[:, NRHS:], mom[:, :NRHS]], 1)
    band = SHIFT * mom + SCALE * shifted
    blocks = [band[:, i * NRHS : i * NRHS + size] for i in range(SSTEP)]
    work = jnp.concatenate(blocks + [mom[:, :size]], 0)
    lane = lax.broadcasted_iota(jnp.int32, (1, size), 1)
    for j in range(0, size, step):
        off = j % 8
        if off == 0 and j:
            work = work[8:]
        inside = (lane >= j) & (lane < j + step)
        rows = work[off : off + step]
        cols = [jnp.broadcast_to(rows[:, j + t : j + t + 1], (step, size)) for t in range(step)]
        inverse = inverse4([[cols[t][s : s + 1] for t in range(step)] for s in range(step)])
        new = []
        for s in range(step):
            row = inverse[s][0] * rows[0:1]
            unit = inverse[s][0]
            for t in range(1, step):
                row = row + inverse[s][t] * rows[t : t + 1]
                unit = jnp.where(lane == j + t, inverse[s][t], unit)
            new.append(jnp.where(inside, unit, row))
        acc = work[:, j : j + 1] * new[0]
        for t in range(1, step):
            acc = acc + work[:, j + t : j + t + 1] * new[t]
        work = jnp.where(inside, acc, work - acc)
    return work[8:]


def coef_rows(coef_t):
    pad = jnp.zeros((NRHS, NRHS), F32)
    eye = (
        lax.broadcasted_iota(jnp.int32, (NRHS, PIECE), 0)
        == lax.broadcasted_iota(jnp.int32, (NRHS, PIECE), 1)
    ).astype(F32)
    same = jnp.concatenate([coef_t, pad], 1)
    up = jnp.concatenate([pad, coef_t], 1)
    left = eye - (SHIFT * same + SCALE * up)
    l_hi, l_mid, l_lo = pieces(left)
    c_hi, c_mid, _ = pieces(same)
    none = jnp.zeros((NRHS, PIECE), BF16)
    rows = [
        [l_hi, l_hi, l_hi],
        [l_mid, l_mid, none],
        [l_lo, none, none],
        [c_hi, c_hi, none],
        [c_mid, none, none],
    ]
    return jnp.concatenate([jnp.concatenate(r, 1) for r in rows], 0)


def combine(coefs, panel, plane, emit):
    for y in range(0, NY, 2):
        block = jnp.concatenate([panel[plane, y], panel[plane, y + 1]], 1)
        out = jnp.dot(coefs, block, preferred_element_type=F32)
        left = out[:NRHS] + out[NRHS : 2 * NRHS] + out[2 * NRHS : 3 * NRHS]
        step = out[3 * NRHS : 4 * NRHS] + out[4 * NRHS :]
        for k in range(2):
            emit(y + k, left[:, k * NZ : (k + 1) * NZ], step[:, k * NZ : (k + 1) * NZ])


def pack(right, diag, places, sems):
    copies = []
    for i, (out, at) in enumerate(places):
        copies.append(
            pltpu.make_async_copy(
                right.at[:, pl.ds(at, SSTEP)], out.at[pl.ds(0, NRHS)], sems.at[2 * i]
            )
        )
        copies.append(
            pltpu.make_async_copy(diag.at[pl.ds(at, SSTEP)], out.at[NRHS], sems.at[2 * i + 1])
        )
    for copy in copies:
        copy.start()
    return copies


def pack_kernel(info, right, diag, near_same, near_next, far_same, far_next, sems):
    count = info[0]
    even = info[1] % 2 == 0
    places = (
        (near_same, jnp.where(even, count - SSTEP, 0)),
        (near_next, jnp.where(even, 0, count - SSTEP)),
        (far_same, jnp.where(even, count - 2 * SSTEP, SSTEP)),
        (far_next, jnp.where(even, SSTEP, count - 2 * SSTEP)),
    )
    for copy in pack(right, diag, places, sems):
        copy.wait()


def inner_kernel(info, right, diag, panel, mom, field_0, field_1, field_2, field_3):
    count = info[0]
    rows = NY * CX
    fields = (field_0, field_1, field_2, field_3)

    def load(p):
        for y in range(NY):
            field_0[p, y] = right[pl.Slice(p * NY + y, NRHS, rows), :]

    over(0, CX, load)

    def keep_of(p):
        return (p < count - SSTEP).astype(F32)

    def split(p):
        keep = keep_of(p + SSTEP)
        for y in range(NY):
            store_pieces(panel, p + SSTEP, y, 0, field_0[p + SSTEP, y] * keep)

    over(0, MID, split)
    weight = 1.0 / SCALE
    for power in range(1, SSTEP + 1):
        src = fields[power - 1]

        def apply(p, inner):
            keep = keep_of(p)

            def emit(y, value):
                if power < SSTEP:
                    fields[power][p, y] = value
                if inner:
                    store_pieces(panel, p, y, power, value * keep)

            plane_step(
                (src, p - 1), (src, p), (src, p + 1),
                lambda y: coef_of(diag[p, pl.ds(y, 1), :]), weight, emit,
            )

        for p in range(power, SSTEP):
            apply(p, False)
            apply(CX - 1 - p, False)
        over(SSTEP, CX - SSTEP, lambda p: apply(p, True))

    def two(i, acc):
        return moment_sum(panel, SSTEP + 2 * i + 1, moment_sum(panel, SSTEP + 2 * i, acc))

    mom[...] = moment_blocks(lax.fori_loop(0, MID // 2, two, moment_zero()))


def load_halo(info, same, following, field_l, field_u, diags):
    even = info[1] % 2 == 0

    def pick(at):
        a, b = same[at, :], following[at, :]
        return jnp.where(even, b, a), jnp.where(even, a, b)

    for i in range(SSTEP):
        for y in range(NY):
            low, high = pick(pl.Slice(i * NY + y, NRHS, SSTEP * NY))
            field_l[i, y] = low
            field_u[SSTEP - 1 - i, y] = high
        low, high = pick(pl.ds((NRHS * SSTEP + i) * NY, NY))
        diags[i] = low
        diags[SSTEP + i] = high


def edge_kernel(
    info, same, following, diag, mom_in, field_0, field_1, field_2, field_3, panel_in,
    panel, mom, side_l, side_u, diags,
):
    count = info[0]
    fields = (field_0, field_1, field_2, field_3)
    acc = moment_zero()
    load_halo(info, same, following, side_l.at[0], side_u.at[0], diags)
    for top in (False, True):
        side = side_u if top else side_l
        outside = jnp.where(info[2 if top else 1] > 0, 1.0 / SCALE, 0.0).astype(F32)

        def own(q):
            return count - 1 - q if top else q

        def slot(q):
            return CX - 1 - q if top else q

        for power in range(SSTEP + 1):

            def source(level, q):
                if q <= level - 1:
                    return side.at[level], q - (level - SSTEP)
                return fields[level], own(q)

            for q in range(power, SSTEP):
                split_plane(panel, slot(q), power, fields[power], own(q))
            if power == 0:
                continue
            for q in range(power - SSTEP, power):

                def coef(y):
                    if q >= 0:
                        return coef_of(diag[own(q), pl.ds(y, 1), :])
                    return coef_of(diags[SSTEP - 1 - q if top else q + SSTEP, pl.ds(y, 1), :])

                def emit(y, value):
                    if power < SSTEP:
                        side[power, q - (power - SSTEP), y] = value
                    if q >= 0:
                        store_pieces(panel, slot(q), y, power, value)

                plane_step(
                    source(power - 1, q - 1), source(power - 1, q), source(power - 1, q + 1),
                    coef, outside if q < 0 else 1.0 / SCALE, emit,
                )
            if top:
                acc = moment_sum(panel, power - 1, acc)
    for q in range(SSTEP):
        acc = moment_sum(panel, CX - 1 - q, acc)
    mom[...] = mom_in[...] + moment_blocks(acc)


def ghost_kernel(
    info, same, following, diag, diags, side_l, side_u, panel, coef, far_l, far_u, far_b, far_diags
):
    count = info[0]
    for i in range(MIDDLE - CX):
        coef[CX + i] = jnp.zeros((NY, NZ), F32)
    for i in range(CX):
        coef[SSTEP + i] = coef_of(diag[i])
    for i in range(SSTEP):
        coef[i] = coef_of(diags[i])
        coef[SSTEP + count + i] = coef_of(diags[SSTEP + i])
    load_halo(info, same, following, far_l, far_u, far_diags)
    for top in (False, True):
        side, far_a = (side_u, far_u) if top else (side_l, far_l)
        weight = jnp.where(info[2 if top else 1] > 0, 1.0 / SCALE, 0.0).astype(F32)
        shift = SSTEP if top else 0
        buffers = (far_a, far_b)
        for power in range(SSTEP + 1):
            for q in range(power - SSTEP, 0):
                split_plane(panel, q + SSTEP + shift, power, side.at[power], q - (power - SSTEP))
            if power == 0:
                continue
            src, dst = buffers[(power - 1) % 2], buffers[power % 2]

            def source(q):
                if q <= power - 6:
                    return src, q - (power - 9)
                return side.at[power - 1], q - (power - 5)

            for q in range(power - 8, power - 4):

                def diag_row(y):
                    if q >= -SSTEP:
                        return coef_of(diags[SSTEP - 1 - q if top else q + SSTEP, pl.ds(y, 1), :])
                    return coef_of(far_diags[-1 - q if top else q + 2 * SSTEP, pl.ds(y, 1), :])

                def emit(y, value):
                    if power < SSTEP:
                        dst[q - (power - 8), y] = value
                    if q >= -SSTEP:
                        store_pieces(panel, q + SSTEP + shift, y, power, value)

                plane_step(source(q - 1), source(q), source(q + 1), diag_row, weight, emit)


def middle_kernel(
    info, mom_in, coef, panel_in, ghost, panel, mom, iterate, field_0, field_1, field_2, field_3
):
    count = info[0]
    coefs = coef_rows(solve(mom_in[...]))

    def weight_of(plane):
        inside = (
            ((plane >= SSTEP) | (info[1] > 0))
            & ((plane < SSTEP + count) | (info[2] > 0))
            & (plane < 2 * SSTEP + count)
        )
        return jnp.where(inside, 1.0 / SCALE, 0.0).astype(F32)

    def update(store, plane, at, own):
        def emit(y, left, step):
            field_0[at, y] = left
            if own:
                iterate[at - SSTEP, y] = step

        combine(coefs, store, plane, emit)

    for i in range(MIDDLE - CX):
        field_0[CX + i] = jnp.zeros(FIELD, F32)
    for i in range(SSTEP):
        iterate[CX - SSTEP + i] = jnp.zeros(FIELD, F32)
    over(0, SSTEP, lambda p: update(ghost, p, p, False))
    over(0, CX - SSTEP, lambda p: update(panel_in, p, p + SSTEP, True))
    over(0, SSTEP, lambda p: update(panel_in, CX - SSTEP + p, count + p, True))
    over(0, SSTEP, lambda p: update(ghost, 2 * SSTEP - 1 - p, count + SSTEP + p, False))
    fields = (field_0, field_1, field_2, field_3)

    def keep_of(p):
        return (p < SSTEP + count).astype(F32)

    def apply(power, p, own):
        src = fields[power - 1]
        keep = keep_of(p)
        if own and power == 1:
            for y in range(NY):
                store_pieces(panel, p - SSTEP, y, 0, src[p, y] * keep)

        def emit(y, value):
            if power < SSTEP:
                fields[power][p, y] = value
            if own:
                store_pieces(panel, p - SSTEP, y, power, value * keep)

        plane_step(
            (src, p - 1), (src, p), (src, p + 1),
            lambda y: coef[p, pl.ds(y, 1), :], weight_of(p), emit,
        )

    def step(p, acc):
        acc = moment_sum(panel, p - 7 - SSTEP, acc)
        for power in range(SSTEP, 0, -1):
            apply(power, p - 2 * (power - 1), True)
        return acc

    def partial_step(p, acc):
        if SSTEP <= p - 7 < SSTEP + CX:
            acc = moment_sum(panel, p - 7 - SSTEP, acc)
        for power in range(SSTEP, 0, -1):
            q = p - 2 * (power - 1)
            if power <= q < MIDDLE - power:
                apply(power, q, SSTEP <= q < SSTEP + CX)
        return acc

    acc = moment_zero()
    for p in range(1, 11):
        acc = partial_step(p, acc)
    acc = lax.fori_loop(11, 20, step, acc)
    for p in range(20, 27):
        acc = partial_step(p, acc)
    mom[...] = moment_blocks(acc)


def last_kernel(info, mom_in, panel, iterate, solution_field, residual, new_field, new_residual, sems):
    rows = NY * CX
    group = 4
    coefs = coef_rows(solve(mom_in[...]))

    def copies(i):
        planes = pl.ds(i * group, group)
        return [
            pltpu.make_async_copy(new_field.at[:, planes], solution_field.at[:, planes], sems.at[0, i]),
            pltpu.make_async_copy(new_residual.at[:, planes], residual.at[:, planes], sems.at[1, i]),
        ]

    flat = NRHS * rows, NZ
    flat_field, flat_residual = new_field.reshape(flat), new_residual.reshape(flat)

    def body(i, carry):
        for k in range(group):
            p = i * group + k

            def emit(y, left, step):
                at = pl.Slice(p * NY + y, NRHS, rows)
                flat_residual[at, :] = left
                flat_field[at, :] = iterate[p, y] + step

            combine(coefs, panel, p, emit)
        for copy in copies(i):
            copy.start()
        return carry

    lax.fori_loop(0, CX // group, body, 0)
    for i in range(CX // group):
        for copy in copies(i):
            copy.wait()


SMEM_SPEC = pl.BlockSpec(memory_space=pltpu.SMEM)
VMEM_SPEC = pl.BlockSpec(memory_space=pltpu.VMEM)
HBM_SPEC = pl.BlockSpec(memory_space=pltpu.HBM)


def call(body, limit, operands, outs, scratch, kept_operands=(), far_operands=(), cost=1, aliases={}):
    operands = [
        pltpu.with_memory_space_constraint(x, pltpu.VMEM)
        if i in kept_operands
        else pltpu.with_memory_space_constraint(x, pltpu.HBM)
        if i in far_operands
        else x
        for i, x in enumerate(operands)
    ]
    return pl.pallas_call(
        body,
        out_shape=[pltpu.VMEM(s, d) if kept else jax.ShapeDtypeStruct(s, d) for s, d, kept in outs],
        in_specs=[SMEM_SPEC]
        + [HBM_SPEC if i in far_operands else VMEM_SPEC for i in range(1, len(operands))],
        out_specs=[VMEM_SPEC if kept is not None else HBM_SPEC for _, _, kept in outs],
        scratch_shapes=scratch,
        input_output_aliases=aliases,
        cost_estimate=pl.CostEstimate(
            flops=cost * 1_000_000_000, bytes_accessed=cost * 3_000_000, transcendentals=0
        ),
        compiler_params=pltpu.CompilerParams(vmem_limit_bytes=limit * 1024 * 1024),
    )(*operands)


def reduce_all(value, size, beside=None):
    if size == 128:
        rounds = [(1, 2), (2, 4), (8, 4), (32, 4)]
    else:
        rounds = [(1 << b, 2) for b in range(size.bit_length() - 1)]
    for place_in_order, (stride, width) in enumerate(rounds):
        total = value
        if beside is not None and place_in_order == 2:
            total, beside = lax.optimization_barrier((total, beside))
        for turn in range(1, width):
            route = []
            for i in range(size):
                place = i // stride % width
                route.append((i, i + ((place + turn) % width - place) * stride))
            total = total + lax.ppermute(value, AXES, route)
        value = total
    return value, beside


def local(right_side, diagonal, counts):
    count = counts[0]
    size = lax.axis_size(AXES)
    me = lax.axis_index(AXES)
    info = jnp.stack([count, me, size - 1 - me]).astype(jnp.int32)

    packed = ((NRHS + 1, SSTEP, NY, NZ), F32, True)
    panel_shape = ((CX,) + PANEL, BF16, True)
    near_same, near_next, far_same, far_next = call(
        pack_kernel,
        4,
        (info, right_side, diagonal),
        [packed] * 4,
        [pltpu.SemaphoreType.DMA((8,))],
        far_operands=(1, 2),
    )
    same = [(i, i ^ 1) for i in range(size)]
    following = [(i, i + 1) for i in range(1, size - 1, 2)] + [(i + 1, i) for i in range(1, size - 1, 2)]
    halo = ((NRHS + 1) * SSTEP * NY, NZ)
    next_halo = lax.ppermute(near_next, AXES, following).reshape(halo)
    same_halo = lax.ppermute(near_same, AXES, same).reshape(halo)
    panel, mom_inner, f0, f1, f2, f3 = call(
        inner_kernel,
        8,
        (info, right_side.reshape(NRHS * CX * NY, NZ), diagonal),
        [panel_shape, ((NRHS, NZ), F32, False)] + [((CX,) + FIELD, F32, True)] * SSTEP,
        [],
        cost=4,
    )
    panel, mom, side_l, side_u, diags = call(
        edge_kernel,
        8,
        (info, same_halo, next_halo, diagonal, mom_inner, f0, f1, f2, f3, panel),
        [
            panel_shape,
            ((NRHS, NZ), F32, False),
            ((SSTEP, SSTEP) + FIELD, F32, True),
            ((SSTEP, SSTEP) + FIELD, F32, True),
            ((2 * SSTEP, NY, NZ), F32, True),
        ],
        [],
        (5, 6, 7, 8, 9),
        cost=4,
        aliases={9: 0},
    )
    mom, far_next, far_same = lax.optimization_barrier((mom, far_next, far_same))
    far_next = lax.ppermute(far_next, AXES, following).reshape(halo)
    far_same = lax.ppermute(far_same, AXES, same).reshape(halo)
    ghost, coef = call(
        ghost_kernel,
        8,
        (info, far_same, far_next, diagonal, diags, side_l, side_u),
        [((2 * SSTEP,) + PANEL, BF16, True), ((MIDDLE, NY, NZ), F32, True)],
        [pltpu.VMEM((SSTEP,) + FIELD, F32)] * 3 + [pltpu.VMEM((2 * SSTEP, NY, NZ), F32)],
        (4, 5, 6),
        cost=3,
    )
    mom, coef = reduce_all(mom, size, coef)
    panel, mom, iterate = call(
        middle_kernel,
        16,
        (info, mom, coef, panel, ghost),
        [
            panel_shape,
            ((NRHS, NZ), F32, False),
            ((CX,) + FIELD, F32, True),
        ],
        [pltpu.VMEM((MIDDLE,) + FIELD, F32)] * SSTEP,
        (2, 3, 4),
        cost=10,
        aliases={3: 0},
    )
    mom, _ = reduce_all(mom, size)
    shape = right_side.shape
    solution_field, residual = call(
        last_kernel,
        8,
        (info, mom, panel, iterate),
        [(shape, F32, None), (shape, F32, None)],
        [pltpu.VMEM(shape, F32), pltpu.VMEM(shape, F32), pltpu.SemaphoreType.DMA((2, CX // 4))],
        (2, 3),
        cost=4,
    )
    return (solution_field, residual)


def solution(mesh):
    in_specs = (
        P(None, AXES, None, None),
        P(AXES, None, None),
        P(AXES),
    )
    out_specs = (P(None, AXES, None, None), P(None, AXES, None, None))
    return jax.shard_map(local, mesh=mesh, in_specs=in_specs, out_specs=out_specs, check_vma=False)
```

time: 113 us -> 104 us (0.920)
  Pallas kernels: 47.6 us -> 42.9 us
  starting transfers between devices: 41.2 us -> 38.3 us
  waiting for transfers between devices: 22.5 us -> 21.3 us
    ppermute x4, starting transfers between devices: 9.6 us -> 4.45 us  [the longest x1 2.98 us: local(): far_same = lax.ppermute(far_same, AXES, same).reshape(halo)]
    pallas_call x5 -> x6, Pallas kernels: 45.4 us -> 42.9 us  [call(): pl.pallas_call(body, out_shape=[pltpu.VMEM(s, d) if kept else jax.ShapeDt...]
    ppermute x20, starting transfers between devices: 31.6 us -> 33.8 us  [reduce_all(): total = total + lax.ppermute(value, AXES, route)]
    pallas_call x1 -> x0, Pallas kernels: 2.18 us -> none  [local(): pl.pallas_call(pack_kernel, out_shape=[pltpu.VMEM(packed[0], F32)] * 4, i...]
    ppermute x20, waiting for transfers between devices: 22.5 us -> 21.3 us  [reduce_all(): total = total + lax.ppermute(value, AXES, route)]
  transfers between devices with their start and end apart: 24 -> 24, of which waited for: 14 -> 15; matrix products, arithmetic and copies ran while one was open for 0% -> 0% of each run, Pallas kernels for 11% -> 12%
where the time goes in v3:
time: 104 us
  Pallas kernels  42.9 us (41%)
  starting transfers between devices  38.3 us (37%)
  waiting for transfers between devices  21.3 us (20%)
  between operations  1.77 us (2%)
    pallas_call x6, Pallas kernels, call(): pl.pallas_call(body, out_shape=[pltpu.VMEM(s, d) if kept else jax.ShapeDt...  42.9 us
    ppermute x20, starting transfers between devices, reduce_all(): total = total + lax.ppermute(value, AXES, route)  33.8 us
    ppermute x20, waiting for transfers between devices, reduce_all(): total = total + lax.ppermute(value, AXES, route)  21.3 us
    ppermute x1, starting transfers between devices, local(): far_same = lax.ppermute(far_same, AXES, same).reshape(halo)  2.98 us
  transfers between devices with their start and end apart: 24, of which 15 were waited for; matrix products, arithmetic and copies ran while one was open for 0% of the time, Pallas kernels for 12%

profile of v3, /device:TPU:0, one launch (start us, length us, event | category | flops | bytes accessed | tf_op | source)
XLA Modules:
  0.0 104.3 jit_solution(8074923558614915952)
XLA Ops:
  0.6 0.0 copy-start
  0.6 0.0 copy-start.1
  1.5 0.1 pad_add_fusion.info
  1.5 2.2 %shard_map.50 = (f32[17,4,16,128]{3,2,1,0:T(8,128)S(1)}, f32[17,4,16,128]{3,2,1,0:T(8,128)S(1)}, f32[17,4,16,128]{3,2,1,0:T(8,128)S(1)}, f32[17,4,16,128]{3,2,1,0:T(8,128)S(1)}) custom-call(s32[3]{0:T(128)S(1)} %pad_add_fusion.info, f32[16,16,16,128]{3,2,1,0:T(8,128)} %right.1, f32[16,16,128]{2,1,0:T(8,128)} %diag.7), custom_call_target="tpu_custom_call" | custom-call | flops 1000000000 | bytes 3000000 | tf_op jit(solution)/shard_map/pallas_call | solution.py:517
  3.7 0.1 collective-permute-start
  3.8 0.7 collective-permute-start.1
  4.5 0.0 copy-done
  4.5 0.0 copy-done.1
  4.5 8.1 %shard_map.51 = (bf16[16,16,240,128]{3,2,1,0:T(8,128)(2,1)S(1)}, f32[16,128]{1,0:T(8,128)S(1)}, f32[16,16,16,128]{3,2,1,0:T(8,128)S(1)}, f32[16,16,16,128]{3,2,1...) custom-call(s32[3]{0:T(128)S(1)} %pad_add_fusion.info, f32[4096,128]{1,0:T(8,128)S(1)} %bitcast.9, ...), custom_call_target="tpu_custom_call" | custom-call | flops 4000000000 | bytes 12000000 | tf_op jit(solution)/shard_map/pallas_call | solution.py:517
  12.7 0.0 collective-permute-done
  12.7 0.0 collective-permute-done.1
  12.7 5.2 %shard_map.52 = (bf16[16,16,240,128]{3,2,1,0:T(8,128)(2,1)S(1)}, f32[16,128]{1,0:T(8,128)S(1)}, f32[4,4,16,16,128]{4,3,2,1,0:T(8,128)S(1)}, f32[4,4,16,16,128]{4,3,2,1,0:T(8,128)S(1)}, f32[8,16,128]{2,1,0:T(8,128)S(1)}) custom-call(s32[3]{0:T(128)S(1)} %pad_add_fusion.info, f32[1088,128]{1,0:T(8,128)S(1)} %bitcast.7, ...), custom_call_target="tpu_custom_call", output_to_operand_aliasing={{0}: (9, {})} | custom-call | flops 4000000000 | bytes 12000000 | tf_op jit(solution)/shard_map/pallas_call | solution.py:517
  17.9 3.0 %collective-permute-start.6 = (f32[17,4,16,128]{3,2,1,0:T(8,128)S(1)}, f32[17,4,16,128]{3,2,1,0:T(8,128)S(1)}, u32[]{:S(2)}, u32[]{:S(2)}) collective-permute-start(f32[17,4,16,128]{3,2,1,0:T(8,128)S(1)} %get-tuple-element.39), channel_id=1, source_target_pairs={{0,1},{1,0},{2,3},{3,2},{4,5},{5,4},{6,7},{7,6},{8,9},{9,8},{10,11... | collective-permute-start | bytes 1671176 | tf_op jit(solution)/shard_map/ppermute | solution.py:598
  20.9 0.7 collective-permute-start.7
  21.6 2.9 %collective-permute-start.2 = (f32[16,128]{1,0:T(8,128)S(1)}, f32[16,128]{1,0:T(8,128)S(1)}, u32[]{:S(2)}, u32[]{:S(2)}) collective-permute-start(f32[16,128]{1,0:T(8,128)S(1)} %get-tuple-element.38), channel_id=1, source_target_pairs={{0,1},{1,0},{2,3},{3,2},{4,5},{5,4},{6,7},{7,6},{8,9},{9,8},{10,11... | collective-permute-start | bytes 24584 | tf_op jit(solution)/shard_map/ppermute | solution.py:546
  24.5 0.8 collective-permute-done.2
  25.3 4.4 %collective-permute-start.5 = (f32[16,128]{1,0:T(8,128)S(1)}, f32[16,128]{1,0:T(8,128)S(1)}, u32[]{:S(2)}, u32[]{:S(2)}) collective-permute-start(f32[16,128]{1,0:T(8,128)S(1)} %add.64), channel_id=1, source_target_pairs={{0,6},{1,7},{2,0},{3,1},{4,2},{5,3},{6,4},{7,5},{8,14},{9,15},{10,... | collective-permute-start | bytes 24584 | tf_op jit(solution)/shard_map/ppermute | solution.py:546
  29.7 0.1 collective-permute-start.4
  29.8 1.4 %collective-permute-start.3 = (f32[16,128]{1,0:T(8,128)S(1)}, f32[16,128]{1,0:T(8,128)S(1)}, u32[]{:S(2)}, u32[]{:S(2)}) collective-permute-start(f32[16,128]{1,0:T(8,128)S(1)} %add.64), channel_id=1, source_target_pairs={{0,2},{1,3},{2,4},{3,5},{4,6},{5,7},{6,0},{7,1},{8,10},{9,11},{10,... | collective-permute-start | bytes 24584 | tf_op jit(solution)/shard_map/ppermute | solution.py:546
  31.3 0.9 collective-permute-done.5
  32.2 2.8 %collective-permute-done.4 = f32[16,128]{1,0:T(8,128)S(1)} collective-permute-done((f32[16,128]{1,0:T(8,128)S(1)}, f32[16,128]{1,0:T(8,128)S(1)}, u32[]{:S(2)}, u32[]{:S(2)}) %collective-permute-start.4) | collective-permute-done | bytes 8224 | tf_op jit(solution)/shard_map/ppermute | solution.py:546
  35.0 0.0 collective-permute-done.3
  35.0 6.0 %collective-permute-start.10 = (f32[16,128]{1,0:T(8,128)S(1)}, f32[16,128]{1,0:T(8,128)S(1)}, u32[]{:S(2)}, u32[]{:S(2)}) collective-permute-start(f32[16,128]{1,0:T(8,128)S(1)} %add_add_fusion.5), channel_id=1, source_target_pairs={{0,24},{1,25},{2,26},{3,27},{4,28},{5,29},{6,30},{7,31},{8,0},{9,1... | collective-permute-start | bytes 24584 | tf_op jit(solution)/shard_map/ppermute | solution.py:546
  41.0 0.0 collective-permute-start.9
  41.0 0.9 collective-permute-start.8
  42.0 0.0 collective-permute-done.6
  42.0 0.0 collective-permute-done.7
  42.0 4.0 %shard_map.53 = (bf16[8,16,240,128]{3,2,1,0:T(8,128)(2,1)S(1)}, f32[24,16,128]{2,1,0:T(8,128)S(1)}) custom-call(s32[3]{0:T(128)S(1)} %pad_add_fusion.info, f32[1088,128]{1,0:T(8,128)S(1)} %bitcast.10, f32[1088,128]{1,0:T(8,128)S(1)} %bitcast.11, f32[16,16,128]{2,1,0:T(8,128)S(1)} %copy-done, f32[8,16,128]{2,1,0:T(8,128)S(1)} %get-tuple-element.41.diags, ...), custom_call_target="tpu_custom_call" | custom-call | flops 3000000000 | bytes 9000000 | tf_op jit(solution)/shard_map/pallas_call | solution.py:517
  45.9 0.0 collective-permute-done.10
  45.9 0.2 collective-permute-done.9
  46.2 0.0 collective-permute-done.8
  46.2 3.5 %collective-permute-start.13 = (f32[16,128]{1,0:T(8,128)S(1)}, f32[16,128]{1,0:T(8,128)S(1)}, u32[]{:S(2)}, u32[]{:S(2)}) collective-permute-start(f32[16,128]{1,0:T(8,128)S(1)} %add_add_fusion.4), channel_id=1, source_target_pairs={{0,96},{1,97},{2,98},{3,99},{4,100},{5,101},{6,102},{7,103},{8,104... | collective-permute-start | bytes 24584 | tf_op jit(solution)/shard_map/ppermute | solution.py:546
  49.6 0.4 collective-permute-start.12
  50.0 0.9 collective-permute-start.11
  51.0 0.1 collective-permute-done.13
  51.0 3.8 %collective-permute-done.12 = f32[16,128]{1,0:T(8,128)S(1)} collective-permute-done((f32[16,128]{1,0:T(8,128)S(1)}, f32[16,128]{1,0:T(8,128)S(1)}, u32[]{:S(2)}, u32[]{:S(2)}) %collective-permute-start.12) | collective-permute-done | bytes 8224 | tf_op jit(solution)/shard_map/ppermute | solution.py:546
  54.8 0.1 collective-permute-done.11
  54.9 15.3 %shard_map.54 = (bf16[16,16,240,128]{3,2,1,0:T(8,128)(2,1)S(1)}, f32[16,128]{1,0:T(8,128)S(1)}, f32[16,16,16,128]{3,2,1,0:T(8,128)S(1)}) custom-call(s32[3]{0:T(128)S(1)} %pad_add_fusion.info, f32[16,128]{1,0:T(8,128)S(1)} %add_add_fusion.3.mom_in, f32[24,16,128]{2,1,0:T(8,128)S(1)} %get-tuple-element.46.coef, ...), custom_call_target="tpu_custom_call", output_to_operand_aliasing={{0}: (3, {})} | custom-call | flops 10000000000 | bytes 30000000 | tf_op jit(solution)/shard_map/pallas_call | solution.py:517
  70.2 0.1 collective-permute-start.14
  70.3 1.2 %collective-permute-done.14 = f32[16,128]{1,0:T(8,128)S(1)} collective-permute-done((f32[16,128]{1,0:T(8,128)S(1)}, f32[16,128]{1,0:T(8,128)S(1)}, u32[]{:S(2)}, u32[]{:S(2)}) %collective-permute-start.14) | collective-permute-done | bytes 8224 | tf_op jit(solution)/shard_map/ppermute | solution.py:546
  71.5 3.6 %collective-permute-start.17 = (f32[16,128]{1,0:T(8,128)S(1)}, f32[16,128]{1,0:T(8,128)S(1)}, u32[]{:S(2)}, u32[]{:S(2)}) collective-permute-start(f32[16,128]{1,0:T(8,128)S(1)} %add.74), channel_id=1, source_target_pairs={{0,6},{1,7},{2,0},{3,1},{4,2},{5,3},{6,4},{7,5},{8,14},{9,15},{10,... | collective-permute-start | bytes 24584 | tf_op jit(solution)/shard_map/ppermute | solution.py:546
  75.1 0.0 collective-permute-start.16
  75.1 0.9 collective-permute-start.15
  75.9 0.5 collective-permute-done.17
  76.4 3.8 %collective-permute-done.16 = f32[16,128]{1,0:T(8,128)S(1)} collective-permute-done((f32[16,128]{1,0:T(8,128)S(1)}, f32[16,128]{1,0:T(8,128)S(1)}, u32[]{:S(2)}, u32[]{:S(2)}) %collective-permute-start.16) | collective-permute-done | bytes 8224 | tf_op jit(solution)/shard_map/ppermute | solution.py:546
  80.2 0.0 collective-permute-done.15
  80.2 2.5 %collective-permute-start.20 = (f32[16,128]{1,0:T(8,128)S(1)}, f32[16,128]{1,0:T(8,128)S(1)}, u32[]{:S(2)}, u32[]{:S(2)}) collective-permute-start(f32[16,128]{1,0:T(8,128)S(1)} %add_add_fusion.2), channel_id=1, source_target_pairs={{0,24},{1,25},{2,26},{3,27},{4,28},{5,29},{6,30},{7,31},{8,0},{9,1... | collective-permute-start | bytes 24584 | tf_op jit(solution)/shard_map/ppermute | solution.py:546
  82.7 1.6 %collective-permute-start.19 = (f32[16,128]{1,0:T(8,128)S(1)}, f32[16,128]{1,0:T(8,128)S(1)}, u32[]{:S(2)}, u32[]{:S(2)}) collective-permute-start(f32[16,128]{1,0:T(8,128)S(1)} %add_add_fusion.2), channel_id=1, source_target_pairs={{0,16},{1,17},{2,18},{3,19},{4,20},{5,21},{6,22},{7,23},{8,24},{9,... | collective-permute-start | bytes 24584 | tf_op jit(solution)/shard_map/ppermute | solution.py:546
  84.3 1.3 %collective-permute-start.18 = (f32[16,128]{1,0:T(8,128)S(1)}, f32[16,128]{1,0:T(8,128)S(1)}, u32[]{:S(2)}, u32[]{:S(2)}) collective-permute-start(f32[16,128]{1,0:T(8,128)S(1)} %add_add_fusion.2), channel_id=1, source_target_pairs={{0,8},{1,9},{2,10},{3,11},{4,12},{5,13},{6,14},{7,15},{8,16},{9,17... | collective-permute-start | bytes 24584 | tf_op jit(solution)/shard_map/ppermute | solution.py:546
  85.6 0.0 collective-permute-done.20
  85.6 2.3 %collective-permute-done.19 = f32[16,128]{1,0:T(8,128)S(1)} collective-permute-done((f32[16,128]{1,0:T(8,128)S(1)}, f32[16,128]{1,0:T(8,128)S(1)}, u32[]{:S(2)}, u32[]{:S(2)}) %collective-permute-start.19) | collective-permute-done | bytes 8224 | tf_op jit(solution)/shard_map/ppermute | solution.py:546
  87.9 1.3 %collective-permute-done.18 = f32[16,128]{1,0:T(8,128)S(1)} collective-permute-done((f32[16,128]{1,0:T(8,128)S(1)}, f32[16,128]{1,0:T(8,128)S(1)}, u32[]{:S(2)}, u32[]{:S(2)}) %collective-permute-start.18) | collective-permute-done | bytes 8224 | tf_op jit(solution)/shard_map/ppermute | solution.py:546
  89.2 0.6 collective-permute-start.23
  89.7 1.5 %collective-permute-start.22 = (f32[16,128]{1,0:T(8,128)S(1)}, f32[16,128]{1,0:T(8,128)S(1)}, u32[]{:S(2)}, u32[]{:S(2)}) collective-permute-start(f32[16,128]{1,0:T(8,128)S(1)} %add_add_fusion.1), channel_id=1, source_target_pairs={{0,64},{1,65},{2,66},{3,67},{4,68},{5,69},{6,70},{7,71},{8,72},{9,... | collective-permute-start | bytes 24584 | tf_op jit(solution)/shard_map/ppermute | solution.py:546
  91.2 1.3 %collective-permute-start.21 = (f32[16,128]{1,0:T(8,128)S(1)}, f32[16,128]{1,0:T(8,128)S(1)}, u32[]{:S(2)}, u32[]{:S(2)}) collective-permute-start(f32[16,128]{1,0:T(8,128)S(1)} %add_add_fusion.1), channel_id=1, source_target_pairs={{0,32},{1,33},{2,34},{3,35},{4,36},{5,37},{6,38},{7,39},{8,40},{9,... | collective-permute-start | bytes 24584 | tf_op jit(solution)/shard_map/ppermute | solution.py:546
  92.5 0.3 collective-permute-done.23
  92.8 2.1 %collective-permute-done.22 = f32[16,128]{1,0:T(8,128)S(1)} collective-permute-done((f32[16,128]{1,0:T(8,128)S(1)}, f32[16,128]{1,0:T(8,128)S(1)}, u32[]{:S(2)}, u32[]{:S(2)}) %collective-permute-start.22) | collective-permute-done | bytes 8224 | tf_op jit(solution)/shard_map/ppermute | solution.py:546
  94.9 1.2 %collective-permute-done.21 = f32[16,128]{1,0:T(8,128)S(1)} collective-permute-done((f32[16,128]{1,0:T(8,128)S(1)}, f32[16,128]{1,0:T(8,128)S(1)}, u32[]{:S(2)}, u32[]{:S(2)}) %collective-permute-start.21) | collective-permute-done | bytes 8224 | tf_op jit(solution)/shard_map/ppermute | solution.py:546
  96.1 8.1 %shard_map.55 = (f32[16,16,16,128]{3,2,1,0:T(8,128)}, f32[16,16,16,128]{3,2,1,0:T(8,128)}) custom-call(s32[3]{0:T(128)S(1)} %pad_add_fusion.info, f32[16,128]{1,0:T(8,128)S(1)} %add_add_fusion.mom_in, bf16[16,16,240,128]{3,2,1,0:T(8,128)(2,1)S(1)} %get-tuple-element.50.panel, f32[16,16,16,128]{3,2,1,0:T(8,128)S(1)} %get-tuple-element.51.iterate), custom_call_target="tpu_custom_call" | custom-call | flops 4000000000 | bytes 12000000 | tf_op jit(solution)/shard_map/pallas_call | solution.py:517
  (8 shorter events, 0.0 us)
Async XLA Ops:
  0.6 3.9 %copy-start = (f32[16,16,128]{2,1,0:T(8,128)S(1)}, f32[16,16,128]{2,1,0:T(8,128)}, u32[]{:S(2)}) copy-start(f32[16,16,128]{2,1,0:T(8,128)} %diag.7) | copy-start | bytes 393220
  0.6 3.9 %copy-start.1 = (f32[16,16,16,128]{3,2,1,0:T(8,128)S(1)}, f32[16,16,16,128]{3,2,1,0:T(8,128)}, u32[]{:S(2)}) copy-start(f32[16,16,16,128]{3,2,1,0:T(8,128)} %right.1) | copy-start | bytes 6291460
  3.7 8.9 %collective-permute-start = (f32[17,4,16,128]{3,2,1,0:T(8,128)S(1)}, f32[17,4,16,128]{3,2,1,0:T(8,128)S(1)}, u32[]{:S(2)}, u32[]{:S(2)}) collective-permute-start(f32[17,4,16,128]{3,2,1,0:T(8,128)S(1)} %get-tuple-element.27), channel_id=1, source_target_pairs={{0,1},{1,0},{2,3},{3,2},{4,5},{5,4},{6,7},{7,6},{8,9},{9,8},{10,11... | collective-permute-start | bytes 1671176 | tf_op jit(solution)/shard_map/ppermute | solution.py:571
  3.8 8.9 %collective-permute-start.1 = (f32[17,4,16,128]{3,2,1,0:T(8,128)S(1)}, f32[17,4,16,128]{3,2,1,0:T(8,128)S(1)}, u32[]{:S(2)}, u32[]{:S(2)}) collective-permute-start(f32[17,4,16,128]{3,2,1,0:T(8,128)S(1)} %get-tuple-element.28), channel_id=1, source_target_pairs={{1,2},{3,4},{5,6},{7,8},{9,10},{11,12},{13,14},{15,16},{17,18},{19... | collective-permute-start | bytes 1671176 | tf_op jit(solution)/shard_map/ppermute | solution.py:570
  17.9 24.0 %collective-permute-start.6 = (f32[17,4,16,128]{3,2,1,0:T(8,128)S(1)}, f32[17,4,16,128]{3,2,1,0:T(8,128)S(1)}, u32[]{:S(2)}, u32[]{:S(2)}) collective-permute-start(f32[17,4,16,128]{3,2,1,0:T(8,128)S(1)} %get-tuple-element.39), channel_id=1, source_target_pairs={{0,1},{1,0},{2,3},{3,2},{4,5},{5,4},{6,7},{7,6},{8,9},{9,8},{10,11... | collective-permute-start | bytes 1671176 | tf_op jit(solution)/shard_map/ppermute | solution.py:598
  20.9 21.1 %collective-permute-start.7 = (f32[17,4,16,128]{3,2,1,0:T(8,128)S(1)}, f32[17,4,16,128]{3,2,1,0:T(8,128)S(1)}, u32[]{:S(2)}, u32[]{:S(2)}) collective-permute-start(f32[17,4,16,128]{3,2,1,0:T(8,128)S(1)} %get-tuple-element.40), channel_id=1, source_target_pairs={{1,2},{3,4},{5,6},{7,8},{9,10},{11,12},{13,14},{15,16},{17,18},{19... | collective-permute-start | bytes 1671176 | tf_op jit(solution)/shard_map/ppermute | solution.py:597
  21.6 3.7 %collective-permute-start.2 = (f32[16,128]{1,0:T(8,128)S(1)}, f32[16,128]{1,0:T(8,128)S(1)}, u32[]{:S(2)}, u32[]{:S(2)}) collective-permute-start(f32[16,128]{1,0:T(8,128)S(1)} %get-tuple-element.38), channel_id=1, source_target_pairs={{0,1},{1,0},{2,3},{3,2},{4,5},{5,4},{6,7},{7,6},{8,9},{9,8},{10,11... | collective-permute-start | bytes 24584 | tf_op jit(solution)/shard_map/ppermute | solution.py:546
  25.3 6.9 %collective-permute-start.5 = (f32[16,128]{1,0:T(8,128)S(1)}, f32[16,128]{1,0:T(8,128)S(1)}, u32[]{:S(2)}, u32[]{:S(2)}) collective-permute-start(f32[16,128]{1,0:T(8,128)S(1)} %add.64), channel_id=1, source_target_pairs={{0,6},{1,7},{2,0},{3,1},{4,2},{5,3},{6,4},{7,5},{8,14},{9,15},{10,... | collective-permute-start | bytes 24584 | tf_op jit(solution)/shard_map/ppermute | solution.py:546
  29.7 5.3 %collective-permute-start.4 = (f32[16,128]{1,0:T(8,128)S(1)}, f32[16,128]{1,0:T(8,128)S(1)}, u32[]{:S(2)}, u32[]{:S(2)}) collective-permute-start(f32[16,128]{1,0:T(8,128)S(1)} %add.64), channel_id=1, source_target_pairs={{0,4},{1,5},{2,6},{3,7},{4,0},{5,1},{6,2},{7,3},{8,12},{9,13},{10,... | collective-permute-start | bytes 24584 | tf_op jit(solution)/shard_map/ppermute | solution.py:546
  29.8 5.2 %collective-permute-start.3 = (f32[16,128]{1,0:T(8,128)S(1)}, f32[16,128]{1,0:T(8,128)S(1)}, u32[]{:S(2)}, u32[]{:S(2)}) collective-permute-start(f32[16,128]{1,0:T(8,128)S(1)} %add.64), channel_id=1, source_target_pairs={{0,2},{1,3},{2,4},{3,5},{4,6},{5,7},{6,0},{7,1},{8,10},{9,11},{10,... | collective-permute-start | bytes 24584 | tf_op jit(solution)/shard_map/ppermute | solution.py:546
  35.0 10.9 %collective-permute-start.10 = (f32[16,128]{1,0:T(8,128)S(1)}, f32[16,128]{1,0:T(8,128)S(1)}, u32[]{:S(2)}, u32[]{:S(2)}) collective-permute-start(f32[16,128]{1,0:T(8,128)S(1)} %add_add_fusion.5), channel_id=1, source_target_pairs={{0,24},{1,25},{2,26},{3,27},{4,28},{5,29},{6,30},{7,31},{8,0},{9,1... | collective-permute-start | bytes 24584 | tf_op jit(solution)/shard_map/ppermute | solution.py:546
  41.0 5.2 %collective-permute-start.9 = (f32[16,128]{1,0:T(8,128)S(1)}, f32[16,128]{1,0:T(8,128)S(1)}, u32[]{:S(2)}, u32[]{:S(2)}) collective-permute-start(f32[16,128]{1,0:T(8,128)S(1)} %add_add_fusion.5), channel_id=1, source_target_pairs={{0,16},{1,17},{2,18},{3,19},{4,20},{5,21},{6,22},{7,23},{8,24},{9,... | collective-permute-start | bytes 24584 | tf_op jit(solution)/shard_map/ppermute | solution.py:546
  41.0 5.2 %collective-permute-start.8 = (f32[16,128]{1,0:T(8,128)S(1)}, f32[16,128]{1,0:T(8,128)S(1)}, u32[]{:S(2)}, u32[]{:S(2)}) collective-permute-start(f32[16,128]{1,0:T(8,128)S(1)} %add_add_fusion.5), channel_id=1, source_target_pairs={{0,8},{1,9},{2,10},{3,11},{4,12},{5,13},{6,14},{7,15},{8,16},{9,17... | collective-permute-start | bytes 24584 | tf_op jit(solution)/shard_map/ppermute | solution.py:546
  46.2 4.8 %collective-permute-start.13 = (f32[16,128]{1,0:T(8,128)S(1)}, f32[16,128]{1,0:T(8,128)S(1)}, u32[]{:S(2)}, u32[]{:S(2)}) collective-permute-start(f32[16,128]{1,0:T(8,128)S(1)} %add_add_fusion.4), channel_id=1, source_target_pairs={{0,96},{1,97},{2,98},{3,99},{4,100},{5,101},{6,102},{7,103},{8,104... | collective-permute-start | bytes 24584 | tf_op jit(solution)/shard_map/ppermute | solution.py:546
  49.6 5.2 %collective-permute-start.12 = (f32[16,128]{1,0:T(8,128)S(1)}, f32[16,128]{1,0:T(8,128)S(1)}, u32[]{:S(2)}, u32[]{:S(2)}) collective-permute-start(f32[16,128]{1,0:T(8,128)S(1)} %add_add_fusion.4), channel_id=1, source_target_pairs={{0,64},{1,65},{2,66},{3,67},{4,68},{5,69},{6,70},{7,71},{8,72},{9,... | collective-permute-start | bytes 24584 | tf_op jit(solution)/shard_map/ppermute | solution.py:546
  50.0 4.9 %collective-permute-start.11 = (f32[16,128]{1,0:T(8,128)S(1)}, f32[16,128]{1,0:T(8,128)S(1)}, u32[]{:S(2)}, u32[]{:S(2)}) collective-permute-start(f32[16,128]{1,0:T(8,128)S(1)} %add_add_fusion.4), channel_id=1, source_target_pairs={{0,32},{1,33},{2,34},{3,35},{4,36},{5,37},{6,38},{7,39},{8,40},{9,... | collective-permute-start | bytes 24584 | tf_op jit(solution)/shard_map/ppermute | solution.py:546
  70.2 1.3 %collective-permute-start.14 = (f32[16,128]{1,0:T(8,128)S(1)}, f32[16,128]{1,0:T(8,128)S(1)}, u32[]{:S(2)}, u32[]{:S(2)}) collective-permute-start(f32[16,128]{1,0:T(8,128)S(1)} %get-tuple-element.49), channel_id=1, source_target_pairs={{0,1},{1,0},{2,3},{3,2},{4,5},{5,4},{6,7},{7,6},{8,9},{9,8},{10,11... | collective-permute-start | bytes 24584 | tf_op jit(solution)/shard_map/ppermute | solution.py:546
  71.5 4.9 %collective-permute-start.17 = (f32[16,128]{1,0:T(8,128)S(1)}, f32[16,128]{1,0:T(8,128)S(1)}, u32[]{:S(2)}, u32[]{:S(2)}) collective-permute-start(f32[16,128]{1,0:T(8,128)S(1)} %add.74), channel_id=1, source_target_pairs={{0,6},{1,7},{2,0},{3,1},{4,2},{5,3},{6,4},{7,5},{8,14},{9,15},{10,... | collective-permute-start | bytes 24584 | tf_op jit(solution)/shard_map/ppermute | solution.py:546
  75.1 5.2 %collective-permute-start.16 = (f32[16,128]{1,0:T(8,128)S(1)}, f32[16,128]{1,0:T(8,128)S(1)}, u32[]{:S(2)}, u32[]{:S(2)}) collective-permute-start(f32[16,128]{1,0:T(8,128)S(1)} %add.74), channel_id=1, source_target_pairs={{0,4},{1,5},{2,6},{3,7},{4,0},{5,1},{6,2},{7,3},{8,12},{9,13},{10,... | collective-permute-start | bytes 24584 | tf_op jit(solution)/shard_map/ppermute | solution.py:546
  75.1 5.2 %collective-permute-start.15 = (f32[16,128]{1,0:T(8,128)S(1)}, f32[16,128]{1,0:T(8,128)S(1)}, u32[]{:S(2)}, u32[]{:S(2)}) collective-permute-start(f32[16,128]{1,0:T(8,128)S(1)} %add.74), channel_id=1, source_target_pairs={{0,2},{1,3},{2,4},{3,5},{4,6},{5,7},{6,0},{7,1},{8,10},{9,11},{10,... | collective-permute-start | bytes 24584 | tf_op jit(solution)/shard_map/ppermute | solution.py:546
  80.2 5.4 %collective-permute-start.20 = (f32[16,128]{1,0:T(8,128)S(1)}, f32[16,128]{1,0:T(8,128)S(1)}, u32[]{:S(2)}, u32[]{:S(2)}) collective-permute-start(f32[16,128]{1,0:T(8,128)S(1)} %add_add_fusion.2), channel_id=1, source_target_pairs={{0,24},{1,25},{2,26},{3,27},{4,28},{5,29},{6,30},{7,31},{8,0},{9,1... | collective-permute-start | bytes 24584 | tf_op jit(solution)/shard_map/ppermute | solution.py:546
  82.7 5.2 %collective-permute-start.19 = (f32[16,128]{1,0:T(8,128)S(1)}, f32[16,128]{1,0:T(8,128)S(1)}, u32[]{:S(2)}, u32[]{:S(2)}) collective-permute-start(f32[16,128]{1,0:T(8,128)S(1)} %add_add_fusion.2), channel_id=1, source_target_pairs={{0,16},{1,17},{2,18},{3,19},{4,20},{5,21},{6,22},{7,23},{8,24},{9,... | collective-permute-start | bytes 24584 | tf_op jit(solution)/shard_map/ppermute | solution.py:546
  84.3 4.9 %collective-permute-start.18 = (f32[16,128]{1,0:T(8,128)S(1)}, f32[16,128]{1,0:T(8,128)S(1)}, u32[]{:S(2)}, u32[]{:S(2)}) collective-permute-start(f32[16,128]{1,0:T(8,128)S(1)} %add_add_fusion.2), channel_id=1, source_target_pairs={{0,8},{1,9},{2,10},{3,11},{4,12},{5,13},{6,14},{7,15},{8,16},{9,17... | collective-permute-start | bytes 24584 | tf_op jit(solution)/shard_map/ppermute | solution.py:546
  89.2 3.7 %collective-permute-start.23 = (f32[16,128]{1,0:T(8,128)S(1)}, f32[16,128]{1,0:T(8,128)S(1)}, u32[]{:S(2)}, u32[]{:S(2)}) collective-permute-start(f32[16,128]{1,0:T(8,128)S(1)} %add_add_fusion.1), channel_id=1, source_target_pairs={{0,96},{1,97},{2,98},{3,99},{4,100},{5,101},{6,102},{7,103},{8,104... | collective-permute-start | bytes 24584 | tf_op jit(solution)/shard_map/ppermute | solution.py:546
  89.7 5.2 %collective-permute-start.22 = (f32[16,128]{1,0:T(8,128)S(1)}, f32[16,128]{1,0:T(8,128)S(1)}, u32[]{:S(2)}, u32[]{:S(2)}) collective-permute-start(f32[16,128]{1,0:T(8,128)S(1)} %add_add_fusion.1), channel_id=1, source_target_pairs={{0,64},{1,65},{2,66},{3,67},{4,68},{5,69},{6,70},{7,71},{8,72},{9,... | collective-permute-start | bytes 24584 | tf_op jit(solution)/shard_map/ppermute | solution.py:546
  91.2 4.9 %collective-permute-start.21 = (f32[16,128]{1,0:T(8,128)S(1)}, f32[16,128]{1,0:T(8,128)S(1)}, u32[]{:S(2)}, u32[]{:S(2)}) collective-permute-start(f32[16,128]{1,0:T(8,128)S(1)} %add_add_fusion.1), channel_id=1, source_target_pairs={{0,32},{1,33},{2,34},{3,35},{4,36},{5,37},{6,38},{7,39},{8,40},{9,... | collective-permute-start | bytes 24584 | tf_op jit(solution)/shard_map/ppermute | solution.py:546

commit v4 on v3

--- a/solution.py
+++ b/solution.py
@@ -1,3 +1,5 @@
+import functools
+
 import jax
 import jax.numpy as jnp
 from jax import lax
@@ -14,6 +16,7 @@
 NZ = 128
 KB = SSTEP + 1
 PIECE = KB * NRHS
+ROUNDS = ((1, 2), (32, 4), (8, 4), (2, 4))
 MID = CX - 2 * SSTEP
 MIDDLE = CX + 2 * SSTEP
 AXES = ("grp", "dom")
@@ -276,18 +279,19 @@
 def load_halo(info, same, following, field_l, field_u, diags):
     even = info[1] % 2 == 0
 
-    def pick(at):
-        a, b = same[at, :], following[at, :]
-        return jnp.where(even, b, a), jnp.where(even, a, b)
-
-    for i in range(SSTEP):
-        for y in range(NY):
-            low, high = pick(pl.Slice(i * NY + y, NRHS, SSTEP * NY))
-            field_l[i, y] = low
-            field_u[SSTEP - 1 - i, y] = high
-        low, high = pick(pl.ds((NRHS * SSTEP + i) * NY, NY))
-        diags[i] = low
-        diags[SSTEP + i] = high
+    def pick(at, top):
+        return jnp.where(even, same[at, :], following[at, :]) if top else jnp.where(
+            even, following[at, :], same[at, :]
+        )
+
+    for top, field in ((False, field_l), (True, field_u)):
+        if field is None:
+            continue
+        for i in range(SSTEP):
+            for y in range(NY):
+                at = pl.Slice(i * NY + y, NRHS, SSTEP * NY)
+                field[SSTEP - 1 - i if top else i, y] = pick(at, top)
+            diags[i + SSTEP if top else i] = pick(pl.ds((NRHS * SSTEP + i) * NY, NY), top)
 
 
 def edge_kernel(
@@ -336,60 +340,61 @@
                     source(power - 1, q - 1), source(power - 1, q), source(power - 1, q + 1),
                     coef, outside if q < 0 else 1.0 / SCALE, emit,
                 )
+                if top and power == SSTEP and q:
+                    acc = moment_sum(panel, slot(q - 1), acc)
             if top:
                 acc = moment_sum(panel, power - 1, acc)
-    for q in range(SSTEP):
-        acc = moment_sum(panel, CX - 1 - q, acc)
+    acc = moment_sum(panel, CX - SSTEP, acc)
     mom[...] = mom_in[...] + moment_blocks(acc)
 
 
-def ghost_kernel(
-    info, same, following, diag, diags, side_l, side_u, panel, coef, far_l, far_u, far_b, far_diags
-):
-    count = info[0]
-    for i in range(MIDDLE - CX):
-        coef[CX + i] = jnp.zeros((NY, NZ), F32)
-    for i in range(CX):
-        coef[SSTEP + i] = coef_of(diag[i])
-    for i in range(SSTEP):
-        coef[i] = coef_of(diags[i])
-        coef[SSTEP + count + i] = coef_of(diags[SSTEP + i])
-    load_halo(info, same, following, far_l, far_u, far_diags)
-    for top in (False, True):
-        side, far_a = (side_u, far_u) if top else (side_l, far_l)
-        weight = jnp.where(info[2 if top else 1] > 0, 1.0 / SCALE, 0.0).astype(F32)
-        shift = SSTEP if top else 0
-        buffers = (far_a, far_b)
-        for power in range(SSTEP + 1):
-            for q in range(power - SSTEP, 0):
-                split_plane(panel, q + SSTEP + shift, power, side.at[power], q - (power - SSTEP))
-            if power == 0:
-                continue
-            src, dst = buffers[(power - 1) % 2], buffers[power % 2]
-
-            def source(q):
-                if q <= power - 6:
-                    return src, q - (power - 9)
-                return side.at[power - 1], q - (power - 5)
-
-            for q in range(power - 8, power - 4):
-
-                def diag_row(y):
-                    if q >= -SSTEP:
-                        return coef_of(diags[SSTEP - 1 - q if top else q + SSTEP, pl.ds(y, 1), :])
-                    return coef_of(far_diags[-1 - q if top else q + 2 * SSTEP, pl.ds(y, 1), :])
-
-                def emit(y, value):
-                    if power < SSTEP:
-                        dst[q - (power - 8), y] = value
-                    if q >= -SSTEP:
-                        store_pieces(panel, q + SSTEP + shift, y, power, value)
-
-                plane_step(source(q - 1), source(q), source(q + 1), diag_row, weight, emit)
+def ghost_kernel(top, info, same, following, diag, diags, side, panel, *rest):
+    far_a, far_b, far_diags = rest[-3:]
+    if not top:
+        coef_out, count = rest[0], info[0]
+        for i in range(MIDDLE - CX):
+            coef_out[CX + i] = jnp.zeros((NY, NZ), F32)
+        for i in range(CX):
+            coef_out[SSTEP + i] = coef_of(diag[i])
+        for i in range(SSTEP):
+            coef_out[i] = coef_of(diags[i])
+            coef_out[SSTEP + count + i] = coef_of(diags[SSTEP + i])
+    if top:
+        load_halo(info, same, following, None, far_a, far_diags)
+    else:
+        load_halo(info, same, following, far_a, None, far_diags)
+    weight = jnp.where(info[2 if top else 1] > 0, 1.0 / SCALE, 0.0).astype(F32)
+    buffers = (far_a, far_b)
+    for power in range(SSTEP + 1):
+        for q in range(power - SSTEP, 0):
+            split_plane(panel, q + SSTEP, power, side.at[power], q - (power - SSTEP))
+        if power == 0:
+            continue
+        src, dst = buffers[(power - 1) % 2], buffers[power % 2]
+
+        def source(q):
+            if q <= power - 6:
+                return src, q - (power - 9)
+            return side.at[power - 1], q - (power - 5)
+
+        for q in range(power - 8, power - 4):
+
+            def diag_row(y):
+                if q >= -SSTEP:
+                    return coef_of(diags[SSTEP - 1 - q if top else q + SSTEP, pl.ds(y, 1), :])
+                return coef_of(far_diags[-1 - q if top else q + 2 * SSTEP, pl.ds(y, 1), :])
+
+            def emit(y, value):
+                if power < SSTEP:
+                    dst[q - (power - 8), y] = value
+                if q >= -SSTEP:
+                    store_pieces(panel, q + SSTEP, y, power, value)
+
+            plane_step(source(q - 1), source(q), source(q + 1), diag_row, weight, emit)
 
 
 def middle_kernel(
-    info, mom_in, coef, panel_in, ghost, panel, mom, iterate, field_0, field_1, field_2, field_3
+    info, mom_in, coef, panel_in, ghost_l, ghost_u, panel, mom, iterate, field_0, field_1, field_2, field_3
 ):
     count = info[0]
     coefs = coef_rows(solve(mom_in[...]))
@@ -414,10 +419,14 @@
         field_0[CX + i] = jnp.zeros(FIELD, F32)
     for i in range(SSTEP):
         iterate[CX - SSTEP + i] = jnp.zeros(FIELD, F32)
-    over(0, SSTEP, lambda p: update(ghost, p, p, False))
-    over(0, CX - SSTEP, lambda p: update(panel_in, p, p + SSTEP, True))
-    over(0, SSTEP, lambda p: update(panel_in, CX - SSTEP + p, count + p, True))
-    over(0, SSTEP, lambda p: update(ghost, 2 * SSTEP - 1 - p, count + SSTEP + p, False))
+    for p in range(SSTEP):
+        update(ghost_l, p, p, False)
+    for p in range(CX - SSTEP):
+        update(panel_in, p, p + SSTEP, True)
+    for p in range(SSTEP):
+        update(panel_in, CX - SSTEP + p, count + p, True)
+    for p in range(SSTEP):
+        update(ghost_u, SSTEP - 1 - p, count + SSTEP + p, False)
     fields = (field_0, field_1, field_2, field_3)
 
     def keep_of(p):
@@ -529,15 +538,16 @@
     )(*operands)
 
 
-def reduce_all(value, size, beside=None):
+def reduce_all(value, size, beside=()):
     if size == 128:
-        rounds = [(1, 2), (2, 4), (8, 4), (32, 4)]
+        rounds = ROUNDS
     else:
         rounds = [(1 << b, 2) for b in range(size.bit_length() - 1)]
-    for place_in_order, (stride, width) in enumerate(rounds):
+    beside = list(beside)
+    for order, (stride, width) in enumerate(rounds):
         total = value
-        if beside is not None and place_in_order == 2:
-            total, beside = lax.optimization_barrier((total, beside))
+        if 2 <= order < 2 + len(beside):
+            total, beside[order - 2] = lax.optimization_barrier((total, beside[order - 2]))
         for turn in range(1, width):
             route = []
             for i in range(size):
@@ -596,27 +606,29 @@
     mom, far_next, far_same = lax.optimization_barrier((mom, far_next, far_same))
     far_next = lax.ppermute(far_next, AXES, following).reshape(halo)
     far_same = lax.ppermute(far_same, AXES, same).reshape(halo)
-    ghost, coef = call(
-        ghost_kernel,
-        8,
-        (info, far_same, far_next, diagonal, diags, side_l, side_u),
-        [((2 * SSTEP,) + PANEL, BF16, True), ((MIDDLE, NY, NZ), F32, True)],
-        [pltpu.VMEM((SSTEP,) + FIELD, F32)] * 3 + [pltpu.VMEM((2 * SSTEP, NY, NZ), F32)],
-        (4, 5, 6),
-        cost=3,
-    )
-    mom, coef = reduce_all(mom, size, coef)
+    ghosts = []
+    for top, side in ((False, side_l), (True, side_u)):
+        ghosts.append(call(
+            functools.partial(ghost_kernel, top),
+            8,
+            (info, far_same, far_next, diagonal, diags, side),
+            [((SSTEP,) + PANEL, BF16, True)] + [((MIDDLE, NY, NZ), F32, True)] * (not top),
+            [pltpu.VMEM((SSTEP,) + FIELD, F32)] * 2 + [pltpu.VMEM((2 * SSTEP, NY, NZ), F32)],
+            (4, 5),
+            cost=2,
+        ))
+    mom, ((ghost_l, coef), (ghost_u,)) = reduce_all(mom, size, ghosts)
     panel, mom, iterate = call(
         middle_kernel,
         16,
-        (info, mom, coef, panel, ghost),
+        (info, mom, coef, panel, ghost_l, ghost_u),
         [
             panel_shape,
             ((NRHS, NZ), F32, False),
             ((CX,) + FIELD, F32, True),
         ],
         [pltpu.VMEM((MIDDLE,) + FIELD, F32)] * SSTEP,
-        (2, 3, 4),
+        (2, 3, 4, 5),
         cost=10,
         aliases={3: 0},
     )

time: 104 us -> 103 us (level)
  starting transfers between devices: 38.3 us -> 35.2 us
    ppermute x20, starting transfers between devices: 33.8 us -> 30.7 us  [reduce_all(): total = total + lax.ppermute(value, AXES, route)]
    pallas_call x6 -> x7, Pallas kernels: 42.9 us -> 43.8 us  [call(): pl.pallas_call(body, out_shape=[pltpu.VMEM(s, d) if kept else jax.ShapeDt...]
  transfers between devices with their start and end apart: 24 -> 24, of which waited for: 15 -> 16; matrix products, arithmetic and copies ran while one was open for 0% -> 0% of each run, Pallas kernels for 12% -> 13%
where the time goes in v4:
time: 103 us; the launch traced here: 102 us
  Pallas kernels  43.8 us (43%)
  starting transfers between devices  35.2 us (34%)
  waiting for transfers between devices  21.6 us (21%)
  between operations  1.78 us (2%)
    pallas_call x7, Pallas kernels, call(): pl.pallas_call(body, out_shape=[pltpu.VMEM(s, d) if kept else jax.ShapeDt...  43.8 us
    ppermute x20, starting transfers between devices, reduce_all(): total = total + lax.ppermute(value, AXES, route)  30.7 us
    ppermute x20, waiting for transfers between devices, reduce_all(): total = total + lax.ppermute(value, AXES, route)  21.6 us
    ppermute x1, starting transfers between devices, local(): far_same = lax.ppermute(far_same, AXES, same).reshape(halo)  2.98 us
  transfers between devices with their start and end apart: 24, of which 16 were waited for; matrix products, arithmetic and copies ran while one was open for 0% of the time, Pallas kernels for 13%

profile of v4, /device:TPU:0, one launch (start us, length us, event | category | flops | bytes accessed | tf_op | source)
XLA Modules:
  0.0 102.5 jit_solution(2555891200858079549)
XLA Ops:
  0.6 0.0 copy-start
  0.6 0.0 copy-start.1
  1.5 0.1 pad_add_fusion.info
  1.5 2.2 %shard_map.50 = (f32[17,4,16,128]{3,2,1,0:T(8,128)S(1)}, f32[17,4,16,128]{3,2,1,0:T(8,128)S(1)}, f32[17,4,16,128]{3,2,1,0:T(8,128)S(1)}, f32[17,4,16,128]{3,2,1,0:T(8,128)S(1)}) custom-call(s32[3]{0:T(128)S(1)} %pad_add_fusion.info, f32[16,16,16,128]{3,2,1,0:T(8,128)} %right.1, f32[16,16,128]{2,1,0:T(8,128)} %diag.9), custom_call_target="tpu_custom_call" | custom-call | flops 1000000000 | bytes 3000000 | tf_op jit(solution)/shard_map/pallas_call | solution.py:526
  3.7 0.1 collective-permute-start
  3.8 0.7 collective-permute-start.1
  4.5 0.0 copy-done
  4.5 0.0 copy-done.1
  4.5 8.1 %shard_map.51 = (bf16[16,16,240,128]{3,2,1,0:T(8,128)(2,1)S(1)}, f32[16,128]{1,0:T(8,128)S(1)}, f32[16,16,16,128]{3,2,1,0:T(8,128)S(1)}, f32[16,16,16,128]{3,2,1...) custom-call(s32[3]{0:T(128)S(1)} %pad_add_fusion.info, f32[4096,128]{1,0:T(8,128)S(1)} %bitcast.9, ...), custom_call_target="tpu_custom_call" | custom-call | flops 4000000000 | bytes 12000000 | tf_op jit(solution)/shard_map/pallas_call | solution.py:526
  12.7 0.0 collective-permute-done
  12.7 0.0 collective-permute-done.1
  12.7 5.5 %shard_map.52 = (bf16[16,16,240,128]{3,2,1,0:T(8,128)(2,1)S(1)}, f32[16,128]{1,0:T(8,128)S(1)}, f32[4,4,16,16,128]{4,3,2,1,0:T(8,128)S(1)}, f32[4,4,16,16,128]{4,3,2,1,0:T(8,128)S(1)}, f32[8,16,128]{2,1,0:T(8,128)S(1)}) custom-call(s32[3]{0:T(128)S(1)} %pad_add_fusion.info, f32[1088,128]{1,0:T(8,128)S(1)} %bitcast.7, ...), custom_call_target="tpu_custom_call", output_to_operand_aliasing={{0}: (9, {})} | custom-call | flops 4000000000 | bytes 12000000 | tf_op jit(solution)/shard_map/pallas_call | solution.py:526
  18.2 3.0 %collective-permute-start.6 = (f32[17,4,16,128]{3,2,1,0:T(8,128)S(1)}, f32[17,4,16,128]{3,2,1,0:T(8,128)S(1)}, u32[]{:S(2)}, u32[]{:S(2)}) collective-permute-start(f32[17,4,16,128]{3,2,1,0:T(8,128)S(1)} %get-tuple-element.42), channel_id=1, source_target_pairs={{0,1},{1,0},{2,3},{3,2},{4,5},{5,4},{6,7},{7,6},{8,9},{9,8},{10,11... | collective-permute-start | bytes 1671176 | tf_op jit(solution)/shard_map/ppermute | solution.py:608
  21.2 0.7 collective-permute-start.7
  21.9 2.9 %collective-permute-start.2 = (f32[16,128]{1,0:T(8,128)S(1)}, f32[16,128]{1,0:T(8,128)S(1)}, u32[]{:S(2)}, u32[]{:S(2)}) collective-permute-start(f32[16,128]{1,0:T(8,128)S(1)} %get-tuple-element.41), channel_id=1, source_target_pairs={{0,1},{1,0},{2,3},{3,2},{4,5},{5,4},{6,7},{7,6},{8,9},{9,8},{10,11... | collective-permute-start | bytes 24584 | tf_op jit(solution)/shard_map/ppermute | solution.py:556
  24.8 0.8 collective-permute-done.2
  25.6 11.7 %collective-permute-start.5 = (f32[16,128]{1,0:T(8,128)S(1)}, f32[16,128]{1,0:T(8,128)S(1)}, u32[]{:S(2)}, u32[]{:S(2)}) collective-permute-start(f32[16,128]{1,0:T(8,128)S(1)} %add.64), channel_id=1, source_target_pairs={{0,96},{1,97},{2,98},{3,99},{4,100},{5,101},{6,102},{7,103},{8,104... | collective-permute-start | bytes 24584 | tf_op jit(solution)/shard_map/ppermute | solution.py:556
  37.3 0.3 collective-permute-start.4
  37.6 1.0 collective-permute-start.3
  38.6 0.1 collective-permute-done.5
  38.7 3.8 %collective-permute-done.4 = f32[16,128]{1,0:T(8,128)S(1)} collective-permute-done((f32[16,128]{1,0:T(8,128)S(1)}, f32[16,128]{1,0:T(8,128)S(1)}, u32[]{:S(2)}, u32[]{:S(2)}) %collective-permute-start.4) | collective-permute-done | bytes 8224 | tf_op jit(solution)/shard_map/ppermute | solution.py:556
  42.5 0.1 collective-permute-done.3
  42.5 2.0 %collective-permute-start.10 = (f32[16,128]{1,0:T(8,128)S(1)}, f32[16,128]{1,0:T(8,128)S(1)}, u32[]{:S(2)}, u32[]{:S(2)}) collective-permute-start(f32[16,128]{1,0:T(8,128)S(1)} %add_add_fusion.5), channel_id=1, source_target_pairs={{0,24},{1,25},{2,26},{3,27},{4,28},{5,29},{6,30},{7,31},{8,0},{9,1... | collective-permute-start | bytes 24584 | tf_op jit(solution)/shard_map/ppermute | solution.py:556
  44.5 0.0 collective-permute-start.9
  44.5 0.9 collective-permute-start.8
  45.5 0.0 collective-permute-done.6
  45.5 0.0 collective-permute-done.7
  45.5 2.5 %shard_map.53 = (bf16[4,16,240,128]{3,2,1,0:T(8,128)(2,1)S(1)}, f32[24,16,128]{2,1,0:T(8,128)S(1)}) custom-call(s32[3]{0:T(128)S(1)} %pad_add_fusion.info, f32[1088,128]{1,0:T(8,128)S(1)} %bitcast.10, f32[1088,128]{1,0:T(8,128)S(1)} %bitcast.12, f32[16,16,128]{2,1,0:T(8,128)S(1)} %copy-done, f32[8,16,128]{2,1,0:T(8,128)S(1)} %get-tuple-element.44.diags, ...), custom_call_target="tpu_custom_call" | custom-call | flops 2000000000 | bytes 6000000 | tf_op jit(solution)/shard_map/pallas_call | solution.py:526
  48.0 0.0 collective-permute-done.10
  48.0 1.7 %collective-permute-done.9 = f32[16,128]{1,0:T(8,128)S(1)} collective-permute-done((f32[16,128]{1,0:T(8,128)S(1)}, f32[16,128]{1,0:T(8,128)S(1)}, u32[]{:S(2)}, u32[]{:S(2)}) %collective-permute-start.9) | collective-permute-done | bytes 8224 | tf_op jit(solution)/shard_map/ppermute | solution.py:556
  49.7 0.0 collective-permute-done.8
  49.7 0.1 collective-permute-start.13
  49.8 0.3 collective-permute-start.12
  50.1 1.7 %collective-permute-start.11 = (f32[16,128]{1,0:T(8,128)S(1)}, f32[16,128]{1,0:T(8,128)S(1)}, u32[]{:S(2)}, u32[]{:S(2)}) collective-permute-start(f32[16,128]{1,0:T(8,128)S(1)} %add_add_fusion.4), channel_id=1, source_target_pairs={{0,2},{1,3},{2,4},{3,5},{4,6},{5,7},{6,0},{7,1},{8,10},{9,11},{10,... | collective-permute-start | bytes 24584 | tf_op jit(solution)/shard_map/ppermute | solution.py:556
  51.8 2.5 %shard_map.54.ghost_u = bf16[4,16,240,128]{3,2,1,0:T(8,128)(2,1)S(1)} custom-call(s32[3]{0:T(128)S(1)} %pad_add_fusion.info, f32[1088,128]{1,0:T(8,128)S(1)} %bitcast.11, f32[1088,128]{1,0:T(8,128)S(1)} %bitcast.13, f32[16,16,128]{2,1,0:T(8,128)S(1)} %copy-done, f32[8,16,128]{2,1,0:T(8,128)S(1)} %get-tuple-element.44.diags, ...), custom_call_target="tpu_custom_call" | custom-call | flops 2000000000 | bytes 6000000 | tf_op jit(solution)/shard_map/pallas_call | solution.py:526
  54.3 0.0 collective-permute-done.13
  54.3 0.7 collective-permute-done.12
  55.0 1.1 %collective-permute-done.11 = f32[16,128]{1,0:T(8,128)S(1)} collective-permute-done((f32[16,128]{1,0:T(8,128)S(1)}, f32[16,128]{1,0:T(8,128)S(1)}, u32[]{:S(2)}, u32[]{:S(2)}) %collective-permute-start.11) | collective-permute-done | bytes 8224 | tf_op jit(solution)/shard_map/ppermute | solution.py:556
  56.1 14.9 %shard_map.55 = (bf16[16,16,240,128]{3,2,1,0:T(8,128)(2,1)S(1)}, f32[16,128]{1,0:T(8,128)S(1)}, f32[16,16,16,128]{3,2,1,0:T(8,128)S(1)}) custom-call(s32[3]{0:T(128)S(1)} %pad_add_fusion.info, f32[16,128]{1,0:T(8,128)S(1)} %add_add_fusion.3.mom_in, f32[24,16,128]{2,1,0:T(8,128)S(1)} %get-tuple-element.51.coef, ...), custom_call_target="tpu_custom_call", output_to_operand_aliasing={{0}: (3, {})} | custom-call | flops 10000000000 | bytes 30000000 | tf_op jit(solution)/shard_map/pallas_call | solution.py:526
  71.0 0.1 collective-permute-start.14
  71.1 1.2 %collective-permute-done.14 = f32[16,128]{1,0:T(8,128)S(1)} collective-permute-done((f32[16,128]{1,0:T(8,128)S(1)}, f32[16,128]{1,0:T(8,128)S(1)}, u32[]{:S(2)}, u32[]{:S(2)}) %collective-permute-start.14) | collective-permute-done | bytes 8224 | tf_op jit(solution)/shard_map/ppermute | solution.py:556
  72.3 0.6 collective-permute-start.17
  72.9 0.5 collective-permute-start.16
  73.3 1.4 %collective-permute-start.15 = (f32[16,128]{1,0:T(8,128)S(1)}, f32[16,128]{1,0:T(8,128)S(1)}, u32[]{:S(2)}, u32[]{:S(2)}) collective-permute-start(f32[16,128]{1,0:T(8,128)S(1)} %add.74), channel_id=1, source_target_pairs={{0,32},{1,33},{2,34},{3,35},{4,36},{5,37},{6,38},{7,39},{8,40},{9,... | collective-permute-start | bytes 24584 | tf_op jit(solution)/shard_map/ppermute | solution.py:556
  74.7 1.2 %collective-permute-done.17 = f32[16,128]{1,0:T(8,128)S(1)} collective-permute-done((f32[16,128]{1,0:T(8,128)S(1)}, f32[16,128]{1,0:T(8,128)S(1)}, u32[]{:S(2)}, u32[]{:S(2)}) %collective-permute-start.17) | collective-permute-done | bytes 8224 | tf_op jit(solution)/shard_map/ppermute | solution.py:556
  75.9 2.1 %collective-permute-done.16 = f32[16,128]{1,0:T(8,128)S(1)} collective-permute-done((f32[16,128]{1,0:T(8,128)S(1)}, f32[16,128]{1,0:T(8,128)S(1)}, u32[]{:S(2)}, u32[]{:S(2)}) %collective-permute-start.16) | collective-permute-done | bytes 8224 | tf_op jit(solution)/shard_map/ppermute | solution.py:556
  78.0 0.6 collective-permute-done.15
  78.6 1.6 %collective-permute-start.20 = (f32[16,128]{1,0:T(8,128)S(1)}, f32[16,128]{1,0:T(8,128)S(1)}, u32[]{:S(2)}, u32[]{:S(2)}) collective-permute-start(f32[16,128]{1,0:T(8,128)S(1)} %add_add_fusion.2), channel_id=1, source_target_pairs={{0,24},{1,25},{2,26},{3,27},{4,28},{5,29},{6,30},{7,31},{8,0},{9,1... | collective-permute-start | bytes 24584 | tf_op jit(solution)/shard_map/ppermute | solution.py:556
  80.2 1.4 %collective-permute-start.19 = (f32[16,128]{1,0:T(8,128)S(1)}, f32[16,128]{1,0:T(8,128)S(1)}, u32[]{:S(2)}, u32[]{:S(2)}) collective-permute-start(f32[16,128]{1,0:T(8,128)S(1)} %add_add_fusion.2), channel_id=1, source_target_pairs={{0,16},{1,17},{2,18},{3,19},{4,20},{5,21},{6,22},{7,23},{8,24},{9,... | collective-permute-start | bytes 24584 | tf_op jit(solution)/shard_map/ppermute | solution.py:556
  81.6 0.5 collective-permute-start.18
  82.1 0.2 collective-permute-done.20
  82.3 3.1 %collective-permute-done.19 = f32[16,128]{1,0:T(8,128)S(1)} collective-permute-done((f32[16,128]{1,0:T(8,128)S(1)}, f32[16,128]{1,0:T(8,128)S(1)}, u32[]{:S(2)}, u32[]{:S(2)}) %collective-permute-start.19) | collective-permute-done | bytes 8224 | tf_op jit(solution)/shard_map/ppermute | solution.py:556
  85.4 1.1 %collective-permute-done.18 = f32[16,128]{1,0:T(8,128)S(1)} collective-permute-done((f32[16,128]{1,0:T(8,128)S(1)}, f32[16,128]{1,0:T(8,128)S(1)}, u32[]{:S(2)}, u32[]{:S(2)}) %collective-permute-start.18) | collective-permute-done | bytes 8224 | tf_op jit(solution)/shard_map/ppermute | solution.py:556
  86.4 2.0 %collective-permute-start.23 = (f32[16,128]{1,0:T(8,128)S(1)}, f32[16,128]{1,0:T(8,128)S(1)}, u32[]{:S(2)}, u32[]{:S(2)}) collective-permute-start(f32[16,128]{1,0:T(8,128)S(1)} %add_add_fusion.1), channel_id=1, source_target_pairs={{0,6},{1,7},{2,0},{3,1},{4,2},{5,3},{6,4},{7,5},{8,14},{9,15},{10,... | collective-permute-start | bytes 24584 | tf_op jit(solution)/shard_map/ppermute | solution.py:556
  88.5 0.9 collective-permute-start.22
  89.4 0.9 collective-permute-start.21
  90.2 0.0 collective-permute-done.23
  90.2 3.4 %collective-permute-done.22 = f32[16,128]{1,0:T(8,128)S(1)} collective-permute-done((f32[16,128]{1,0:T(8,128)S(1)}, f32[16,128]{1,0:T(8,128)S(1)}, u32[]{:S(2)}, u32[]{:S(2)}) %collective-permute-start.22) | collective-permute-done | bytes 8224 | tf_op jit(solution)/shard_map/ppermute | solution.py:556
  93.6 0.6 collective-permute-done.21
  94.2 8.1 %shard_map.56 = (f32[16,16,16,128]{3,2,1,0:T(8,128)}, f32[16,16,16,128]{3,2,1,0:T(8,128)}) custom-call(s32[3]{0:T(128)S(1)} %pad_add_fusion.info, f32[16,128]{1,0:T(8,128)S(1)} %add_add_fusion.mom_in, bf16[16,16,240,128]{3,2,1,0:T(8,128)(2,1)S(1)} %get-tuple-element.56.panel, f32[16,16,16,128]{3,2,1,0:T(8,128)S(1)} %get-tuple-element.57.iterate), custom_call_target="tpu_custom_call" | custom-call | flops 4000000000 | bytes 12000000 | tf_op jit(solution)/shard_map/pallas_call | solution.py:526
  (8 shorter events, 0.0 us)
Async XLA Ops:
  0.6 3.9 %copy-start = (f32[16,16,128]{2,1,0:T(8,128)S(1)}, f32[16,16,128]{2,1,0:T(8,128)}, u32[]{:S(2)}) copy-start(f32[16,16,128]{2,1,0:T(8,128)} %diag.9) | copy-start | bytes 393220
  0.6 3.9 %copy-start.1 = (f32[16,16,16,128]{3,2,1,0:T(8,128)S(1)}, f32[16,16,16,128]{3,2,1,0:T(8,128)}, u32[]{:S(2)}) copy-start(f32[16,16,16,128]{3,2,1,0:T(8,128)} %right.1) | copy-start | bytes 6291460
  3.7 8.9 %collective-permute-start = (f32[17,4,16,128]{3,2,1,0:T(8,128)S(1)}, f32[17,4,16,128]{3,2,1,0:T(8,128)S(1)}, u32[]{:S(2)}, u32[]{:S(2)}) collective-permute-start(f32[17,4,16,128]{3,2,1,0:T(8,128)S(1)} %get-tuple-element.30), channel_id=1, source_target_pairs={{0,1},{1,0},{2,3},{3,2},{4,5},{5,4},{6,7},{7,6},{8,9},{9,8},{10,11... | collective-permute-start | bytes 1671176 | tf_op jit(solution)/shard_map/ppermute | solution.py:581
  3.8 8.9 %collective-permute-start.1 = (f32[17,4,16,128]{3,2,1,0:T(8,128)S(1)}, f32[17,4,16,128]{3,2,1,0:T(8,128)S(1)}, u32[]{:S(2)}, u32[]{:S(2)}) collective-permute-start(f32[17,4,16,128]{3,2,1,0:T(8,128)S(1)} %get-tuple-element.31), channel_id=1, source_target_pairs={{1,2},{3,4},{5,6},{7,8},{9,10},{11,12},{13,14},{15,16},{17,18},{19... | collective-permute-start | bytes 1671176 | tf_op jit(solution)/shard_map/ppermute | solution.py:580
  18.2 27.3 %collective-permute-start.6 = (f32[17,4,16,128]{3,2,1,0:T(8,128)S(1)}, f32[17,4,16,128]{3,2,1,0:T(8,128)S(1)}, u32[]{:S(2)}, u32[]{:S(2)}) collective-permute-start(f32[17,4,16,128]{3,2,1,0:T(8,128)S(1)} %get-tuple-element.42), channel_id=1, source_target_pairs={{0,1},{1,0},{2,3},{3,2},{4,5},{5,4},{6,7},{7,6},{8,9},{9,8},{10,11... | collective-permute-start | bytes 1671176 | tf_op jit(solution)/shard_map/ppermute | solution.py:608
  21.2 24.3 %collective-permute-start.7 = (f32[17,4,16,128]{3,2,1,0:T(8,128)S(1)}, f32[17,4,16,128]{3,2,1,0:T(8,128)S(1)}, u32[]{:S(2)}, u32[]{:S(2)}) collective-permute-start(f32[17,4,16,128]{3,2,1,0:T(8,128)S(1)} %get-tuple-element.43), channel_id=1, source_target_pairs={{1,2},{3,4},{5,6},{7,8},{9,10},{11,12},{13,14},{15,16},{17,18},{19... | collective-permute-start | bytes 1671176 | tf_op jit(solution)/shard_map/ppermute | solution.py:607
  21.9 3.7 %collective-permute-start.2 = (f32[16,128]{1,0:T(8,128)S(1)}, f32[16,128]{1,0:T(8,128)S(1)}, u32[]{:S(2)}, u32[]{:S(2)}) collective-permute-start(f32[16,128]{1,0:T(8,128)S(1)} %get-tuple-element.41), channel_id=1, source_target_pairs={{0,1},{1,0},{2,3},{3,2},{4,5},{5,4},{6,7},{7,6},{8,9},{9,8},{10,11... | collective-permute-start | bytes 24584 | tf_op jit(solution)/shard_map/ppermute | solution.py:556
  25.6 13.1 %collective-permute-start.5 = (f32[16,128]{1,0:T(8,128)S(1)}, f32[16,128]{1,0:T(8,128)S(1)}, u32[]{:S(2)}, u32[]{:S(2)}) collective-permute-start(f32[16,128]{1,0:T(8,128)S(1)} %add.64), channel_id=1, source_target_pairs={{0,96},{1,97},{2,98},{3,99},{4,100},{5,101},{6,102},{7,103},{8,104... | collective-permute-start | bytes 24584 | tf_op jit(solution)/shard_map/ppermute | solution.py:556
  37.3 5.2 %collective-permute-start.4 = (f32[16,128]{1,0:T(8,128)S(1)}, f32[16,128]{1,0:T(8,128)S(1)}, u32[]{:S(2)}, u32[]{:S(2)}) collective-permute-start(f32[16,128]{1,0:T(8,128)S(1)} %add.64), channel_id=1, source_target_pairs={{0,64},{1,65},{2,66},{3,67},{4,68},{5,69},{6,70},{7,71},{8,72},{9,... | collective-permute-start | bytes 24584 | tf_op jit(solution)/shard_map/ppermute | solution.py:556
  37.6 4.9 %collective-permute-start.3 = (f32[16,128]{1,0:T(8,128)S(1)}, f32[16,128]{1,0:T(8,128)S(1)}, u32[]{:S(2)}, u32[]{:S(2)}) collective-permute-start(f32[16,128]{1,0:T(8,128)S(1)} %add.64), channel_id=1, source_target_pairs={{0,32},{1,33},{2,34},{3,35},{4,36},{5,37},{6,38},{7,39},{8,40},{9,... | collective-permute-start | bytes 24584 | tf_op jit(solution)/shard_map/ppermute | solution.py:556
  42.5 5.5 %collective-permute-start.10 = (f32[16,128]{1,0:T(8,128)S(1)}, f32[16,128]{1,0:T(8,128)S(1)}, u32[]{:S(2)}, u32[]{:S(2)}) collective-permute-start(f32[16,128]{1,0:T(8,128)S(1)} %add_add_fusion.5), channel_id=1, source_target_pairs={{0,24},{1,25},{2,26},{3,27},{4,28},{5,29},{6,30},{7,31},{8,0},{9,1... | collective-permute-start | bytes 24584 | tf_op jit(solution)/shard_map/ppermute | solution.py:556
  44.5 5.2 %collective-permute-start.9 = (f32[16,128]{1,0:T(8,128)S(1)}, f32[16,128]{1,0:T(8,128)S(1)}, u32[]{:S(2)}, u32[]{:S(2)}) collective-permute-start(f32[16,128]{1,0:T(8,128)S(1)} %add_add_fusion.5), channel_id=1, source_target_pairs={{0,16},{1,17},{2,18},{3,19},{4,20},{5,21},{6,22},{7,23},{8,24},{9,... | collective-permute-start | bytes 24584 | tf_op jit(solution)/shard_map/ppermute | solution.py:556
  44.5 5.2 %collective-permute-start.8 = (f32[16,128]{1,0:T(8,128)S(1)}, f32[16,128]{1,0:T(8,128)S(1)}, u32[]{:S(2)}, u32[]{:S(2)}) collective-permute-start(f32[16,128]{1,0:T(8,128)S(1)} %add_add_fusion.5), channel_id=1, source_target_pairs={{0,8},{1,9},{2,10},{3,11},{4,12},{5,13},{6,14},{7,15},{8,16},{9,17... | collective-permute-start | bytes 24584 | tf_op jit(solution)/shard_map/ppermute | solution.py:556
  49.7 4.6 %collective-permute-start.13 = (f32[16,128]{1,0:T(8,128)S(1)}, f32[16,128]{1,0:T(8,128)S(1)}, u32[]{:S(2)}, u32[]{:S(2)}) collective-permute-start(f32[16,128]{1,0:T(8,128)S(1)} %add_add_fusion.4), channel_id=1, source_target_pairs={{0,6},{1,7},{2,0},{3,1},{4,2},{5,3},{6,4},{7,5},{8,14},{9,15},{10,... | collective-permute-start | bytes 24584 | tf_op jit(solution)/shard_map/ppermute | solution.py:556
  49.8 5.2 %collective-permute-start.12 = (f32[16,128]{1,0:T(8,128)S(1)}, f32[16,128]{1,0:T(8,128)S(1)}, u32[]{:S(2)}, u32[]{:S(2)}) collective-permute-start(f32[16,128]{1,0:T(8,128)S(1)} %add_add_fusion.4), channel_id=1, source_target_pairs={{0,4},{1,5},{2,6},{3,7},{4,0},{5,1},{6,2},{7,3},{8,12},{9,13},{10,... | collective-permute-start | bytes 24584 | tf_op jit(solution)/shard_map/ppermute | solution.py:556
  50.1 6.0 %collective-permute-start.11 = (f32[16,128]{1,0:T(8,128)S(1)}, f32[16,128]{1,0:T(8,128)S(1)}, u32[]{:S(2)}, u32[]{:S(2)}) collective-permute-start(f32[16,128]{1,0:T(8,128)S(1)} %add_add_fusion.4), channel_id=1, source_target_pairs={{0,2},{1,3},{2,4},{3,5},{4,6},{5,7},{6,0},{7,1},{8,10},{9,11},{10,... | collective-permute-start | bytes 24584 | tf_op jit(solution)/shard_map/ppermute | solution.py:556
  71.0 1.3 %collective-permute-start.14 = (f32[16,128]{1,0:T(8,128)S(1)}, f32[16,128]{1,0:T(8,128)S(1)}, u32[]{:S(2)}, u32[]{:S(2)}) collective-permute-start(f32[16,128]{1,0:T(8,128)S(1)} %get-tuple-element.55), channel_id=1, source_target_pairs={{0,1},{1,0},{2,3},{3,2},{4,5},{5,4},{6,7},{7,6},{8,9},{9,8},{10,11... | collective-permute-start | bytes 24584 | tf_op jit(solution)/shard_map/ppermute | solution.py:556
  72.3 3.7 %collective-permute-start.17 = (f32[16,128]{1,0:T(8,128)S(1)}, f32[16,128]{1,0:T(8,128)S(1)}, u32[]{:S(2)}, u32[]{:S(2)}) collective-permute-start(f32[16,128]{1,0:T(8,128)S(1)} %add.74), channel_id=1, source_target_pairs={{0,96},{1,97},{2,98},{3,99},{4,100},{5,101},{6,102},{7,103},{8,104... | collective-permute-start | bytes 24584 | tf_op jit(solution)/shard_map/ppermute | solution.py:556
  72.9 5.2 %collective-permute-start.16 = (f32[16,128]{1,0:T(8,128)S(1)}, f32[16,128]{1,0:T(8,128)S(1)}, u32[]{:S(2)}, u32[]{:S(2)}) collective-permute-start(f32[16,128]{1,0:T(8,128)S(1)} %add.74), channel_id=1, source_target_pairs={{0,64},{1,65},{2,66},{3,67},{4,68},{5,69},{6,70},{7,71},{8,72},{9,... | collective-permute-start | bytes 24584 | tf_op jit(solution)/shard_map/ppermute | solution.py:556
  73.3 5.3 %collective-permute-start.15 = (f32[16,128]{1,0:T(8,128)S(1)}, f32[16,128]{1,0:T(8,128)S(1)}, u32[]{:S(2)}, u32[]{:S(2)}) collective-permute-start(f32[16,128]{1,0:T(8,128)S(1)} %add.74), channel_id=1, source_target_pairs={{0,32},{1,33},{2,34},{3,35},{4,36},{5,37},{6,38},{7,39},{8,40},{9,... | collective-permute-start | bytes 24584 | tf_op jit(solution)/shard_map/ppermute | solution.py:556
  78.6 3.7 %collective-permute-start.20 = (f32[16,128]{1,0:T(8,128)S(1)}, f32[16,128]{1,0:T(8,128)S(1)}, u32[]{:S(2)}, u32[]{:S(2)}) collective-permute-start(f32[16,128]{1,0:T(8,128)S(1)} %add_add_fusion.2), channel_id=1, source_target_pairs={{0,24},{1,25},{2,26},{3,27},{4,28},{5,29},{6,30},{7,31},{8,0},{9,1... | collective-permute-start | bytes 24584 | tf_op jit(solution)/shard_map/ppermute | solution.py:556
  80.2 5.2 %collective-permute-start.19 = (f32[16,128]{1,0:T(8,128)S(1)}, f32[16,128]{1,0:T(8,128)S(1)}, u32[]{:S(2)}, u32[]{:S(2)}) collective-permute-start(f32[16,128]{1,0:T(8,128)S(1)} %add_add_fusion.2), channel_id=1, source_target_pairs={{0,16},{1,17},{2,18},{3,19},{4,20},{5,21},{6,22},{7,23},{8,24},{9,... | collective-permute-start | bytes 24584 | tf_op jit(solution)/shard_map/ppermute | solution.py:556
  81.6 4.9 %collective-permute-start.18 = (f32[16,128]{1,0:T(8,128)S(1)}, f32[16,128]{1,0:T(8,128)S(1)}, u32[]{:S(2)}, u32[]{:S(2)}) collective-permute-start(f32[16,128]{1,0:T(8,128)S(1)} %add_add_fusion.2), channel_id=1, source_target_pairs={{0,8},{1,9},{2,10},{3,11},{4,12},{5,13},{6,14},{7,15},{8,16},{9,17... | collective-permute-start | bytes 24584 | tf_op jit(solution)/shard_map/ppermute | solution.py:556
  86.4 3.8 %collective-permute-start.23 = (f32[16,128]{1,0:T(8,128)S(1)}, f32[16,128]{1,0:T(8,128)S(1)}, u32[]{:S(2)}, u32[]{:S(2)}) collective-permute-start(f32[16,128]{1,0:T(8,128)S(1)} %add_add_fusion.1), channel_id=1, source_target_pairs={{0,6},{1,7},{2,0},{3,1},{4,2},{5,3},{6,4},{7,5},{8,14},{9,15},{10,... | collective-permute-start | bytes 24584 | tf_op jit(solution)/shard_map/ppermute | solution.py:556
  88.5 5.2 %collective-permute-start.22 = (f32[16,128]{1,0:T(8,128)S(1)}, f32[16,128]{1,0:T(8,128)S(1)}, u32[]{:S(2)}, u32[]{:S(2)}) collective-permute-start(f32[16,128]{1,0:T(8,128)S(1)} %add_add_fusion.1), channel_id=1, source_target_pairs={{0,4},{1,5},{2,6},{3,7},{4,0},{5,1},{6,2},{7,3},{8,12},{9,13},{10,... | collective-permute-start | bytes 24584 | tf_op jit(solution)/shard_map/ppermute | solution.py:556
  89.4 4.9 %collective-permute-start.21 = (f32[16,128]{1,0:T(8,128)S(1)}, f32[16,128]{1,0:T(8,128)S(1)}, u32[]{:S(2)}, u32[]{:S(2)}) collective-permute-start(f32[16,128]{1,0:T(8,128)S(1)} %add_add_fusion.1), channel_id=1, source_target_pairs={{0,2},{1,3},{2,4},{3,5},{4,6},{5,7},{6,0},{7,1},{8,10},{9,11},{10,... | collective-permute-start | bytes 24584 | tf_op jit(solution)/shard_map/ppermute | solution.py:556

commit v5 on v4

--- a/solution.py
+++ b/solution.py
@@ -503,7 +503,8 @@
             copy.start()
         return carry
 
-    lax.fori_loop(0, CX // group, body, 0)
+    for i in range(CX // group):
+        body(i, 0)
     for i in range(CX // group):
         for copy in copies(i):
             copy.wait()

time: 103 us -> 102 us (level)
  transfers between devices with their start and end apart: 24 -> 24, of which waited for: 16 -> 15; matrix products, arithmetic and copies ran while one was open for 0% -> 0% of each run, Pallas kernels for 13% -> 13%
where the time goes in v5:
time: 102 us
  Pallas kernels  43.4 us (43%)
  starting transfers between devices  35.2 us (35%)
  waiting for transfers between devices  21.5 us (21%)
  between operations  1.78 us (2%)
    pallas_call x7, Pallas kernels, call(): pl.pallas_call(body, out_shape=[pltpu.VMEM(s, d) if kept else jax.ShapeDt...  43.4 us
    ppermute x20, starting transfers between devices, reduce_all(): total = total + lax.ppermute(value, AXES, route)  30.8 us
    ppermute x20, waiting for transfers between devices, reduce_all(): total = total + lax.ppermute(value, AXES, route)  21.5 us
    ppermute x1, starting transfers between devices, local(): far_same = lax.ppermute(far_same, AXES, same).reshape(halo)  2.98 us
  transfers between devices with their start and end apart: 24, of which 15 were waited for; matrix products, arithmetic and copies ran while one was open for 0% of the time, Pallas kernels for 13%

profile of v5, /device:TPU:0, one launch (start us, length us, event | category | flops | bytes accessed | tf_op | source)
XLA Modules:
  0.0 102.1 jit_solution(3083647606937319826)
XLA Ops:
  0.6 0.0 copy-start
  0.6 0.0 copy-start.1
  1.5 0.1 pad_add_fusion.info
  1.5 2.2 %shard_map.50 = (f32[17,4,16,128]{3,2,1,0:T(8,128)S(1)}, f32[17,4,16,128]{3,2,1,0:T(8,128)S(1)}, f32[17,4,16,128]{3,2,1,0:T(8,128)S(1)}, f32[17,4,16,128]{3,2,1,0:T(8,128)S(1)}) custom-call(s32[3]{0:T(128)S(1)} %pad_add_fusion.info, f32[16,16,16,128]{3,2,1,0:T(8,128)} %right.1, f32[16,16,128]{2,1,0:T(8,128)} %diag.9), custom_call_target="tpu_custom_call" | custom-call | flops 1000000000 | bytes 3000000 | tf_op jit(solution)/shard_map/pallas_call | solution.py:527
  3.7 0.1 collective-permute-start
  3.8 0.7 collective-permute-start.1
  4.5 0.0 copy-done
  4.5 0.0 copy-done.1
  4.5 8.1 %shard_map.51 = (bf16[16,16,240,128]{3,2,1,0:T(8,128)(2,1)S(1)}, f32[16,128]{1,0:T(8,128)S(1)}, f32[16,16,16,128]{3,2,1,0:T(8,128)S(1)}, f32[16,16,16,128]{3,2,1...) custom-call(s32[3]{0:T(128)S(1)} %pad_add_fusion.info, f32[4096,128]{1,0:T(8,128)S(1)} %bitcast.9, ...), custom_call_target="tpu_custom_call" | custom-call | flops 4000000000 | bytes 12000000 | tf_op jit(solution)/shard_map/pallas_call | solution.py:527
  12.7 0.0 collective-permute-done
  12.7 0.0 collective-permute-done.1
  12.7 5.5 %shard_map.52 = (bf16[16,16,240,128]{3,2,1,0:T(8,128)(2,1)S(1)}, f32[16,128]{1,0:T(8,128)S(1)}, f32[4,4,16,16,128]{4,3,2,1,0:T(8,128)S(1)}, f32[4,4,16,16,128]{4,3,2,1,0:T(8,128)S(1)}, f32[8,16,128]{2,1,0:T(8,128)S(1)}) custom-call(s32[3]{0:T(128)S(1)} %pad_add_fusion.info, f32[1088,128]{1,0:T(8,128)S(1)} %bitcast.7, ...), custom_call_target="tpu_custom_call", output_to_operand_aliasing={{0}: (9, {})} | custom-call | flops 4000000000 | bytes 12000000 | tf_op jit(solution)/shard_map/pallas_call | solution.py:527
  18.2 3.0 %collective-permute-start.6 = (f32[17,4,16,128]{3,2,1,0:T(8,128)S(1)}, f32[17,4,16,128]{3,2,1,0:T(8,128)S(1)}, u32[]{:S(2)}, u32[]{:S(2)}) collective-permute-start(f32[17,4,16,128]{3,2,1,0:T(8,128)S(1)} %get-tuple-element.42), channel_id=1, source_target_pairs={{0,1},{1,0},{2,3},{3,2},{4,5},{5,4},{6,7},{7,6},{8,9},{9,8},{10,11... | collective-permute-start | bytes 1671176 | tf_op jit(solution)/shard_map/ppermute | solution.py:609
  21.2 0.7 collective-permute-start.7
  21.9 3.0 %collective-permute-start.2 = (f32[16,128]{1,0:T(8,128)S(1)}, f32[16,128]{1,0:T(8,128)S(1)}, u32[]{:S(2)}, u32[]{:S(2)}) collective-permute-start(f32[16,128]{1,0:T(8,128)S(1)} %get-tuple-element.41), channel_id=1, source_target_pairs={{0,1},{1,0},{2,3},{3,2},{4,5},{5,4},{6,7},{7,6},{8,9},{9,8},{10,11... | collective-permute-start | bytes 24584 | tf_op jit(solution)/shard_map/ppermute | solution.py:557
  24.8 0.8 collective-permute-done.2
  25.7 11.6 %collective-permute-start.5 = (f32[16,128]{1,0:T(8,128)S(1)}, f32[16,128]{1,0:T(8,128)S(1)}, u32[]{:S(2)}, u32[]{:S(2)}) collective-permute-start(f32[16,128]{1,0:T(8,128)S(1)} %add.64), channel_id=1, source_target_pairs={{0,96},{1,97},{2,98},{3,99},{4,100},{5,101},{6,102},{7,103},{8,104... | collective-permute-start | bytes 24584 | tf_op jit(solution)/shard_map/ppermute | solution.py:557
  37.3 0.3 collective-permute-start.4
  37.6 1.0 %collective-permute-start.3 = (f32[16,128]{1,0:T(8,128)S(1)}, f32[16,128]{1,0:T(8,128)S(1)}, u32[]{:S(2)}, u32[]{:S(2)}) collective-permute-start(f32[16,128]{1,0:T(8,128)S(1)} %add.64), channel_id=1, source_target_pairs={{0,32},{1,33},{2,34},{3,35},{4,36},{5,37},{6,38},{7,39},{8,40},{9,... | collective-permute-start | bytes 24584 | tf_op jit(solution)/shard_map/ppermute | solution.py:557
  38.6 0.0 collective-permute-done.5
  38.7 3.8 %collective-permute-done.4 = f32[16,128]{1,0:T(8,128)S(1)} collective-permute-done((f32[16,128]{1,0:T(8,128)S(1)}, f32[16,128]{1,0:T(8,128)S(1)}, u32[]{:S(2)}, u32[]{:S(2)}) %collective-permute-start.4) | collective-permute-done | bytes 8224 | tf_op jit(solution)/shard_map/ppermute | solution.py:557
  42.4 0.1 collective-permute-done.3
  42.5 2.0 %collective-permute-start.10 = (f32[16,128]{1,0:T(8,128)S(1)}, f32[16,128]{1,0:T(8,128)S(1)}, u32[]{:S(2)}, u32[]{:S(2)}) collective-permute-start(f32[16,128]{1,0:T(8,128)S(1)} %add_add_fusion.5), channel_id=1, source_target_pairs={{0,24},{1,25},{2,26},{3,27},{4,28},{5,29},{6,30},{7,31},{8,0},{9,1... | collective-permute-start | bytes 24584 | tf_op jit(solution)/shard_map/ppermute | solution.py:557
  44.5 0.0 collective-permute-start.9
  44.5 0.9 collective-permute-start.8
  45.5 0.0 collective-permute-done.6
  45.5 0.0 collective-permute-done.7
  45.5 2.5 %shard_map.53 = (bf16[4,16,240,128]{3,2,1,0:T(8,128)(2,1)S(1)}, f32[24,16,128]{2,1,0:T(8,128)S(1)}) custom-call(s32[3]{0:T(128)S(1)} %pad_add_fusion.info, f32[1088,128]{1,0:T(8,128)S(1)} %bitcast.10, f32[1088,128]{1,0:T(8,128)S(1)} %bitcast.12, f32[16,16,128]{2,1,0:T(8,128)S(1)} %copy-done, f32[8,16,128]{2,1,0:T(8,128)S(1)} %get-tuple-element.44.diags, ...), custom_call_target="tpu_custom_call" | custom-call | flops 2000000000 | bytes 6000000 | tf_op jit(solution)/shard_map/pallas_call | solution.py:527
  48.0 0.0 collective-permute-done.10
  48.0 1.7 %collective-permute-done.9 = f32[16,128]{1,0:T(8,128)S(1)} collective-permute-done((f32[16,128]{1,0:T(8,128)S(1)}, f32[16,128]{1,0:T(8,128)S(1)}, u32[]{:S(2)}, u32[]{:S(2)}) %collective-permute-start.9) | collective-permute-done | bytes 8224 | tf_op jit(solution)/shard_map/ppermute | solution.py:557
  49.7 0.0 collective-permute-done.8
  49.7 0.1 collective-permute-start.13
  49.8 0.4 collective-permute-start.12
  50.2 1.6 %collective-permute-start.11 = (f32[16,128]{1,0:T(8,128)S(1)}, f32[16,128]{1,0:T(8,128)S(1)}, u32[]{:S(2)}, u32[]{:S(2)}) collective-permute-start(f32[16,128]{1,0:T(8,128)S(1)} %add_add_fusion.4), channel_id=1, source_target_pairs={{0,2},{1,3},{2,4},{3,5},{4,6},{5,7},{6,0},{7,1},{8,10},{9,11},{10,... | collective-permute-start | bytes 24584 | tf_op jit(solution)/shard_map/ppermute | solution.py:557
  51.8 2.5 %shard_map.54.ghost_u = bf16[4,16,240,128]{3,2,1,0:T(8,128)(2,1)S(1)} custom-call(s32[3]{0:T(128)S(1)} %pad_add_fusion.info, f32[1088,128]{1,0:T(8,128)S(1)} %bitcast.11, f32[1088,128]{1,0:T(8,128)S(1)} %bitcast.13, f32[16,16,128]{2,1,0:T(8,128)S(1)} %copy-done, f32[8,16,128]{2,1,0:T(8,128)S(1)} %get-tuple-element.44.diags, ...), custom_call_target="tpu_custom_call" | custom-call | flops 2000000000 | bytes 6000000 | tf_op jit(solution)/shard_map/pallas_call | solution.py:527
  54.3 0.0 collective-permute-done.13
  54.3 0.7 collective-permute-done.12
  55.0 1.1 %collective-permute-done.11 = f32[16,128]{1,0:T(8,128)S(1)} collective-permute-done((f32[16,128]{1,0:T(8,128)S(1)}, f32[16,128]{1,0:T(8,128)S(1)}, u32[]{:S(2)}, u32[]{:S(2)}) %collective-permute-start.11) | collective-permute-done | bytes 8224 | tf_op jit(solution)/shard_map/ppermute | solution.py:557
  56.1 14.9 %shard_map.55 = (bf16[16,16,240,128]{3,2,1,0:T(8,128)(2,1)S(1)}, f32[16,128]{1,0:T(8,128)S(1)}, f32[16,16,16,128]{3,2,1,0:T(8,128)S(1)}) custom-call(s32[3]{0:T(128)S(1)} %pad_add_fusion.info, f32[16,128]{1,0:T(8,128)S(1)} %add_add_fusion.3.mom_in, f32[24,16,128]{2,1,0:T(8,128)S(1)} %get-tuple-element.51.coef, ...), custom_call_target="tpu_custom_call", output_to_operand_aliasing={{0}: (3, {})} | custom-call | flops 10000000000 | bytes 30000000 | tf_op jit(solution)/shard_map/pallas_call | solution.py:527
  71.0 0.1 collective-permute-start.14
  71.1 1.2 %collective-permute-done.14 = f32[16,128]{1,0:T(8,128)S(1)} collective-permute-done((f32[16,128]{1,0:T(8,128)S(1)}, f32[16,128]{1,0:T(8,128)S(1)}, u32[]{:S(2)}, u32[]{:S(2)}) %collective-permute-start.14) | collective-permute-done | bytes 8224 | tf_op jit(solution)/shard_map/ppermute | solution.py:557
  72.3 0.6 collective-permute-start.17
  72.8 0.5 collective-permute-start.16
  73.3 1.4 %collective-permute-start.15 = (f32[16,128]{1,0:T(8,128)S(1)}, f32[16,128]{1,0:T(8,128)S(1)}, u32[]{:S(2)}, u32[]{:S(2)}) collective-permute-start(f32[16,128]{1,0:T(8,128)S(1)} %add.74), channel_id=1, source_target_pairs={{0,32},{1,33},{2,34},{3,35},{4,36},{5,37},{6,38},{7,39},{8,40},{9,... | collective-permute-start | bytes 24584 | tf_op jit(solution)/shard_map/ppermute | solution.py:557
  74.7 1.2 %collective-permute-done.17 = f32[16,128]{1,0:T(8,128)S(1)} collective-permute-done((f32[16,128]{1,0:T(8,128)S(1)}, f32[16,128]{1,0:T(8,128)S(1)}, u32[]{:S(2)}, u32[]{:S(2)}) %collective-permute-start.17) | collective-permute-done | bytes 8224 | tf_op jit(solution)/shard_map/ppermute | solution.py:557
  75.9 2.1 %collective-permute-done.16 = f32[16,128]{1,0:T(8,128)S(1)} collective-permute-done((f32[16,128]{1,0:T(8,128)S(1)}, f32[16,128]{1,0:T(8,128)S(1)}, u32[]{:S(2)}, u32[]{:S(2)}) %collective-permute-start.16) | collective-permute-done | bytes 8224 | tf_op jit(solution)/shard_map/ppermute | solution.py:557
  78.0 0.6 collective-permute-done.15
  78.6 1.6 %collective-permute-start.20 = (f32[16,128]{1,0:T(8,128)S(1)}, f32[16,128]{1,0:T(8,128)S(1)}, u32[]{:S(2)}, u32[]{:S(2)}) collective-permute-start(f32[16,128]{1,0:T(8,128)S(1)} %add_add_fusion.2), channel_id=1, source_target_pairs={{0,24},{1,25},{2,26},{3,27},{4,28},{5,29},{6,30},{7,31},{8,0},{9,1... | collective-permute-start | bytes 24584 | tf_op jit(solution)/shard_map/ppermute | solution.py:557
  80.2 1.4 %collective-permute-start.19 = (f32[16,128]{1,0:T(8,128)S(1)}, f32[16,128]{1,0:T(8,128)S(1)}, u32[]{:S(2)}, u32[]{:S(2)}) collective-permute-start(f32[16,128]{1,0:T(8,128)S(1)} %add_add_fusion.2), channel_id=1, source_target_pairs={{0,16},{1,17},{2,18},{3,19},{4,20},{5,21},{6,22},{7,23},{8,24},{9,... | collective-permute-start | bytes 24584 | tf_op jit(solution)/shard_map/ppermute | solution.py:557
  81.5 0.5 collective-permute-start.18
  82.1 0.2 collective-permute-done.20
  82.2 3.1 %collective-permute-done.19 = f32[16,128]{1,0:T(8,128)S(1)} collective-permute-done((f32[16,128]{1,0:T(8,128)S(1)}, f32[16,128]{1,0:T(8,128)S(1)}, u32[]{:S(2)}, u32[]{:S(2)}) %collective-permute-start.19) | collective-permute-done | bytes 8224 | tf_op jit(solution)/shard_map/ppermute | solution.py:557
  85.3 1.1 %collective-permute-done.18 = f32[16,128]{1,0:T(8,128)S(1)} collective-permute-done((f32[16,128]{1,0:T(8,128)S(1)}, f32[16,128]{1,0:T(8,128)S(1)}, u32[]{:S(2)}, u32[]{:S(2)}) %collective-permute-start.18) | collective-permute-done | bytes 8224 | tf_op jit(solution)/shard_map/ppermute | solution.py:557
  86.4 2.0 %collective-permute-start.23 = (f32[16,128]{1,0:T(8,128)S(1)}, f32[16,128]{1,0:T(8,128)S(1)}, u32[]{:S(2)}, u32[]{:S(2)}) collective-permute-start(f32[16,128]{1,0:T(8,128)S(1)} %add_add_fusion.1), channel_id=1, source_target_pairs={{0,6},{1,7},{2,0},{3,1},{4,2},{5,3},{6,4},{7,5},{8,14},{9,15},{10,... | collective-permute-start | bytes 24584 | tf_op jit(solution)/shard_map/ppermute | solution.py:557
  88.4 0.9 collective-permute-start.22
  89.4 0.9 collective-permute-start.21
  90.2 0.0 collective-permute-done.23
  90.2 3.4 %collective-permute-done.22 = f32[16,128]{1,0:T(8,128)S(1)} collective-permute-done((f32[16,128]{1,0:T(8,128)S(1)}, f32[16,128]{1,0:T(8,128)S(1)}, u32[]{:S(2)}, u32[]{:S(2)}) %collective-permute-start.22) | collective-permute-done | bytes 8224 | tf_op jit(solution)/shard_map/ppermute | solution.py:557
  93.6 0.6 collective-permute-done.21
  94.2 7.7 %shard_map.56 = (f32[16,16,16,128]{3,2,1,0:T(8,128)}, f32[16,16,16,128]{3,2,1,0:T(8,128)}) custom-call(s32[3]{0:T(128)S(1)} %pad_add_fusion.info, f32[16,128]{1,0:T(8,128)S(1)} %add_add_fusion.mom_in, bf16[16,16,240,128]{3,2,1,0:T(8,128)(2,1)S(1)} %get-tuple-element.56.panel, f32[16,16,16,128]{3,2,1,0:T(8,128)S(1)} %get-tuple-element.57.iterate), custom_call_target="tpu_custom_call" | custom-call | flops 4000000000 | bytes 12000000 | tf_op jit(solution)/shard_map/pallas_call | solution.py:527
  (8 shorter events, 0.0 us)
Async XLA Ops:
  0.6 3.9 %copy-start = (f32[16,16,128]{2,1,0:T(8,128)S(1)}, f32[16,16,128]{2,1,0:T(8,128)}, u32[]{:S(2)}) copy-start(f32[16,16,128]{2,1,0:T(8,128)} %diag.9) | copy-start | bytes 393220
  0.6 3.9 %copy-start.1 = (f32[16,16,16,128]{3,2,1,0:T(8,128)S(1)}, f32[16,16,16,128]{3,2,1,0:T(8,128)}, u32[]{:S(2)}) copy-start(f32[16,16,16,128]{3,2,1,0:T(8,128)} %right.1) | copy-start | bytes 6291460
  3.7 8.9 %collective-permute-start = (f32[17,4,16,128]{3,2,1,0:T(8,128)S(1)}, f32[17,4,16,128]{3,2,1,0:T(8,128)S(1)}, u32[]{:S(2)}, u32[]{:S(2)}) collective-permute-start(f32[17,4,16,128]{3,2,1,0:T(8,128)S(1)} %get-tuple-element.30), channel_id=1, source_target_pairs={{0,1},{1,0},{2,3},{3,2},{4,5},{5,4},{6,7},{7,6},{8,9},{9,8},{10,11... | collective-permute-start | bytes 1671176 | tf_op jit(solution)/shard_map/ppermute | solution.py:582
  3.8 8.9 %collective-permute-start.1 = (f32[17,4,16,128]{3,2,1,0:T(8,128)S(1)}, f32[17,4,16,128]{3,2,1,0:T(8,128)S(1)}, u32[]{:S(2)}, u32[]{:S(2)}) collective-permute-start(f32[17,4,16,128]{3,2,1,0:T(8,128)S(1)} %get-tuple-element.31), channel_id=1, source_target_pairs={{1,2},{3,4},{5,6},{7,8},{9,10},{11,12},{13,14},{15,16},{17,18},{19... | collective-permute-start | bytes 1671176 | tf_op jit(solution)/shard_map/ppermute | solution.py:581
  18.2 27.3 %collective-permute-start.6 = (f32[17,4,16,128]{3,2,1,0:T(8,128)S(1)}, f32[17,4,16,128]{3,2,1,0:T(8,128)S(1)}, u32[]{:S(2)}, u32[]{:S(2)}) collective-permute-start(f32[17,4,16,128]{3,2,1,0:T(8,128)S(1)} %get-tuple-element.42), channel_id=1, source_target_pairs={{0,1},{1,0},{2,3},{3,2},{4,5},{5,4},{6,7},{7,6},{8,9},{9,8},{10,11... | collective-permute-start | bytes 1671176 | tf_op jit(solution)/shard_map/ppermute | solution.py:609
  21.2 24.3 %collective-permute-start.7 = (f32[17,4,16,128]{3,2,1,0:T(8,128)S(1)}, f32[17,4,16,128]{3,2,1,0:T(8,128)S(1)}, u32[]{:S(2)}, u32[]{:S(2)}) collective-permute-start(f32[17,4,16,128]{3,2,1,0:T(8,128)S(1)} %get-tuple-element.43), channel_id=1, source_target_pairs={{1,2},{3,4},{5,6},{7,8},{9,10},{11,12},{13,14},{15,16},{17,18},{19... | collective-permute-start | bytes 1671176 | tf_op jit(solution)/shard_map/ppermute | solution.py:608
  21.9 3.8 %collective-permute-start.2 = (f32[16,128]{1,0:T(8,128)S(1)}, f32[16,128]{1,0:T(8,128)S(1)}, u32[]{:S(2)}, u32[]{:S(2)}) collective-permute-start(f32[16,128]{1,0:T(8,128)S(1)} %get-tuple-element.41), channel_id=1, source_target_pairs={{0,1},{1,0},{2,3},{3,2},{4,5},{5,4},{6,7},{7,6},{8,9},{9,8},{10,11... | collective-permute-start | bytes 24584 | tf_op jit(solution)/shard_map/ppermute | solution.py:557
  25.7 13.0 %collective-permute-start.5 = (f32[16,128]{1,0:T(8,128)S(1)}, f32[16,128]{1,0:T(8,128)S(1)}, u32[]{:S(2)}, u32[]{:S(2)}) collective-permute-start(f32[16,128]{1,0:T(8,128)S(1)} %add.64), channel_id=1, source_target_pairs={{0,96},{1,97},{2,98},{3,99},{4,100},{5,101},{6,102},{7,103},{8,104... | collective-permute-start | bytes 24584 | tf_op jit(solution)/shard_map/ppermute | solution.py:557
  37.3 5.2 %collective-permute-start.4 = (f32[16,128]{1,0:T(8,128)S(1)}, f32[16,128]{1,0:T(8,128)S(1)}, u32[]{:S(2)}, u32[]{:S(2)}) collective-permute-start(f32[16,128]{1,0:T(8,128)S(1)} %add.64), channel_id=1, source_target_pairs={{0,64},{1,65},{2,66},{3,67},{4,68},{5,69},{6,70},{7,71},{8,72},{9,... | collective-permute-start | bytes 24584 | tf_op jit(solution)/shard_map/ppermute | solution.py:557
  37.6 4.9 %collective-permute-start.3 = (f32[16,128]{1,0:T(8,128)S(1)}, f32[16,128]{1,0:T(8,128)S(1)}, u32[]{:S(2)}, u32[]{:S(2)}) collective-permute-start(f32[16,128]{1,0:T(8,128)S(1)} %add.64), channel_id=1, source_target_pairs={{0,32},{1,33},{2,34},{3,35},{4,36},{5,37},{6,38},{7,39},{8,40},{9,... | collective-permute-start | bytes 24584 | tf_op jit(solution)/shard_map/ppermute | solution.py:557
  42.5 5.5 %collective-permute-start.10 = (f32[16,128]{1,0:T(8,128)S(1)}, f32[16,128]{1,0:T(8,128)S(1)}, u32[]{:S(2)}, u32[]{:S(2)}) collective-permute-start(f32[16,128]{1,0:T(8,128)S(1)} %add_add_fusion.5), channel_id=1, source_target_pairs={{0,24},{1,25},{2,26},{3,27},{4,28},{5,29},{6,30},{7,31},{8,0},{9,1... | collective-permute-start | bytes 24584 | tf_op jit(solution)/shard_map/ppermute | solution.py:557
  44.5 5.2 %collective-permute-start.9 = (f32[16,128]{1,0:T(8,128)S(1)}, f32[16,128]{1,0:T(8,128)S(1)}, u32[]{:S(2)}, u32[]{:S(2)}) collective-permute-start(f32[16,128]{1,0:T(8,128)S(1)} %add_add_fusion.5), channel_id=1, source_target_pairs={{0,16},{1,17},{2,18},{3,19},{4,20},{5,21},{6,22},{7,23},{8,24},{9,... | collective-permute-start | bytes 24584 | tf_op jit(solution)/shard_map/ppermute | solution.py:557
  44.5 5.2 %collective-permute-start.8 = (f32[16,128]{1,0:T(8,128)S(1)}, f32[16,128]{1,0:T(8,128)S(1)}, u32[]{:S(2)}, u32[]{:S(2)}) collective-permute-start(f32[16,128]{1,0:T(8,128)S(1)} %add_add_fusion.5), channel_id=1, source_target_pairs={{0,8},{1,9},{2,10},{3,11},{4,12},{5,13},{6,14},{7,15},{8,16},{9,17... | collective-permute-start | bytes 24584 | tf_op jit(solution)/shard_map/ppermute | solution.py:557
  49.7 4.6 %collective-permute-start.13 = (f32[16,128]{1,0:T(8,128)S(1)}, f32[16,128]{1,0:T(8,128)S(1)}, u32[]{:S(2)}, u32[]{:S(2)}) collective-permute-start(f32[16,128]{1,0:T(8,128)S(1)} %add_add_fusion.4), channel_id=1, source_target_pairs={{0,6},{1,7},{2,0},{3,1},{4,2},{5,3},{6,4},{7,5},{8,14},{9,15},{10,... | collective-permute-start | bytes 24584 | tf_op jit(solution)/shard_map/ppermute | solution.py:557
  49.8 5.2 %collective-permute-start.12 = (f32[16,128]{1,0:T(8,128)S(1)}, f32[16,128]{1,0:T(8,128)S(1)}, u32[]{:S(2)}, u32[]{:S(2)}) collective-permute-start(f32[16,128]{1,0:T(8,128)S(1)} %add_add_fusion.4), channel_id=1, source_target_pairs={{0,4},{1,5},{2,6},{3,7},{4,0},{5,1},{6,2},{7,3},{8,12},{9,13},{10,... | collective-permute-start | bytes 24584 | tf_op jit(solution)/shard_map/ppermute | solution.py:557
  50.2 5.9 %collective-permute-start.11 = (f32[16,128]{1,0:T(8,128)S(1)}, f32[16,128]{1,0:T(8,128)S(1)}, u32[]{:S(2)}, u32[]{:S(2)}) collective-permute-start(f32[16,128]{1,0:T(8,128)S(1)} %add_add_fusion.4), channel_id=1, source_target_pairs={{0,2},{1,3},{2,4},{3,5},{4,6},{5,7},{6,0},{7,1},{8,10},{9,11},{10,... | collective-permute-start | bytes 24584 | tf_op jit(solution)/shard_map/ppermute | solution.py:557
  71.0 1.3 %collective-permute-start.14 = (f32[16,128]{1,0:T(8,128)S(1)}, f32[16,128]{1,0:T(8,128)S(1)}, u32[]{:S(2)}, u32[]{:S(2)}) collective-permute-start(f32[16,128]{1,0:T(8,128)S(1)} %get-tuple-element.55), channel_id=1, source_target_pairs={{0,1},{1,0},{2,3},{3,2},{4,5},{5,4},{6,7},{7,6},{8,9},{9,8},{10,11... | collective-permute-start | bytes 24584 | tf_op jit(solution)/shard_map/ppermute | solution.py:557
  72.3 3.7 %collective-permute-start.17 = (f32[16,128]{1,0:T(8,128)S(1)}, f32[16,128]{1,0:T(8,128)S(1)}, u32[]{:S(2)}, u32[]{:S(2)}) collective-permute-start(f32[16,128]{1,0:T(8,128)S(1)} %add.74), channel_id=1, source_target_pairs={{0,96},{1,97},{2,98},{3,99},{4,100},{5,101},{6,102},{7,103},{8,104... | collective-permute-start | bytes 24584 | tf_op jit(solution)/shard_map/ppermute | solution.py:557
  72.8 5.2 %collective-permute-start.16 = (f32[16,128]{1,0:T(8,128)S(1)}, f32[16,128]{1,0:T(8,128)S(1)}, u32[]{:S(2)}, u32[]{:S(2)}) collective-permute-start(f32[16,128]{1,0:T(8,128)S(1)} %add.74), channel_id=1, source_target_pairs={{0,64},{1,65},{2,66},{3,67},{4,68},{5,69},{6,70},{7,71},{8,72},{9,... | collective-permute-start | bytes 24584 | tf_op jit(solution)/shard_map/ppermute | solution.py:557
  73.3 5.3 %collective-permute-start.15 = (f32[16,128]{1,0:T(8,128)S(1)}, f32[16,128]{1,0:T(8,128)S(1)}, u32[]{:S(2)}, u32[]{:S(2)}) collective-permute-start(f32[16,128]{1,0:T(8,128)S(1)} %add.74), channel_id=1, source_target_pairs={{0,32},{1,33},{2,34},{3,35},{4,36},{5,37},{6,38},{7,39},{8,40},{9,... | collective-permute-start | bytes 24584 | tf_op jit(solution)/shard_map/ppermute | solution.py:557
  78.6 3.7 %collective-permute-start.20 = (f32[16,128]{1,0:T(8,128)S(1)}, f32[16,128]{1,0:T(8,128)S(1)}, u32[]{:S(2)}, u32[]{:S(2)}) collective-permute-start(f32[16,128]{1,0:T(8,128)S(1)} %add_add_fusion.2), channel_id=1, source_target_pairs={{0,24},{1,25},{2,26},{3,27},{4,28},{5,29},{6,30},{7,31},{8,0},{9,1... | collective-permute-start | bytes 24584 | tf_op jit(solution)/shard_map/ppermute | solution.py:557
  80.2 5.2 %collective-permute-start.19 = (f32[16,128]{1,0:T(8,128)S(1)}, f32[16,128]{1,0:T(8,128)S(1)}, u32[]{:S(2)}, u32[]{:S(2)}) collective-permute-start(f32[16,128]{1,0:T(8,128)S(1)} %add_add_fusion.2), channel_id=1, source_target_pairs={{0,16},{1,17},{2,18},{3,19},{4,20},{5,21},{6,22},{7,23},{8,24},{9,... | collective-permute-start | bytes 24584 | tf_op jit(solution)/shard_map/ppermute | solution.py:557
  81.5 4.9 %collective-permute-start.18 = (f32[16,128]{1,0:T(8,128)S(1)}, f32[16,128]{1,0:T(8,128)S(1)}, u32[]{:S(2)}, u32[]{:S(2)}) collective-permute-start(f32[16,128]{1,0:T(8,128)S(1)} %add_add_fusion.2), channel_id=1, source_target_pairs={{0,8},{1,9},{2,10},{3,11},{4,12},{5,13},{6,14},{7,15},{8,16},{9,17... | collective-permute-start | bytes 24584 | tf_op jit(solution)/shard_map/ppermute | solution.py:557
  86.4 3.8 %collective-permute-start.23 = (f32[16,128]{1,0:T(8,128)S(1)}, f32[16,128]{1,0:T(8,128)S(1)}, u32[]{:S(2)}, u32[]{:S(2)}) collective-permute-start(f32[16,128]{1,0:T(8,128)S(1)} %add_add_fusion.1), channel_id=1, source_target_pairs={{0,6},{1,7},{2,0},{3,1},{4,2},{5,3},{6,4},{7,5},{8,14},{9,15},{10,... | collective-permute-start | bytes 24584 | tf_op jit(solution)/shard_map/ppermute | solution.py:557
  88.4 5.2 %collective-permute-start.22 = (f32[16,128]{1,0:T(8,128)S(1)}, f32[16,128]{1,0:T(8,128)S(1)}, u32[]{:S(2)}, u32[]{:S(2)}) collective-permute-start(f32[16,128]{1,0:T(8,128)S(1)} %add_add_fusion.1), channel_id=1, source_target_pairs={{0,4},{1,5},{2,6},{3,7},{4,0},{5,1},{6,2},{7,3},{8,12},{9,13},{10,... | collective-permute-start | bytes 24584 | tf_op jit(solution)/shard_map/ppermute | solution.py:557
  89.4 4.9 %collective-permute-start.21 = (f32[16,128]{1,0:T(8,128)S(1)}, f32[16,128]{1,0:T(8,128)S(1)}, u32[]{:S(2)}, u32[]{:S(2)}) collective-permute-start(f32[16,128]{1,0:T(8,128)S(1)} %add_add_fusion.1), channel_id=1, source_target_pairs={{0,2},{1,3},{2,4},{3,5},{4,6},{5,7},{6,0},{7,1},{8,10},{9,11},{10,... | collective-permute-start | bytes 24584 | tf_op jit(solution)/shard_map/ppermute | solution.py:557
